TPU v7x, 512 devices: a whole 4x4x16 slice. The times are simulated.
512 devices in a mesh: pair: 32 (over z_lo, y), virt: 16 (over z_hi, x, core).
Axes of the slice: x: 4, y: 4, z: 16 (z_hi: 2, z_lo: 8; z = z_hi * 8 + z_lo), core: 2. Of those that a mesh axis runs over, the one named last changes fastest.
Arguments:
- lambda_amps: bfloat16 [384, 1024, 1024], P('pair', 'virt'), may hold values from -0.0002975464 to 0.0002975464
- t_amps: bfloat16 [384, 1024, 1024], P('pair', 'virt'), may hold values from -6 to 6
- panel_home: int32 [32], replicated, may hold values from 0 to 31, each once
- pair_list: int32 [264, 2], replicated, may hold values from 0 to 31, as said below
Outputs:
- density: bfloat16 [384, 1024, 1024], P('pair', 'virt')
Inputs may be any that keep to these rules, and one draw needn't show every extreme that they name: `pair_list`: rows are distinct panel pairs with first entry <= second.
All inputs are finite; a program needn't handle non-finite values.
Results may differ from a plain program's by a relative error of at most 0.0049.
Values may be sent and summed in bfloat16 or wider, within the bound.
No kernel may reach another device: no remote copies, remote signals or barrier semaphores. Data moves between devices by JAX's collectives and lax.ppermute only.
A program may use at most 64 MiB of HBM per device.

v0:
```python
import jax
import jax.numpy as jnp
from jax import lax
from jax.sharding import PartitionSpec as P


def onehot(index, count):
    return (index[:, None] == jnp.arange(count)[None, :]).astype(jnp.float32)


def on_device(lambda_amps, t_amps, panel_home, pair_list):
    npanels = lax.axis_size("pair")
    panel_size = lambda_amps.shape[0]
    home = onehot(panel_home, npanels)
    first = jnp.dot(onehot(pair_list[:, 0], npanels), home, precision=lax.Precision.HIGHEST)
    second = jnp.dot(onehot(pair_list[:, 1], npanels), home, precision=lax.Precision.HIGHEST)
    lam, amp = (
        lax.all_to_all(lambda_amps, "pair", split_axis=2, concat_axis=0, tiled=True),
        lax.all_to_all(t_amps, "pair", split_axis=2, concat_axis=0, tiled=True),
    )
    pairs = lam.shape[0]
    lam_flat = lam.reshape(pairs, -1)
    amp_flat = amp.reshape(pairs, -1)
    cross = lax.dot_general(
        lam_flat, amp_flat, (((1,), (1,)), ((), ())), preferred_element_type=jnp.float32
    )
    partial_sym = 0.5 * (cross + cross.T)
    total = lax.psum(partial_sym, ("pair", "virt"))
    panels = jnp.dot(first.T, second, precision=lax.Precision.HIGHEST)
    panels = jnp.minimum(panels + panels.T, 1.0)
    blockmask = jnp.broadcast_to(
        panels[:, None, :, None], (npanels, panel_size, npanels, panel_size)
    )
    inter = (total * blockmask.reshape(pairs, pairs)).astype(jnp.bfloat16)
    result = jnp.dot(inter, amp_flat, preferred_element_type=jnp.float32).astype(jnp.bfloat16)
    result = result.reshape(lam.shape)
    return lax.all_to_all(result, "pair", split_axis=0, concat_axis=2, tiled=True)


def solution(mesh):
    placed = (P("pair", "virt", None), P("pair", "virt", None), P(), P())
    return jax.shard_map(
        on_device, mesh=mesh, in_specs=placed, out_specs=P("pair", "virt", None), check_vma=False
    )
```

profile of v0, /device:TPU:1, one launch (start us, length us, event | category | flops | bytes accessed | tf_op | source)
XLA Modules:
  0.0 787.8 jit_solution(9159878999972155565)
XLA Ops:
  6.5 6.1 copy.43
  12.6 7.4 reshape.22
  20.0 0.0 copy-start.2
  20.0 16.2 %all-to-all-start.1 = ((bf16[32,2,12288]{2,1,0:T(2,128)(2,1)}), bf16[32,2,12288]{2,1,0:T(2,128)(2,1)S(1)}, u32[]{:S(2)}, u32[]{:S(2)}) async-start(bf16[32,2,12288]{2,1,0:T(2,128)(2,1)} %reshape.22), calls=%async_computation.1 | async-start | bytes 3145728 | tf_op jit(solution)/shard_map/all_to_all | solution.py:19
  36.3 0.0 copy-done.2
  36.3 4.8 copy.40
  41.1 7.4 reshape.24
  48.5 0.0 copy-start.3
  48.5 0.0 copy-start.4
  48.5 59.9 %all-to-all-done.1 = bf16[32,2,12288]{2,1,0:T(2,128)(2,1)S(1)} async-done(((bf16[32,2,12288]{2,1,0:T(2,128)(2,1)}), bf16[32,2,12288]{2,1,0:T(2,128)(2,1)S(1)}, u32[]{:S(2)}, u32[]{:S(2)}) %all-to-all-start.1) | async-done | bytes 1572896 | tf_op jit(solution)/shard_map/all_to_all | solution.py:19
  108.4 8.0 %all-to-all-start = ((bf16[32,2,12288]{2,1,0:T(2,128)(2,1)}), bf16[32,2,12288]{2,1,0:T(2,128)(2,1)S(1)}, u32[]{:S(2)}, u32[]{:S(2)}) async-start(bf16[32,2,12288]{2,1,0:T(2,128)(2,1)} %reshape.24), calls=%async_computation | async-start | bytes 3145728 | tf_op jit(solution)/shard_map/all_to_all | solution.py:18
  116.4 0.2 all-reduce.2.cloned.1.call-start
  116.7 0.0 copy-done.3
  116.7 0.0 copy-done.4
  116.7 0.3 fusion.1
  117.0 0.3 fusion.2
  117.2 3.7 reshape.23
  121.0 8.2 %copy.45 = bf16[32,12,64,32]{3,2,1,0:T(8,128)(2,1)} copy(bf16[32,12,64,32]{2,1,3,0:T(8,128)(2,1)} %bitcast.36) | data formatting | bytes 3145728 | tf_op jit(solution)/shard_map/all_to_all | solution.py:19
  129.2 8.5 %reshape.17 = bf16[384,2048]{1,0:T(8,128)(2,1)S(1)} reshape(bf16[32,12,64,32]{3,2,1,0:T(8,128)(2,1)} %copy.45) | data formatting | bytes 3145728 | tf_op jit(solution)/shard_map/reshape | solution.py:23
  137.7 0.0 copy-start
  137.7 50.7 %all-to-all-done = bf16[32,2,12288]{2,1,0:T(2,128)(2,1)S(1)} async-done(((bf16[32,2,12288]{2,1,0:T(2,128)(2,1)}), bf16[32,2,12288]{2,1,0:T(2,128)(2,1)S(1)}, u32[]{:S(2)}, u32[]{:S(2)}) %all-to-all-start) | async-done | bytes 1572896 | tf_op jit(solution)/shard_map/all_to_all | solution.py:18
  188.4 3.7 reshape.25
  192.1 8.2 %copy.42 = bf16[32,12,64,32]{3,2,1,0:T(8,128)(2,1)} copy(bf16[32,12,64,32]{2,1,3,0:T(8,128)(2,1)} %bitcast.37) | data formatting | bytes 3145728 | tf_op jit(solution)/shard_map/all_to_all | solution.py:18
  200.3 9.5 %reshape.16 = bf16[384,2048]{1,0:T(8,128)(2,1)} reshape(bf16[32,12,64,32]{3,2,1,0:T(8,128)(2,1)} %copy.42) | data formatting | bytes 3145728 | tf_op jit(solution)/shard_map/reshape | solution.py:22
  209.8 0.0 copy-done
  209.8 2.4 fusion.8
  212.2 0.2 copy.46
  212.5 0.9 fusion
  213.4 0.0 all-reduce.2.cloned.1.call-update
  213.4 0.2 fusion.9
  213.6 0.1 copy.47
  213.6 3.5 broadcast_in_dim.2
  217.2 0.0 copy-start.1
  217.2 7.1 reshape.18
  224.3 447.0 %all-reduce.2.cloned.1.call-done = f32[384,384]{1,0:T(8,128)} async-done(((f32[384,384]{1,0:T(8,128)}), f32[384,384]{1,0:T(8,128)}) %all-reduce.2.cloned.1.call-update) | async-done | bytes 589840 | tf_op jit(solution)/shard_map/psum | solution.py:28
  671.2 0.0 copy-done.1
  671.2 2.2 convolution_convert_fusion
  673.4 1.6 copy.48
  675.0 6.4 copy.49
  681.4 3.4 reshape.26
  684.8 84.4 %all_to_all.48 = bf16[32,2,12288]{2,1,0:T(2,128)(2,1)} all-to-all(bf16[32,2,12288]{2,1,0:T(2,128)(2,1)} %reshape.26), channel_id=1, replica_groups=mesh['pair'=32,'virt'=16] {'pair'}, dimensions={0} | all-to-all | bytes 3145728 | tf_op jit(solution)/shard_map/all_to_all | solution.py:37
  769.2 5.1 reshape.27
  774.3 2.4 copy.50
  776.7 4.3 copy.51
  (2 shorter events, 0.0 us)
Async XLA Ops:
  20.0 16.2 %copy-start.2 = (bf16[12,64,1024]{2,1,0:T(8,128)(2,1)S(1)}, bf16[12,64,1024]{2,1,0:T(8,128)(2,1)}, u32[]{:S(2)}) copy-start(bf16[12,64,1024]{2,1,0:T(8,128)(2,1)} %param.4) | copy-start | bytes 4718596
  20.0 88.4 %all-to-all-start.1 = ((bf16[32,2,12288]{2,1,0:T(2,128)(2,1)}), bf16[32,2,12288]{2,1,0:T(2,128)(2,1)S(1)}, u32[]{:S(2)}, u32[]{:S(2)}) async-start(bf16[32,2,12288]{2,1,0:T(2,128)(2,1)} %reshape.22), calls=%async_computation.1 | async-start | bytes 3145728 | tf_op jit(solution)/shard_map/all_to_all | solution.py:19
  48.5 68.1 %copy-start.3 = (s32[264,2]{0,1:T(2,128)S(1)}, s32[264,2]{0,1:T(2,128)}, u32[]{:S(2)}) copy-start(s32[264,2]{0,1:T(2,128)} %param.7) | copy-start | bytes 6340
  48.5 68.1 %copy-start.4 = (s32[32]{0:T(128)S(1)}, s32[32]{0:T(128)}, u32[]{:S(2)}) copy-start(s32[32]{0:T(128)} %param.6) | copy-start | bytes 388
  108.4 80.0 %all-to-all-start = ((bf16[32,2,12288]{2,1,0:T(2,128)(2,1)}), bf16[32,2,12288]{2,1,0:T(2,128)(2,1)S(1)}, u32[]{:S(2)}, u32[]{:S(2)}) async-start(bf16[32,2,12288]{2,1,0:T(2,128)(2,1)} %reshape.24), calls=%async_computation | async-start | bytes 3145728 | tf_op jit(solution)/shard_map/all_to_all | solution.py:18
  116.4 554.8 %all-reduce.2.cloned.1.call-start = ((), (), s32[]{:S(2)}) async-start(), calls=%async_computation.3 | async-start | bytes 1179648 | tf_op jit(solution)/shard_map/psum | solution.py:28
  137.7 72.1 %copy-start = (bf16[384,2048]{1,0:T(8,128)(2,1)}, bf16[384,2048]{1,0:T(8,128)(2,1)S(1)}, u32[]{:S(2)}) copy-start(bf16[384,2048]{1,0:T(8,128)(2,1)S(1)} %reshape.17) | copy-start | bytes 4718596
  217.2 454.0 %copy-start.1 = (bf16[384,2048]{1,0:T(8,128)(2,1)S(1)}, bf16[384,2048]{1,0:T(8,128)(2,1)}, u32[]{:S(2)}) copy-start(bf16[384,2048]{1,0:T(8,128)(2,1)} %copy-done) | copy-start | bytes 4718596
Sparse Core Ops, SparseCore 0:
  213.5 457.6 all-reduce.1
where the time goes:
time: 789 us; the launch traced here: 788 us
  waiting for transfers between devices  558 us (71%)
  local copies, waits for them, and re-layouts  102 us (13%)
  blocking collectives  84.4 us (11%)
  starting transfers between devices  24.5 us (3%)
  between operations  13.5 us (2%)
    psum x1, waiting for transfers between devices, on_device(): total = lax.psum(partial_sym, ('pair', 'virt'))  447 us
    all_to_all x1, blocking collectives, on_device(): lax.all_to_all(result, 'pair', split_axis=0, concat_axis=2, tiled=True)  84.4 us
    all_to_all x1, waiting for transfers between devices, on_device(): lax.all_to_all(t_amps, 'pair', split_axis=2, concat_axis=0, tiled=True)  59.9 us
    all_to_all x1, waiting for transfers between devices, on_device(): lax.all_to_all(lambda_amps, 'pair', split_axis=2, concat_axis=0, tiled=True)  50.7 us
    unnamed x18, local copies, waits for them, and re-layouts  41.7 us
    all_to_all x1, starting transfers between devices, on_device(): lax.all_to_all(t_amps, 'pair', split_axis=2, concat_axis=0, tiled=True)  16.2 us
  transfers between devices with their start and end apart: 3, of which 3 were waited for; matrix products, arithmetic and copies ran while one was open for 6% of the time, Pallas kernels for 0%

commit v1 on v0

v1 whole, which is shorter than its diff:
```python
import jax
import jax.numpy as jnp
from jax import lax
from jax.experimental import pallas as pl
from jax.experimental.pallas import tpu as pltpu
from jax.sharding import PartitionSpec as P

ROWS = 16
LANES = 128
BLOCK = 128
VMEM_LIMIT = 48 * 1024 * 1024


def onehot(index, count):
    return (index[:, None] == jnp.arange(count)[None, :]).astype(jnp.float32)


def vmem(count):
    return [pl.BlockSpec(memory_space=pltpu.VMEM)] * count


def call(body, out_shape, args, scratch=()):
    outs = out_shape if isinstance(out_shape, (list, tuple)) else [out_shape]
    specs = vmem(len(outs))
    return pl.pallas_call(
        body,
        out_shape=out_shape,
        in_specs=vmem(len(args)),
        out_specs=specs if isinstance(out_shape, (list, tuple)) else specs[0],
        scratch_shapes=list(scratch),
        compiler_params=pltpu.CompilerParams(vmem_limit_bytes=VMEM_LIMIT),
    )(*args)


def pack(lam_ref, amp_ref, out_ref):
    down, across = lam_ref.shape[1] // ROWS, lam_ref.shape[2] // LANES
    for i in range(down):
        for c in range(across):
            part = (slice(None), slice(i * ROWS, (i + 1) * ROWS), slice(c * LANES, (c + 1) * LANES))
            out_ref[i * across + c, 0] = lam_ref[part]
            out_ref[i * across + c, 1] = amp_ref[part]


def unpack(parts_ref, out_ref):
    down, across = out_ref.shape[1] // ROWS, out_ref.shape[2] // LANES
    for i in range(down):
        for c in range(across):
            out_ref[:, i * ROWS : (i + 1) * ROWS, c * LANES : (c + 1) * LANES] = parts_ref[i * across + c]


def swap_matrix():
    side = ROWS * ROWS
    i = lax.broadcasted_iota(jnp.int32, (side, side), 0)
    j = lax.broadcasted_iota(jnp.int32, (side, side), 1)
    return (j == (i % ROWS) * ROWS + i // ROWS).astype(jnp.float32).astype(jnp.bfloat16)


def upper_blocks(pairs):
    n = pairs // BLOCK
    return [(i, j) for i in range(n) for j in range(i, n)]


def cross_kernel(parts_ref, sym_ref, amp_ref, lam_ref):
    swap = swap_matrix()
    panels, _, panel_size = parts_ref.shape[:3]
    side = ROWS * ROWS
    chunk = 4 * panel_size

    def relayout(step, carry):
        lam = parts_ref[pl.ds(4 * step, 4), 0].reshape(chunk * ROWS, LANES)
        amp = parts_ref[pl.ds(4 * step, 4), 1].reshape(chunk * ROWS, LANES)
        both = jnp.concatenate([lam, amp], axis=1)
        for q in range(chunk // ROWS):
            moved = jnp.dot(swap, both[q * side : (q + 1) * side], preferred_element_type=jnp.float32)
            moved = moved.astype(jnp.bfloat16)
            at = pl.ds(pl.multiple_of(step * chunk + q * ROWS, ROWS), ROWS)
            for s in range(ROWS):
                lam_ref[at, s * LANES : (s + 1) * LANES] = moved[s * ROWS : (s + 1) * ROWS, :LANES]
                amp_ref[at, s * LANES : (s + 1) * LANES] = moved[s * ROWS : (s + 1) * ROWS, LANES:]
        return carry

    lax.fori_loop(0, panels // 4, relayout, 0)
    cross = lax.dot_general(
        lam_ref[...], amp_ref[...], (((1,), (1,)), ((), ())), preferred_element_type=jnp.float32
    )
    sym = 0.5 * (cross + cross.T)
    for n, (i, j) in enumerate(upper_blocks(cross.shape[0])):
        sym_ref[n * BLOCK : (n + 1) * BLOCK] = sym[i * BLOCK : (i + 1) * BLOCK, j * BLOCK : (j + 1) * BLOCK]


def density_kernel(upper_ref, listed_ref, amp_ref, out_ref, inter_ref, flat_ref):
    pairs, depth = amp_ref.shape
    panels = listed_ref.shape[0]
    panel_size = pairs // panels
    row = lax.broadcasted_iota(jnp.int32, (pairs, panels), 0)
    first = lax.broadcasted_iota(jnp.int32, (pairs, panels), 1) * panel_size
    spread = ((row >= first) & (row < first + panel_size)).astype(jnp.float32)
    mask = jnp.dot(spread, listed_ref[...], preferred_element_type=jnp.float32)
    mask = lax.dot_general(mask, spread, (((1,), (1,)), ((), ())), preferred_element_type=jnp.float32)
    for n, (i, j) in enumerate(upper_blocks(pairs)):
        block = upper_ref[n * BLOCK : (n + 1) * BLOCK].astype(jnp.float32)
        rows, cols = slice(i * BLOCK, (i + 1) * BLOCK), slice(j * BLOCK, (j + 1) * BLOCK)
        inter_ref[rows, cols] = (block * mask[rows, cols]).astype(jnp.bfloat16)
        if i != j:
            inter_ref[cols, rows] = (block.T * mask[cols, rows]).astype(jnp.bfloat16)
    wide = 2 * LANES
    for c in range(depth // wide):
        flat_ref[:, c * wide : (c + 1) * wide] = jnp.dot(
            inter_ref[...], amp_ref[:, c * wide : (c + 1) * wide], preferred_element_type=jnp.float32
        ).astype(jnp.bfloat16)
    swap = swap_matrix()

    def relayout(step, carry):
        at = pl.multiple_of(step * 2 * ROWS, 2 * ROWS)
        halves = []
        for h in range(2):
            rows = pl.ds(at + h * ROWS, ROWS)
            halves.append(
                jnp.concatenate([flat_ref[rows, s * LANES : (s + 1) * LANES] for s in range(ROWS)], axis=0)
            )
        moved = jnp.dot(swap, jnp.concatenate(halves, axis=1), preferred_element_type=jnp.float32)
        moved = moved.astype(jnp.bfloat16)
        for h in range(2):
            out_ref[pl.ds(at + h * ROWS, ROWS)] = moved[:, h * LANES : (h + 1) * LANES].reshape(ROWS, ROWS, LANES)
        return carry

    lax.fori_loop(0, pairs // (2 * ROWS), relayout, 0)


def exchange(x, axis):
    return lax.all_to_all(x, axis, split_axis=0, concat_axis=0, tiled=True)


def on_device(lambda_amps, t_amps, panel_home, pair_list):
    npanels = lax.axis_size("pair")
    nslabs = lax.axis_size("virt")
    panel_size, rows, cols = lambda_amps.shape
    pairs = npanels * panel_size
    depth = rows * cols // npanels
    bf16, f32 = jnp.bfloat16, jnp.float32

    home = onehot(panel_home, npanels)
    first = jnp.dot(onehot(pair_list[:, 0], npanels), home, precision=lax.Precision.HIGHEST)
    second = jnp.dot(onehot(pair_list[:, 1], npanels), home, precision=lax.Precision.HIGHEST)
    listed = jnp.dot(first.T, second, precision=lax.Precision.HIGHEST)
    listed = jnp.minimum(listed + listed.T, 1.0)

    parts = call(
        pack,
        jax.ShapeDtypeStruct((npanels, 2, panel_size, ROWS, LANES), bf16),
        (lambda_amps, t_amps),
    )
    parts = exchange(parts, "pair")
    nblocks = len(upper_blocks(pairs))
    sym, amp = call(
        cross_kernel,
        [
            jax.ShapeDtypeStruct((nblocks * BLOCK, BLOCK), f32),
            jax.ShapeDtypeStruct((pairs, depth), bf16),
        ],
        (parts,),
        [pltpu.VMEM((pairs, depth), bf16)],
    )
    own = nblocks * BLOCK // npanels
    terms = exchange(sym.reshape(npanels, own, BLOCK), "pair")
    terms = jnp.broadcast_to(jnp.sum(terms, axis=0), (nslabs, own, BLOCK))
    total = jnp.sum(exchange(terms, "virt"), axis=0).astype(bf16)
    upper = exchange(jnp.broadcast_to(total, (npanels, own, BLOCK)), "pair")
    result = call(
        density_kernel,
        jax.ShapeDtypeStruct((pairs, ROWS, LANES), bf16),
        (upper.reshape(nblocks * BLOCK, BLOCK), listed, amp),
        [pltpu.VMEM((pairs, pairs), bf16), pltpu.VMEM((pairs, depth), bf16)],
    )
    result = exchange(result.reshape(npanels, panel_size, ROWS, LANES), "pair")
    return call(unpack, jax.ShapeDtypeStruct(lambda_amps.shape, bf16), (result,))


def solution(mesh):
    placed = (P("pair", "virt", None), P("pair", "virt", None), P(), P())
    return jax.shard_map(
        on_device, mesh=mesh, in_specs=placed, out_specs=P("pair", "virt", None), check_vma=False
    )
```

time: 789 us -> 336 us (0.43)
  waiting for transfers between devices: 558 us -> 28.7 us
  blocking collectives: 84.4 us -> 265 us
  local copies, waits for them, and re-layouts: 102 us -> 4.32 us
  between operations: 13.5 us -> 0.09 us
  Pallas kernels: 0 us -> 10.8 us
    psum x1 -> x0, waiting for transfers between devices: 447 us -> none  [on_device(): total = lax.psum(partial_sym, ('pair', 'virt'))]
    all_to_all x1 -> x3, blocking collectives: 84.4 us -> 265 us  [exchange(): return lax.all_to_all(x, axis, split_axis=0, concat_axis=0, tiled=True)]
    all_to_all x2, waiting for transfers between devices: 111 us -> 28.7 us  [exchange(): return lax.all_to_all(x, axis, split_axis=0, concat_axis=0, tiled=True)]
    unnamed x18 -> x8, local copies, waits for them, and re-layouts: 41.7 us -> 2.83 us
    reshape x4 -> x0, local copies, waits for them, and re-layouts: 31.5 us -> none  [the longest x1 9.48 us: on_device(): lam_flat = lam.reshape(pairs, -1)]
    all_to_all x4 -> x0, local copies, waits for them, and re-layouts: 23.1 us -> none  [the longest x1 8.2 us: on_device(): lax.all_to_all(t_amps, 'pair', split_axis=2, concat_axis=0, tiled=True)]
    pallas_call x0 -> x4, Pallas kernels: none -> 10.8 us  [call(): pl.pallas_call(body, out_shape=out_shape, in_specs=vmem(len(args)), out_s...]
  transfers between devices with their start and end apart: 3 -> 2, of which waited for: 3 -> 2; matrix products, arithmetic and copies ran while one was open for 6% -> 0% of each run, Pallas kernels for 0% -> 0%
where the time goes in v1:
time: 336 us; the launch traced here: 335 us
  blocking collectives  265 us (79%)
  waiting for transfers between devices  28.7 us (9%)
  starting transfers between devices  25.5 us (8%)
  Pallas kernels  10.8 us (3%)
  local copies, waits for them, and re-layouts  4.32 us (1%)
    all_to_all x3, blocking collectives, exchange(): return lax.all_to_all(x, axis, split_axis=0, concat_axis=0, tiled=True)  265 us
    all_to_all x2, waiting for transfers between devices, exchange(): return lax.all_to_all(x, axis, split_axis=0, concat_axis=0, tiled=True)  28.7 us
    all_to_all x2, starting transfers between devices, exchange(): return lax.all_to_all(x, axis, split_axis=0, concat_axis=0, tiled=True)  25.5 us
    pallas_call x4, Pallas kernels, call(): pl.pallas_call(body, out_shape=out_shape, in_specs=vmem(len(args)), out_s...  10.8 us
  transfers between devices with their start and end apart: 2, of which 2 were waited for; matrix products, arithmetic and copies ran while one was open for 0% of the time, Pallas kernels for 0%

profile of v1, /device:TPU:1, one launch (start us, length us, event | category | flops | bytes accessed | tf_op | source)
XLA Modules:
  0.0 335.1 jit_solution(1417044140625734030)
XLA Ops:
  0.0 0.0 copy-start
  0.0 1.4 copy-done
  1.4 0.0 copy-start.1
  1.4 1.4 copy-done.1
  2.8 2.2 shard_map.46
  5.0 156.0 %all_to_all.25.parts_ref = bf16[32,2,12,16,128]{4,3,2,1,0:T(8,128)(2,1)S(1)} all-to-all(bf16[32,2,12,16,128]{4,3,2,1,0:T(8,128)(2,1)} %shard_map.46), channel_id=1, replica_groups=mesh['pair'=32,'virt'=16] {'pair'}, dimensions={0} | all-to-all | bytes 6291456 | tf_op jit(solution)/shard_map/all_to_all | solution.py:131
  161.1 3.5 %shard_map.47 = (f32[768,128]{1,0:T(8,128)S(1)}, bf16[384,2048]{1,0:T(8,128)(2,1)S(1)}) custom-call(bf16[32,2,12,16,128]{4,3,2,1,0:T(8,128)(2,1)S(1)} %all_to_all.25.parts_ref), custom_call_target="tpu_custom_call" | custom-call | tf_op jit(solution)/shard_map/pallas_call | solution.py:25
  164.5 0.0 copy-start.2
  164.5 0.0 copy-start.3
  164.6 27.8 %all_to_all.26 = f32[32,24,128]{2,1,0:T(8,128)S(1)} all-to-all(f32[32,24,128]{2,1,0:T(8,128)S(1)} %bitcast.11), channel_id=1, replica_groups=mesh['pair'=32,'virt'=16] {'pair'}, dimensions={0} | all-to-all | bytes 786432 | tf_op jit(solution)/shard_map/all_to_all | solution.py:131
  192.4 0.7 broadcast_in_dim.4
  193.0 15.1 %all-to-all-start.2 = ((f32[16,24,128]{2,1,0:T(8,128)}), f32[16,24,128]{2,1,0:T(8,128)S(1)}, u32[]{:S(2)}, u32[]{:S(2)}) async-start(f32[16,24,128]{2,1,0:T(8,128)} %broadcast_in_dim.4), calls=%async_computation.2 | async-start | bytes 393216 | tf_op jit(solution)/shard_map/all_to_all | solution.py:131
  208.2 0.0 copy-done.2
  208.2 15.6 %all-to-all-done.2 = f32[16,24,128]{2,1,0:T(8,128)S(1)} async-done(((f32[16,24,128]{2,1,0:T(8,128)}), f32[16,24,128]{2,1,0:T(8,128)S(1)}, u32[]{:S(2)}, u32[]{:S(2)}) %all-to-all-start.2) | async-done | bytes 196640 | tf_op jit(solution)/shard_map/all_to_all | solution.py:131
  223.8 0.7 broadcast_in_dim.5
  224.5 10.4 %all-to-all-start.3 = ((bf16[32,24,128]{2,1,0:T(8,128)(2,1)}), bf16[32,24,128]{2,1,0:T(8,128)(2,1)S(1)}, u32[]{:S(2)}, u32[]{:S(2)}) async-start(bf16[32,24,128]{2,1,0:T(8,128)(2,1)} %broadcast_in_dim.5), calls=%async_computation.3 | async-start | bytes 393216 | tf_op jit(solution)/shard_map/all_to_all | solution.py:131
  234.9 0.0 copy-done.3
  234.9 0.2 fusion
  235.1 0.2 fusion.1
  235.4 0.4 fusion.7
  235.8 0.1 copy.6
  235.9 13.1 %all-to-all-done.3 = bf16[32,24,128]{2,1,0:T(8,128)(2,1)S(1)} async-done(((bf16[32,24,128]{2,1,0:T(8,128)(2,1)}), bf16[32,24,128]{2,1,0:T(8,128)(2,1)S(1)}, u32[]{:S(2)}, u32[]{:S(2)}) %all-to-all-start.3) | async-done | bytes 196640 | tf_op jit(solution)/shard_map/all_to_all | solution.py:131
  248.9 3.6 %shard_map.48 = bf16[384,16,128]{2,1,0:T(8,128)(2,1)S(1)} custom-call(bf16[768,128]{1,0:T(8,128)(2,1)S(1)} %bitcast.10, f32[32,32]{1,0:T(8,128)S(1)} %fusion.4.listed_ref, bf16[384,2048]{1,0:T(8,128)(2,1)S(1)} %get-tuple-element.8.amp_ref), custom_call_target="tpu_custom_call" | custom-call | tf_op jit(solution)/shard_map/pallas_call | solution.py:25
  252.5 81.0 %all_to_all.27.parts_ref = bf16[32,12,16,128]{3,2,1,0:T(8,128)(2,1)S(1)} all-to-all(bf16[32,12,16,128]{3,2,1,0:T(8,128)(2,1)S(1)} %bitcast.9), channel_id=1, replica_groups=mesh['pair'=32,'virt'=16] {'pair'}, dimensions={0} | all-to-all | bytes 3145728 | tf_op jit(solution)/shard_map/all_to_all | solution.py:131
  333.5 1.6 shard_map.49
  (4 shorter events, 0.1 us)
Async XLA Ops:
  0.0 1.4 copy-start
  1.4 1.4 copy-start.1
  164.5 43.7 %copy-start.2 = (s32[264,2]{0,1:T(2,128)S(1)}, s32[264,2]{0,1:T(2,128)}, u32[]{:S(2)}) copy-start(s32[264,2]{0,1:T(2,128)} %param.7) | copy-start | bytes 6340
  164.5 70.4 %copy-start.3 = (s32[32]{0:T(128)S(1)}, s32[32]{0:T(128)}, u32[]{:S(2)}) copy-start(s32[32]{0:T(128)} %param.6) | copy-start | bytes 388
  193.0 30.8 %all-to-all-start.2 = ((f32[16,24,128]{2,1,0:T(8,128)}), f32[16,24,128]{2,1,0:T(8,128)S(1)}, u32[]{:S(2)}, u32[]{:S(2)}) async-start(f32[16,24,128]{2,1,0:T(8,128)} %broadcast_in_dim.4), calls=%async_computation.2 | async-start | bytes 393216 | tf_op jit(solution)/shard_map/all_to_all | solution.py:131
  224.5 24.4 %all-to-all-start.3 = ((bf16[32,24,128]{2,1,0:T(8,128)(2,1)}), bf16[32,24,128]{2,1,0:T(8,128)(2,1)S(1)}, u32[]{:S(2)}, u32[]{:S(2)}) async-start(bf16[32,24,128]{2,1,0:T(8,128)(2,1)} %broadcast_in_dim.5), calls=%async_computation.3 | async-start | bytes 393216 | tf_op jit(solution)/shard_map/all_to_all | solution.py:131

commit v2 on v1

--- a/solution.py
+++ b/solution.py
@@ -3,7 +3,12 @@
 from jax import lax
 from jax.experimental import pallas as pl
 from jax.experimental.pallas import tpu as pltpu
-from jax.sharding import PartitionSpec as P
+from jax.sharding import Mesh, PartitionSpec as P
+
+PAIR = ("zl", "y")
+VIRT = ("zh", "x", "c")
+PLANE = ("y", "x", "c")
+LINE = ("zl", "zh")
 
 ROWS = 16
 LANES = 128
@@ -132,8 +137,7 @@
 
 
 def on_device(lambda_amps, t_amps, panel_home, pair_list):
-    npanels = lax.axis_size("pair")
-    nslabs = lax.axis_size("virt")
+    npanels = lax.axis_size(PAIR)
     panel_size, rows, cols = lambda_amps.shape
     pairs = npanels * panel_size
     depth = rows * cols // npanels
@@ -150,7 +154,7 @@
         jax.ShapeDtypeStruct((npanels, 2, panel_size, ROWS, LANES), bf16),
         (lambda_amps, t_amps),
     )
-    parts = exchange(parts, "pair")
+    parts = exchange(parts, PAIR)
     nblocks = len(upper_blocks(pairs))
     sym, amp = call(
         cross_kernel,
@@ -161,23 +165,25 @@
         (parts,),
         [pltpu.VMEM((pairs, depth), bf16)],
     )
-    own = nblocks * BLOCK // npanels
-    terms = exchange(sym.reshape(npanels, own, BLOCK), "pair")
-    terms = jnp.broadcast_to(jnp.sum(terms, axis=0), (nslabs, own, BLOCK))
-    total = jnp.sum(exchange(terms, "virt"), axis=0).astype(bf16)
-    upper = exchange(jnp.broadcast_to(total, (npanels, own, BLOCK)), "pair")
+    plane, height = lax.axis_size(PLANE), lax.axis_size(LINE)
+    own = nblocks * BLOCK // plane
+    terms = exchange(sym.reshape(plane, own, BLOCK), PLANE)
+    terms = jnp.broadcast_to(jnp.sum(terms, axis=0), (height, own, BLOCK))
+    total = jnp.sum(exchange(terms, LINE), axis=0).astype(bf16)
+    upper = exchange(jnp.broadcast_to(total, (plane, own, BLOCK)), PLANE)
     result = call(
         density_kernel,
         jax.ShapeDtypeStruct((pairs, ROWS, LANES), bf16),
         (upper.reshape(nblocks * BLOCK, BLOCK), listed, amp),
         [pltpu.VMEM((pairs, pairs), bf16), pltpu.VMEM((pairs, depth), bf16)],
     )
-    result = exchange(result.reshape(npanels, panel_size, ROWS, LANES), "pair")
+    result = exchange(result.reshape(npanels, panel_size, ROWS, LANES), PAIR)
     return call(unpack, jax.ShapeDtypeStruct(lambda_amps.shape, bf16), (result,))
 
 
 def solution(mesh):
-    placed = (P("pair", "virt", None), P("pair", "virt", None), P(), P())
+    fine = Mesh(mesh.devices.reshape(8, 4, 2, 4, 2), PAIR + VIRT)
+    placed = (P(PAIR, VIRT, None), P(PAIR, VIRT, None), P(), P())
     return jax.shard_map(
-        on_device, mesh=mesh, in_specs=placed, out_specs=P("pair", "virt", None), check_vma=False
+        on_device, mesh=fine, in_specs=placed, out_specs=P(PAIR, VIRT, None), check_vma=False
     )

time: 336 us -> 306 us (0.911)
  blocking collectives: 265 us -> 253 us
  starting transfers between devices: 25.5 us -> 14 us
  waiting for transfers between devices: 28.7 us -> 22.8 us
    all_to_all x3, blocking collectives: 265 us -> 253 us  [exchange(): return lax.all_to_all(x, axis, split_axis=0, concat_axis=0, tiled=True)]
    all_to_all x2, starting transfers between devices: 25.5 us -> 14 us  [exchange(): return lax.all_to_all(x, axis, split_axis=0, concat_axis=0, tiled=True)]
    all_to_all x2, waiting for transfers between devices: 28.7 us -> 22.8 us  [exchange(): return lax.all_to_all(x, axis, split_axis=0, concat_axis=0, tiled=True)]
where the time goes in v2:
time: 306 us
  blocking collectives  253 us (83%)
  waiting for transfers between devices  22.8 us (7%)
  starting transfers between devices  14 us (5%)
  Pallas kernels  10.8 us (4%)
  local copies, waits for them, and re-layouts  4.32 us (1%)
    all_to_all x3, blocking collectives, exchange(): return lax.all_to_all(x, axis, split_axis=0, concat_axis=0, tiled=True)  253 us
    all_to_all x2, waiting for transfers between devices, exchange(): return lax.all_to_all(x, axis, split_axis=0, concat_axis=0, tiled=True)  22.8 us
    all_to_all x2, starting transfers between devices, exchange(): return lax.all_to_all(x, axis, split_axis=0, concat_axis=0, tiled=True)  14 us
    pallas_call x4, Pallas kernels, call(): pl.pallas_call(body, out_shape=out_shape, in_specs=vmem(len(args)), out_s...  10.8 us
  transfers between devices with their start and end apart: 2, of which 2 were waited for; matrix products, arithmetic and copies ran while one was open for 0% of the time, Pallas kernels for 0%

profile of v2, /device:TPU:1, one launch (start us, length us, event | category | flops | bytes accessed | tf_op | source)
XLA Modules:
  0.0 305.9 jit_solution(8558315846735838012)
XLA Ops:
  0.0 0.0 copy-start
  0.0 1.4 copy-done
  1.4 0.0 copy-start.1
  1.4 1.4 copy-done.1
  2.8 2.2 shard_map.46
  5.0 156.0 %all_to_all.25.parts_ref = bf16[32,2,12,16,128]{4,3,2,1,0:T(8,128)(2,1)S(1)} all-to-all(bf16[32,2,12,16,128]{4,3,2,1,0:T(8,128)(2,1)} %shard_map.46), channel_id=1, replica_groups=mesh['zl'=8,'y'=4,'zh'=2,'x'=4,'c'=2] {'zl','y'}, dimensions={0} | all-to-all | bytes 6291456 | tf_op jit(solution)/shard_map/all_to_all | solution.py:136
  161.1 3.5 %shard_map.47 = (f32[768,128]{1,0:T(8,128)S(1)}, bf16[384,2048]{1,0:T(8,128)(2,1)S(1)}) custom-call(bf16[32,2,12,16,128]{4,3,2,1,0:T(8,128)(2,1)S(1)} %all_to_all.25.parts_ref), custom_call_target="tpu_custom_call" | custom-call | tf_op jit(solution)/shard_map/pallas_call | solution.py:30
  164.5 0.0 copy-start.2
  164.5 0.0 copy-start.3
  164.6 18.6 %all_to_all.26 = f32[32,24,128]{2,1,0:T(8,128)S(1)} all-to-all(f32[32,24,128]{2,1,0:T(8,128)S(1)} %bitcast.11), channel_id=1, replica_groups=mesh['zl'=8,'y'=4,'zh'=2,'x'=4,'c'=2] {'y','x','c'}, dimensions={0} | all-to-all | bytes 786432 | tf_op jit(solution)/shard_map/all_to_all | solution.py:136
  183.2 0.7 broadcast_in_dim.4
  183.9 7.4 %all-to-all-start.2 = ((f32[16,24,128]{2,1,0:T(8,128)}), f32[16,24,128]{2,1,0:T(8,128)S(1)}, u32[]{:S(2)}, u32[]{:S(2)}) async-start(f32[16,24,128]{2,1,0:T(8,128)} %broadcast_in_dim.4), calls=%async_computation.2 | async-start | bytes 393216 | tf_op jit(solution)/shard_map/all_to_all | solution.py:136
  191.3 0.0 copy-done.2
  191.3 0.0 copy-done.3
  191.4 0.2 fusion
  191.6 0.2 fusion.1
  191.8 0.4 fusion.7
  192.2 0.1 copy.6
  192.3 14.4 %all-to-all-done.2 = f32[16,24,128]{2,1,0:T(8,128)S(1)} async-done(((f32[16,24,128]{2,1,0:T(8,128)}), f32[16,24,128]{2,1,0:T(8,128)S(1)}, u32[]{:S(2)}, u32[]{:S(2)}) %all-to-all-start.2) | async-done | bytes 196640 | tf_op jit(solution)/shard_map/all_to_all | solution.py:136
  206.7 0.7 broadcast_in_dim.5
  207.4 6.6 %all-to-all-start.3 = ((bf16[32,24,128]{2,1,0:T(8,128)(2,1)}), bf16[32,24,128]{2,1,0:T(8,128)(2,1)S(1)}, u32[]{:S(2)}, u32[]{:S(2)}) async-start(bf16[32,24,128]{2,1,0:T(8,128)(2,1)} %broadcast_in_dim.5), calls=%async_computation.3 | async-start | bytes 393216 | tf_op jit(solution)/shard_map/all_to_all | solution.py:136
  214.0 8.4 %all-to-all-done.3 = bf16[32,24,128]{2,1,0:T(8,128)(2,1)S(1)} async-done(((bf16[32,24,128]{2,1,0:T(8,128)(2,1)}), bf16[32,24,128]{2,1,0:T(8,128)(2,1)S(1)}, u32[]{:S(2)}, u32[]{:S(2)}) %all-to-all-start.3) | async-done | bytes 196640 | tf_op jit(solution)/shard_map/all_to_all | solution.py:136
  222.4 3.6 %shard_map.48 = bf16[384,16,128]{2,1,0:T(8,128)(2,1)S(1)} custom-call(bf16[768,128]{1,0:T(8,128)(2,1)S(1)} %bitcast.10, f32[32,32]{1,0:T(8,128)S(1)} %fusion.4.listed_ref, bf16[384,2048]{1,0:T(8,128)(2,1)S(1)} %get-tuple-element.8.amp_ref), custom_call_target="tpu_custom_call" | custom-call | tf_op jit(solution)/shard_map/pallas_call | solution.py:30
  226.0 78.3 %all_to_all.27.parts_ref = bf16[32,12,16,128]{3,2,1,0:T(8,128)(2,1)S(1)} all-to-all(bf16[32,12,16,128]{3,2,1,0:T(8,128)(2,1)S(1)} %bitcast.9), channel_id=1, replica_groups=mesh['zl'=8,'y'=4,'zh'=2,'x'=4,'c'=2] {'zl','y'}, dimensions={0} | all-to-all | bytes 3145728 | tf_op jit(solution)/shard_map/all_to_all | solution.py:136
  304.3 1.6 shard_map.49
  (4 shorter events, 0.1 us)
Async XLA Ops:
  0.0 1.4 copy-start
  1.4 1.4 copy-start.1
  164.5 26.8 %copy-start.2 = (s32[264,2]{0,1:T(2,128)S(1)}, s32[264,2]{0,1:T(2,128)}, u32[]{:S(2)}) copy-start(s32[264,2]{0,1:T(2,128)} %param.7) | copy-start | bytes 6340
  164.5 26.8 %copy-start.3 = (s32[32]{0:T(128)S(1)}, s32[32]{0:T(128)}, u32[]{:S(2)}) copy-start(s32[32]{0:T(128)} %param.6) | copy-start | bytes 388
  183.9 22.8 %all-to-all-start.2 = ((f32[16,24,128]{2,1,0:T(8,128)}), f32[16,24,128]{2,1,0:T(8,128)S(1)}, u32[]{:S(2)}, u32[]{:S(2)}) async-start(f32[16,24,128]{2,1,0:T(8,128)} %broadcast_in_dim.4), calls=%async_computation.2 | async-start | bytes 393216 | tf_op jit(solution)/shard_map/all_to_all | solution.py:136
  207.4 15.0 %all-to-all-start.3 = ((bf16[32,24,128]{2,1,0:T(8,128)(2,1)}), bf16[32,24,128]{2,1,0:T(8,128)(2,1)S(1)}, u32[]{:S(2)}, u32[]{:S(2)}) async-start(bf16[32,24,128]{2,1,0:T(8,128)(2,1)} %broadcast_in_dim.5), calls=%async_computation.3 | async-start | bytes 393216 | tf_op jit(solution)/shard_map/all_to_all | solution.py:136

commit v3 on v2

v3 whole, which is shorter than its diff:
```python
import jax
import jax.numpy as jnp
from jax import lax
from jax.experimental import pallas as pl
from jax.experimental.pallas import tpu as pltpu
from jax.sharding import Mesh, PartitionSpec as P

HALF = ("z4", "y")
PAIR = ("zb",) + HALF
VIRT = ("zh", "x", "c")
PLANE = ("y", "x", "c")
LINE = ("zb", "z4", "zh")

ROWS = 16
LANES = 128
TILES = 2
WIDE = TILES * LANES
SIDE = ROWS * ROWS
STEPS = 4
BLOCK = 128
VMEM_LIMIT = 48 * 1024 * 1024


def onehot(index, count):
    return (index[:, None] == jnp.arange(count)[None, :]).astype(jnp.float32)


def call(body, out_shape, args, scratch=(), scalars=0):
    many = isinstance(out_shape, (list, tuple))
    outs = out_shape if many else [out_shape]
    smem, vmem = (pl.BlockSpec(memory_space=m) for m in (pltpu.SMEM, pltpu.VMEM))
    return pl.pallas_call(
        body,
        out_shape=out_shape,
        in_specs=[smem] * scalars + [vmem] * (len(args) - scalars),
        out_specs=[vmem] * len(outs) if many else vmem,
        scratch_shapes=list(scratch),
        compiler_params=pltpu.CompilerParams(vmem_limit_bytes=VMEM_LIMIT),
    )(*args)


def pack_amp(amp_ref, out_ref):
    across = amp_ref.shape[2] // WIDE
    parts = amp_ref.shape[1] // ROWS * across
    for d in range(parts):
        i, c = divmod(d, across)
        for tile in range(TILES):
            at = c * WIDE + tile * LANES
            part = amp_ref[:, i * ROWS : (i + 1) * ROWS, at : at + LANES]
            out_ref[d, tile] = part
            out_ref[parts + d, tile] = part


def pack_lam(where_ref, lam_ref, *out_refs):
    y = where_ref[2]
    for s, out_ref in enumerate(out_refs):
        for i in range(lam_ref.shape[1] // ROWS):
            for tile in range(TILES):
                at = pl.multiple_of((y ^ s) * WIDE + tile * LANES, LANES)
                out_ref[i, tile] = lam_ref[:, i * ROWS : (i + 1) * ROWS, pl.ds(at, LANES)]


def regroup(where_ref, *refs):
    z4 = where_ref[1]
    ins, outs = refs[:STEPS], refs[STEPS:]
    for u, out_ref in enumerate(outs):
        for s, in_ref in enumerate(ins):
            out_ref[s] = in_ref[z4 ^ u]


def unpack(parts_ref, out_ref):
    across = out_ref.shape[2] // WIDE
    for d in range(parts_ref.shape[0]):
        i, c = divmod(d, across)
        for tile in range(TILES):
            at = c * WIDE + tile * LANES
            out_ref[:, i * ROWS : (i + 1) * ROWS, at : at + LANES] = parts_ref[d, :, tile]


def swap_matrix():
    i = lax.broadcasted_iota(jnp.int32, (SIDE, SIDE), 0)
    j = lax.broadcasted_iota(jnp.int32, (SIDE, SIDE), 1)
    return (j == (i % ROWS) * ROWS + i // ROWS).astype(jnp.float32).astype(jnp.bfloat16)


def to_matrix(swap, tiles, out_ref, first):
    both = jnp.concatenate(tiles, axis=1)
    for q in range(both.shape[0] // SIDE):
        moved = jnp.dot(swap, both[q * SIDE : (q + 1) * SIDE], preferred_element_type=jnp.float32)
        moved = moved.astype(jnp.bfloat16)
        at = pl.ds(pl.multiple_of(first + q * ROWS, ROWS), ROWS)
        for s in range(ROWS):
            out_ref[at, s * WIDE : (s + 1) * WIDE] = moved[s * ROWS : (s + 1) * ROWS]


def upper_blocks(pairs):
    n = pairs // BLOCK
    return [(i, j) for i in range(n) for j in range(i, n)]


def cross_kernel(where_ref, *refs):
    lam_refs, (parts_ref, sym_ref, amp_ref, lam_ref, cross_ref) = refs[:STEPS], refs[STEPS:]
    zb, z4, y = where_ref[0], where_ref[1], where_ref[2]
    swap = swap_matrix()
    panels, _, panel_size = parts_ref.shape[:3]
    chunk = STEPS * panel_size

    def relayout(step, carry):
        tiles = [parts_ref[pl.ds(STEPS * step, STEPS), tile].reshape(chunk * ROWS, LANES) for tile in range(TILES)]
        to_matrix(swap, tiles, amp_ref, step * chunk)
        return carry

    lax.fori_loop(0, panels // STEPS, relayout, 0)
    for u, part_ref in enumerate(lam_refs):
        tiles = [
            jnp.concatenate([part_ref[y ^ k, tile].reshape(panel_size * ROWS, LANES) for k in range(STEPS)], axis=0)
            for tile in range(TILES)
        ]
        to_matrix(swap, tiles, lam_ref, (z4 ^ u) * chunk)
    half = lam_ref.shape[0]
    cross = lax.dot_general(
        lam_ref[...], amp_ref[...], (((1,), (1,)), ((), ())), preferred_element_type=jnp.float32
    )
    cross_ref[pl.ds(pl.multiple_of(zb * half, half), half)] = cross
    cross_ref[pl.ds(pl.multiple_of((1 - zb) * half, half), half)] = jnp.zeros_like(cross)
    sym = 0.5 * (cross_ref[...] + cross_ref[...].T)
    for n, (i, j) in enumerate(upper_blocks(2 * half)):
        sym_ref[n * BLOCK : (n + 1) * BLOCK] = sym[i * BLOCK : (i + 1) * BLOCK, j * BLOCK : (j + 1) * BLOCK]


def density_kernel(where_ref, upper_ref, listed_ref, amp_ref, out_ref, inter_ref, flat_ref):
    pairs, depth = amp_ref.shape
    half = flat_ref.shape[0]
    panels = listed_ref.shape[0]
    panel_size = pairs // panels
    row = lax.broadcasted_iota(jnp.int32, (pairs, panels), 0)
    first = lax.broadcasted_iota(jnp.int32, (pairs, panels), 1) * panel_size
    spread = ((row >= first) & (row < first + panel_size)).astype(jnp.float32)
    mask = jnp.dot(spread, listed_ref[...], preferred_element_type=jnp.float32)
    mask = lax.dot_general(mask, spread, (((1,), (1,)), ((), ())), preferred_element_type=jnp.float32)
    for n, (i, j) in enumerate(upper_blocks(pairs)):
        block = upper_ref[n * BLOCK : (n + 1) * BLOCK].astype(jnp.float32)
        rows, cols = slice(i * BLOCK, (i + 1) * BLOCK), slice(j * BLOCK, (j + 1) * BLOCK)
        inter_ref[rows, cols] = (block * mask[rows, cols]).astype(jnp.bfloat16)
        if i != j:
            inter_ref[cols, rows] = (block.T * mask[cols, rows]).astype(jnp.bfloat16)
    own = inter_ref[pl.ds(pl.multiple_of(where_ref[0] * half, half), half)]
    for c in range(depth // WIDE):
        flat_ref[:, c * WIDE : (c + 1) * WIDE] = jnp.dot(
            own, amp_ref[:, c * WIDE : (c + 1) * WIDE], preferred_element_type=jnp.float32
        ).astype(jnp.bfloat16)
    swap = swap_matrix()

    def relayout(step, carry):
        rows = pl.ds(pl.multiple_of(step * ROWS, ROWS), ROWS)
        both = jnp.concatenate([flat_ref[rows, s * WIDE : (s + 1) * WIDE] for s in range(ROWS)], axis=0)
        moved = jnp.dot(swap, both, preferred_element_type=jnp.float32).astype(jnp.bfloat16)
        for tile in range(TILES):
            out_ref[rows, tile] = moved[:, tile * LANES : (tile + 1) * LANES].reshape(ROWS, ROWS, LANES)
        return carry

    lax.fori_loop(0, half // ROWS, relayout, 0)


def exchange(x, axis):
    return lax.all_to_all(x, axis, split_axis=0, concat_axis=0, tiled=True)


def shifts(parts, axis):
    return [parts[0]] + [
        lax.ppermute(part, axis, [(k, k ^ s) for k in range(STEPS)]) for s, part in enumerate(parts) if s > 0
    ]


def on_device(lambda_amps, t_amps, panel_home, pair_list):
    npanels = lax.axis_size(PAIR)
    panel_size, rows, cols = lambda_amps.shape
    pairs, half = npanels * panel_size, npanels * panel_size // 2
    depth = ROWS * WIDE
    bf16, f32 = jnp.bfloat16, jnp.float32
    where = jnp.stack([lax.axis_index("zb"), lax.axis_index("z4"), lax.axis_index("y")]).astype(jnp.int32)

    home = onehot(panel_home, npanels)
    first = jnp.dot(onehot(pair_list[:, 0], npanels), home, precision=lax.Precision.HIGHEST)
    second = jnp.dot(onehot(pair_list[:, 1], npanels), home, precision=lax.Precision.HIGHEST)
    listed = jnp.dot(first.T, second, precision=lax.Precision.HIGHEST)
    listed = jnp.minimum(listed + listed.T, 1.0)

    part = (TILES, panel_size, ROWS, LANES)
    amp_parts = call(pack_amp, jax.ShapeDtypeStruct((npanels,) + part, bf16), (t_amps,))
    amp_parts = exchange(amp_parts, PAIR)
    four = [jax.ShapeDtypeStruct((STEPS,) + part, bf16)] * STEPS
    lam_parts = shifts(call(pack_lam, four, (where, lambda_amps), scalars=1), "y")
    lam_parts = shifts(call(regroup, four, (where, *lam_parts), scalars=1), "z4")
    nblocks = len(upper_blocks(pairs))
    sym, amp = call(
        cross_kernel,
        [
            jax.ShapeDtypeStruct((nblocks * BLOCK, BLOCK), f32),
            jax.ShapeDtypeStruct((pairs, depth), bf16),
        ],
        (where, *lam_parts, amp_parts),
        [pltpu.VMEM((half, depth), bf16), pltpu.VMEM((pairs, pairs), f32)],
        scalars=1,
    )
    plane, height = lax.axis_size(PLANE), lax.axis_size(LINE)
    own = nblocks * BLOCK // plane
    terms = exchange(sym.reshape(plane, own, BLOCK), PLANE)
    terms = jnp.broadcast_to(jnp.sum(terms, axis=0), (height, own, BLOCK))
    total = jnp.sum(exchange(terms, LINE), axis=0).astype(bf16)
    upper = exchange(jnp.broadcast_to(total, (plane, own, BLOCK)), PLANE)
    result = call(
        density_kernel,
        jax.ShapeDtypeStruct((half, TILES, ROWS, LANES), bf16),
        (where, upper.reshape(nblocks * BLOCK, BLOCK), listed, amp),
        [pltpu.VMEM((pairs, pairs), bf16), pltpu.VMEM((half, depth), bf16)],
        scalars=1,
    )
    result = exchange(result.reshape(npanels // 2, panel_size, TILES, ROWS, LANES), HALF)
    return call(unpack, jax.ShapeDtypeStruct(lambda_amps.shape, bf16), (result,))


def solution(mesh):
    fine = Mesh(mesh.devices.reshape(2, 4, 4, 2, 4, 2), PAIR + VIRT)
    placed = (P(PAIR, VIRT, None), P(PAIR, VIRT, None), P(), P())
    return jax.shard_map(
        on_device, mesh=fine, in_specs=placed, out_specs=P(PAIR, VIRT, None), check_vma=False
    )
```

time: 306 us -> 290 us (0.948)
  blocking collectives: 253 us -> 59.2 us
  waiting for transfers between devices: 22.8 us -> 153 us
  starting transfers between devices: 14 us -> 49.7 us
  Pallas kernels: 10.8 us -> 15.6 us
  local copies, waits for them, and re-layouts: 4.32 us -> 8.91 us
    all_to_all x3 -> x2, blocking collectives: 253 us -> 59.2 us  [exchange(): return lax.all_to_all(x, axis, split_axis=0, concat_axis=0, tiled=True)]
    ppermute x0 -> x6, waiting for transfers between devices: none -> 132 us  [shifts(): lax.ppermute(part, axis, [(k, k ^ s) for k in range(STEPS)])]
    ppermute x0 -> x6, starting transfers between devices: none -> 19.3 us  [shifts(): lax.ppermute(part, axis, [(k, k ^ s) for k in range(STEPS)])]
    all_to_all x2 -> x3, starting transfers between devices: 14 us -> 30.3 us  [exchange(): return lax.all_to_all(x, axis, split_axis=0, concat_axis=0, tiled=True)]
    pallas_call x4 -> x6, Pallas kernels: 10.8 us -> 15.6 us  [call(): pl.pallas_call(body, out_shape=out_shape, in_specs=[smem] * scalars + [vm...]
    unnamed x8 -> x16, local copies, waits for them, and re-layouts: 2.83 us -> 6.66 us
    all_to_all x2 -> x3, waiting for transfers between devices: 22.8 us -> 20.7 us  [exchange(): return lax.all_to_all(x, axis, split_axis=0, concat_axis=0, tiled=True)]
  transfers between devices with their start and end apart: 2 -> 9, of which waited for: 2 -> 8; matrix products, arithmetic and copies ran while one was open for 0% -> 1% of each run, Pallas kernels for 0% -> 1%
where the time goes in v3:
time: 290 us; the launch traced here: 289 us
  waiting for transfers between devices  153 us (53%)
  blocking collectives  59.2 us (20%)
  starting transfers between devices  49.7 us (17%)
  Pallas kernels  15.6 us (5%)
  local copies, waits for them, and re-layouts  8.91 us (3%)
    ppermute x6, waiting for transfers between devices, shifts(): lax.ppermute(part, axis, [(k, k ^ s) for k in range(STEPS)])  132 us
    all_to_all x2, blocking collectives, exchange(): return lax.all_to_all(x, axis, split_axis=0, concat_axis=0, tiled=True)  59.2 us
    all_to_all x3, starting transfers between devices, exchange(): return lax.all_to_all(x, axis, split_axis=0, concat_axis=0, tiled=True)  30.3 us
    all_to_all x3, waiting for transfers between devices, exchange(): return lax.all_to_all(x, axis, split_axis=0, concat_axis=0, tiled=True)  20.7 us
    ppermute x6, starting transfers between devices, shifts(): lax.ppermute(part, axis, [(k, k ^ s) for k in range(STEPS)])  19.3 us
    pallas_call x6, Pallas kernels, call(): pl.pallas_call(body, out_shape=out_shape, in_specs=[smem] * scalars + [vm...  15.6 us
    unnamed x16, local copies, waits for them, and re-layouts  6.66 us
  transfers between devices with their start and end apart: 9, of which 8 were waited for; matrix products, arithmetic and copies ran while one was open for 1% of the time, Pallas kernels for 1%

profile of v3, /device:TPU:1, one launch (start us, length us, event | category | flops | bytes accessed | tf_op | source)
XLA Modules:
  0.0 288.5 jit_solution(8151996613296736316)
XLA Ops:
  0.0 0.0 copy-start.1
  0.0 1.4 copy-done.1
  1.4 2.1 shard_map.48
  3.5 0.0 copy-start
  3.5 16.3 %all-to-all-start = ((bf16[32,2,12,16,128]{4,3,2,1,0:T(8,128)(2,1)}), bf16[32,2,12,16,128]{4,3,2,1,0:T(8,128)(2,1)}, u32[]{:S(2)}, u32[]{:S(2)}) async-start(bf16[32,2,12,16,128]{4,3,2,1,0:T(8,128)(2,1)} %shard_map.48), calls=%async_computation | async-start | bytes 6291456 | tf_op jit(solution)/shard_map/all_to_all | solution.py:166
  19.8 0.1 pad_add_fusion.where_ref
  19.9 0.0 copy-done
  19.9 1.0 shard_map.46
  20.9 3.1 %collective-permute-start = (bf16[4,2,12,16,128]{4,3,2,1,0:T(8,128)(2,1)S(1)}, bf16[4,2,12,16,128]{4,3,2,1,0:T(8,128)(2,1)S(1)}, u32[]{:S(2)}, u32[]{:S(2)}) collective-permute-start(bf16[4,2,12,16,128]{4,3,2,1,0:T(8,128)(2,1)S(1)} %get-tuple-element.16), channel_id=1, source_target_pairs={{0,16},{16,0},{32,48},{48,32},{1,17},{17,1},{33,49},{49,33},{2,18}... | collective-permute-start | bytes 1179656 | tf_op jit(solution)/shard_map/ppermute | solution.py:171
  24.0 4.3 %collective-permute-start.1 = (bf16[4,2,12,16,128]{4,3,2,1,0:T(8,128)(2,1)S(1)}, bf16[4,2,12,16,128]{4,3,2,1,0:T(8,128)(2,1)S(1)}, u32[]{:S(2)}, u32[]{:S(2)}) collective-permute-start(bf16[4,2,12,16,128]{4,3,2,1,0:T(8,128)(2,1)S(1)} %get-tuple-element.17), channel_id=1, source_target_pairs={{0,32},{16,48},{32,0},{48,16},{1,33},{17,49},{33,1},{49,17},{2,34}... | collective-permute-start | bytes 1179656 | tf_op jit(solution)/shard_map/ppermute | solution.py:171
  28.3 2.2 collective-permute-start.2
  30.5 12.4 %collective-permute-done.refs_1_ = bf16[4,2,12,16,128]{4,3,2,1,0:T(8,128)(2,1)S(1)} collective-permute-done((bf16[4,2,12,16,128]{4,3,2,1,0:T(8,128)(2,1)S(1)}, bf16[4,2,12,16,128]{4,3,2,1,0:T(8,128)(2,1)S(1)}, u32[]{:S(2)}, u32[]{:S(2)}) %collective-permute-start) | collective-permute-done | bytes 393248 | tf_op jit(solution)/shard_map/ppermute | solution.py:171
  42.9 9.1 %collective-permute-done.1.refs_2_ = bf16[4,2,12,16,128]{4,3,2,1,0:T(8,128)(2,1)S(1)} collective-permute-done((bf16[4,2,12,16,128]{4,3,2,1,0:T(8,128)(2,1)S(1)}, bf16[4,2,12,16,128]{4,3,2,1,0:T(8,128)(2,1)S(1)}, u32[]{:S(2)}, u32[]{:S(2)}) %collective-permute-start.1) | collective-permute-done | bytes 393248 | tf_op jit(solution)/shard_map/ppermute | solution.py:171
  52.0 6.6 %collective-permute-done.2.refs_3_ = bf16[4,2,12,16,128]{4,3,2,1,0:T(8,128)(2,1)S(1)} collective-permute-done((bf16[4,2,12,16,128]{4,3,2,1,0:T(8,128)(2,1)S(1)}, bf16[4,2,12,16,128]{4,3,2,1,0:T(8,128)(2,1)S(1)}, u32[]{:S(2)}, u32[]{:S(2)}) %collective-permute-start.2) | collective-permute-done | bytes 393248 | tf_op jit(solution)/shard_map/ppermute | solution.py:171
  58.7 0.6 shard_map.47
  59.3 3.8 %collective-permute-start.3 = (bf16[4,2,12,16,128]{4,3,2,1,0:T(8,128)(2,1)S(1)}, bf16[4,2,12,16,128]{4,3,2,1,0:T(8,128)(2,1)S(1)}, u32[]{:S(2)}, u32[]{:S(2)}) collective-permute-start(bf16[4,2,12,16,128]{4,3,2,1,0:T(8,128)(2,1)S(1)} %get-tuple-element.20), channel_id=1, source_target_pairs={{0,64},{64,0},{128,192},{192,128},{1,65},{65,1},{129,193},{193,129... | collective-permute-start | bytes 1179656 | tf_op jit(solution)/shard_map/ppermute | solution.py:171
  63.2 1.9 collective-permute-start.4
  65.1 4.0 %collective-permute-start.5 = (bf16[4,2,12,16,128]{4,3,2,1,0:T(8,128)(2,1)S(1)}, bf16[4,2,12,16,128]{4,3,2,1,0:T(8,128)(2,1)S(1)}, u32[]{:S(2)}, u32[]{:S(2)}) collective-permute-start(bf16[4,2,12,16,128]{4,3,2,1,0:T(8,128)(2,1)S(1)} %get-tuple-element.22), channel_id=1, source_target_pairs={{0,192},{64,128},{128,64},{192,0},{1,193},{65,129},{129,65},{193,1... | collective-permute-start | bytes 1179656 | tf_op jit(solution)/shard_map/ppermute | solution.py:171
  69.1 17.4 %collective-permute-done.3.refs_1_ = bf16[4,2,12,16,128]{4,3,2,1,0:T(8,128)(2,1)S(1)} collective-permute-done((bf16[4,2,12,16,128]{4,3,2,1,0:T(8,128)(2,1)S(1)}, bf16[4,2,12,16,128]{4,3,2,1,0:T(8,128)(2,1)S(1)}, u32[]{:S(2)}, u32[]{:S(2)}) %collective-permute-start.3) | collective-permute-done | bytes 393248 | tf_op jit(solution)/shard_map/ppermute | solution.py:171
  86.5 0.0 copy-start.2
  86.5 0.7 copy-done.2
  87.2 7.7 %collective-permute-done.4.refs_2_ = bf16[4,2,12,16,128]{4,3,2,1,0:T(8,128)(2,1)S(1)} collective-permute-done((bf16[4,2,12,16,128]{4,3,2,1,0:T(8,128)(2,1)S(1)}, bf16[4,2,12,16,128]{4,3,2,1,0:T(8,128)(2,1)S(1)}, u32[]{:S(2)}, u32[]{:S(2)}) %collective-permute-start.4) | collective-permute-done | bytes 393248 | tf_op jit(solution)/shard_map/ppermute | solution.py:171
  95.0 0.8 copy-done.4
  95.7 78.7 %collective-permute-done.5.refs_3_ = bf16[4,2,12,16,128]{4,3,2,1,0:T(8,128)(2,1)S(1)} collective-permute-done((bf16[4,2,12,16,128]{4,3,2,1,0:T(8,128)(2,1)S(1)}, bf16[4,2,12,16,128]{4,3,2,1,0:T(8,128)(2,1)S(1)}, u32[]{:S(2)}, u32[]{:S(2)}) %collective-permute-start.5) | collective-permute-done | bytes 393248 | tf_op jit(solution)/shard_map/ppermute | solution.py:171
  174.4 0.0 copy-start.6
  174.4 0.8 copy-done.6
  175.1 0.0 all-to-all-done.refs_4_
  175.2 0.0 copy-start.3
  175.2 1.0 copy-done.3
  176.2 0.0 copy-start.5
  176.2 1.0 copy-done.5
  177.1 1.0 copy-done.7
  178.1 6.2 %shard_map.49 = (f32[768,128]{1,0:T(8,128)S(1)}, bf16[384,4096]{1,0:T(8,128)(2,1)S(1)}) custom-call(s32[3]{0:T(128)S(1)} %pad_add_fusion.where_ref, bf16[4,2,12,16,128]{4,3,2,1,0:T(8,128)(2,1)S(1)} %get-tuple-element.19.refs_0_, bf16[4,2,12,16,128]{4,3,2,1,0:T(8,128)(2,1)S(1)} %copy-done.3, bf16[4,2,12,16,128]{4,3,2,1,0:T(8,128)(2,1)S(1)} %copy-done.5, ...), custom_call_target="tpu_custom_call" | custom-call | tf_op jit(solution)/shard_map/pallas_call | solution.py:32
  184.3 18.7 %all_to_all.25 = f32[32,24,128]{2,1,0:T(8,128)S(1)} all-to-all(f32[32,24,128]{2,1,0:T(8,128)S(1)} %bitcast.14), channel_id=1, replica_groups=mesh['zb'=2,'z4'=4,'y'=4,'zh'=2,'x'=4,'c'=2] {'y','x','c'}, dimensions={0} | all-to-all | bytes 786432 | tf_op jit(solution)/shard_map/all_to_all | solution.py:166
  203.0 0.7 broadcast_in_dim.4
  203.7 7.4 %all-to-all-start.2 = ((f32[16,24,128]{2,1,0:T(8,128)}), f32[16,24,128]{2,1,0:T(8,128)S(1)}, u32[]{:S(2)}, u32[]{:S(2)}) async-start(f32[16,24,128]{2,1,0:T(8,128)} %broadcast_in_dim.4), calls=%async_computation.2 | async-start | bytes 393216 | tf_op jit(solution)/shard_map/all_to_all | solution.py:166
  211.2 0.8 slice_reduce_fusion
  211.9 0.9 fusion
  212.8 0.9 fusion.1
  213.7 0.4 fusion.7
  214.1 0.1 copy.6
  214.2 12.4 %all-to-all-done.2 = f32[16,24,128]{2,1,0:T(8,128)S(1)} async-done(((f32[16,24,128]{2,1,0:T(8,128)}), f32[16,24,128]{2,1,0:T(8,128)S(1)}, u32[]{:S(2)}, u32[]{:S(2)}) %all-to-all-start.2) | async-done | bytes 196640 | tf_op jit(solution)/shard_map/all_to_all | solution.py:166
  226.6 0.7 broadcast_in_dim.5
  227.3 6.6 %all-to-all-start.3 = ((bf16[32,24,128]{2,1,0:T(8,128)(2,1)}), bf16[32,24,128]{2,1,0:T(8,128)(2,1)S(1)}, u32[]{:S(2)}, u32[]{:S(2)}) async-start(bf16[32,24,128]{2,1,0:T(8,128)(2,1)} %broadcast_in_dim.5), calls=%async_computation.3 | async-start | bytes 393216 | tf_op jit(solution)/shard_map/all_to_all | solution.py:166
  233.9 8.4 %all-to-all-done.3 = bf16[32,24,128]{2,1,0:T(8,128)(2,1)S(1)} async-done(((bf16[32,24,128]{2,1,0:T(8,128)(2,1)}), bf16[32,24,128]{2,1,0:T(8,128)(2,1)S(1)}, u32[]{:S(2)}, u32[]{:S(2)}) %all-to-all-start.3) | async-done | bytes 196640 | tf_op jit(solution)/shard_map/all_to_all | solution.py:166
  242.2 4.2 %shard_map.50 = bf16[192,2,16,128]{3,2,1,0:T(8,128)(2,1)S(1)} custom-call(s32[3]{0:T(128)S(1)} %pad_add_fusion.where_ref, bf16[768,128]{1,0:T(8,128)(2,1)S(1)} %bitcast.13, f32[32,32]{1,0:T(8,128)S(1)} %fusion.4.listed_ref, bf16[384,4096]{1,0:T(8,128)(2,1)S(1)} %get-tuple-element.24.amp_ref), custom_call_target="tpu_custom_call" | custom-call | tf_op jit(solution)/shard_map/pallas_call | solution.py:32
  246.4 40.5 %all_to_all.26.parts_ref = bf16[16,12,2,16,128]{4,3,2,1,0:T(8,128)(2,1)S(1)} all-to-all(bf16[16,12,2,16,128]{4,3,2,1,0:T(8,128)(2,1)S(1)} %bitcast.12), channel_id=1, replica_groups=mesh['zb'=2,'z4'=4,'y'=4,'zh'=2,'x'=4,'c'=2] {'z4','y'}, dimensions={0} | all-to-all | bytes 3145728 | tf_op jit(solution)/shard_map/all_to_all | solution.py:166
  287.0 1.6 shard_map.51
  (5 shorter events, 0.1 us)
Async XLA Ops:
  0.0 1.4 copy-start.1
  3.5 16.4 %copy-start = (bf16[12,64,1024]{2,1,0:T(8,128)(2,1)S(1)}, bf16[12,64,1024]{2,1,0:T(8,128)(2,1)}, u32[]{:S(2)}) copy-start(bf16[12,64,1024]{2,1,0:T(8,128)(2,1)} %lam_ref.1) | copy-start | bytes 4718596
  3.5 171.7 %all-to-all-start = ((bf16[32,2,12,16,128]{4,3,2,1,0:T(8,128)(2,1)}), bf16[32,2,12,16,128]{4,3,2,1,0:T(8,128)(2,1)}, u32[]{:S(2)}, u32[]{:S(2)}) async-start(bf16[32,2,12,16,128]{4,3,2,1,0:T(8,128)(2,1)} %shard_map.48), calls=%async_computation | async-start | bytes 6291456 | tf_op jit(solution)/shard_map/all_to_all | solution.py:166
  20.9 22.0 %collective-permute-start = (bf16[4,2,12,16,128]{4,3,2,1,0:T(8,128)(2,1)S(1)}, bf16[4,2,12,16,128]{4,3,2,1,0:T(8,128)(2,1)S(1)}, u32[]{:S(2)}, u32[]{:S(2)}) collective-permute-start(bf16[4,2,12,16,128]{4,3,2,1,0:T(8,128)(2,1)S(1)} %get-tuple-element.16), channel_id=1, source_target_pairs={{0,16},{16,0},{32,48},{48,32},{1,17},{17,1},{33,49},{49,33},{2,18}... | collective-permute-start | bytes 1179656 | tf_op jit(solution)/shard_map/ppermute | solution.py:171
  24.0 28.1 %collective-permute-start.1 = (bf16[4,2,12,16,128]{4,3,2,1,0:T(8,128)(2,1)S(1)}, bf16[4,2,12,16,128]{4,3,2,1,0:T(8,128)(2,1)S(1)}, u32[]{:S(2)}, u32[]{:S(2)}) collective-permute-start(bf16[4,2,12,16,128]{4,3,2,1,0:T(8,128)(2,1)S(1)} %get-tuple-element.17), channel_id=1, source_target_pairs={{0,32},{16,48},{32,0},{48,16},{1,33},{17,49},{33,1},{49,17},{2,34}... | collective-permute-start | bytes 1179656 | tf_op jit(solution)/shard_map/ppermute | solution.py:171
  28.3 30.4 %collective-permute-start.2 = (bf16[4,2,12,16,128]{4,3,2,1,0:T(8,128)(2,1)S(1)}, bf16[4,2,12,16,128]{4,3,2,1,0:T(8,128)(2,1)S(1)}, u32[]{:S(2)}, u32[]{:S(2)}) collective-permute-start(bf16[4,2,12,16,128]{4,3,2,1,0:T(8,128)(2,1)S(1)} %get-tuple-element.18), channel_id=1, source_target_pairs={{0,48},{16,32},{32,16},{48,0},{1,49},{17,33},{33,17},{49,1},{2,50}... | collective-permute-start | bytes 1179656 | tf_op jit(solution)/shard_map/ppermute | solution.py:171
  59.3 27.2 %collective-permute-start.3 = (bf16[4,2,12,16,128]{4,3,2,1,0:T(8,128)(2,1)S(1)}, bf16[4,2,12,16,128]{4,3,2,1,0:T(8,128)(2,1)S(1)}, u32[]{:S(2)}, u32[]{:S(2)}) collective-permute-start(bf16[4,2,12,16,128]{4,3,2,1,0:T(8,128)(2,1)S(1)} %get-tuple-element.20), channel_id=1, source_target_pairs={{0,64},{64,0},{128,192},{192,128},{1,65},{65,1},{129,193},{193,129... | collective-permute-start | bytes 1179656 | tf_op jit(solution)/shard_map/ppermute | solution.py:171
  63.2 31.8 %collective-permute-start.4 = (bf16[4,2,12,16,128]{4,3,2,1,0:T(8,128)(2,1)S(1)}, bf16[4,2,12,16,128]{4,3,2,1,0:T(8,128)(2,1)S(1)}, u32[]{:S(2)}, u32[]{:S(2)}) collective-permute-start(bf16[4,2,12,16,128]{4,3,2,1,0:T(8,128)(2,1)S(1)} %get-tuple-element.21), channel_id=1, source_target_pairs={{0,128},{64,192},{128,0},{192,64},{1,129},{65,193},{129,1},{193,65... | collective-permute-start | bytes 1179656 | tf_op jit(solution)/shard_map/ppermute | solution.py:171
  65.1 109.3 %collective-permute-start.5 = (bf16[4,2,12,16,128]{4,3,2,1,0:T(8,128)(2,1)S(1)}, bf16[4,2,12,16,128]{4,3,2,1,0:T(8,128)(2,1)S(1)}, u32[]{:S(2)}, u32[]{:S(2)}) collective-permute-start(bf16[4,2,12,16,128]{4,3,2,1,0:T(8,128)(2,1)S(1)} %get-tuple-element.22), channel_id=1, source_target_pairs={{0,192},{64,128},{128,64},{192,0},{1,193},{65,129},{129,65},{193,1... | collective-permute-start | bytes 1179656 | tf_op jit(solution)/shard_map/ppermute | solution.py:171
  86.5 0.7 copy-start.2
  95.0 0.8 copy-start.4
  174.4 0.8 copy-start.6
  175.2 1.0 copy-start.3
  176.2 1.0 copy-start.5
  177.1 1.0 copy-start.7
  203.7 22.8 %all-to-all-start.2 = ((f32[16,24,128]{2,1,0:T(8,128)}), f32[16,24,128]{2,1,0:T(8,128)S(1)}, u32[]{:S(2)}, u32[]{:S(2)}) async-start(f32[16,24,128]{2,1,0:T(8,128)} %broadcast_in_dim.4), calls=%async_computation.2 | async-start | bytes 393216 | tf_op jit(solution)/shard_map/all_to_all | solution.py:166
  227.3 15.0 %all-to-all-start.3 = ((bf16[32,24,128]{2,1,0:T(8,128)(2,1)}), bf16[32,24,128]{2,1,0:T(8,128)(2,1)S(1)}, u32[]{:S(2)}, u32[]{:S(2)}) async-start(bf16[32,24,128]{2,1,0:T(8,128)(2,1)} %broadcast_in_dim.5), calls=%async_computation.3 | async-start | bytes 393216 | tf_op jit(solution)/shard_map/all_to_all | solution.py:166

commit v4 on v3

--- a/solution.py
+++ b/solution.py
@@ -25,30 +25,39 @@
     return (index[:, None] == jnp.arange(count)[None, :]).astype(jnp.float32)
 
 
-def call(body, out_shape, args, scratch=(), scalars=0):
+def call(body, out_shape, args, scratch=(), scalars=0, free_in=(), free_out=()):
     many = isinstance(out_shape, (list, tuple))
     outs = out_shape if many else [out_shape]
-    smem, vmem = (pl.BlockSpec(memory_space=m) for m in (pltpu.SMEM, pltpu.VMEM))
+    smem, vmem, free = (pl.BlockSpec(memory_space=m) for m in (pltpu.SMEM, pltpu.VMEM, pl.ANY))
+    out_specs = [free if n in free_out else vmem for n in range(len(outs))]
     return pl.pallas_call(
         body,
         out_shape=out_shape,
-        in_specs=[smem] * scalars + [vmem] * (len(args) - scalars),
-        out_specs=[vmem] * len(outs) if many else vmem,
+        in_specs=[smem] * scalars + [free if n in free_in else vmem for n in range(scalars, len(args))],
+        out_specs=out_specs if many else out_specs[0],
         scratch_shapes=list(scratch),
         compiler_params=pltpu.CompilerParams(vmem_limit_bytes=VMEM_LIMIT),
     )(*args)
 
 
-def pack_amp(amp_ref, out_ref):
+def dma(count):
+    return pltpu.SemaphoreType.DMA((count,))
+
+
+def pack_amp(amp_ref, out_ref, sems):
     across = amp_ref.shape[2] // WIDE
     parts = amp_ref.shape[1] // ROWS * across
+    copies = []
     for d in range(parts):
         i, c = divmod(d, across)
         for tile in range(TILES):
             at = c * WIDE + tile * LANES
-            part = amp_ref[:, i * ROWS : (i + 1) * ROWS, at : at + LANES]
-            out_ref[d, tile] = part
-            out_ref[parts + d, tile] = part
+            part = amp_ref.at[:, pl.ds(i * ROWS, ROWS), pl.ds(at, LANES)]
+            for twin in (d, parts + d):
+                copies.append(pltpu.make_async_copy(part, out_ref.at[twin, tile], sems.at[len(copies)]))
+                copies[-1].start()
+    for copy in copies:
+        copy.wait()
 
 
 def pack_lam(where_ref, lam_ref, *out_refs):
@@ -68,13 +77,18 @@
             out_ref[s] = in_ref[z4 ^ u]
 
 
-def unpack(parts_ref, out_ref):
+def unpack(parts_ref, out_ref, sems):
     across = out_ref.shape[2] // WIDE
+    copies = []
     for d in range(parts_ref.shape[0]):
         i, c = divmod(d, across)
         for tile in range(TILES):
             at = c * WIDE + tile * LANES
-            out_ref[:, i * ROWS : (i + 1) * ROWS, at : at + LANES] = parts_ref[d, :, tile]
+            part = out_ref.at[:, pl.ds(i * ROWS, ROWS), pl.ds(at, LANES)]
+            copies.append(pltpu.make_async_copy(parts_ref.at[d, :, tile], part, sems.at[len(copies)]))
+            copies[-1].start()
+    for copy in copies:
+        copy.wait()
 
 
 def swap_matrix():
@@ -88,9 +102,28 @@
     for q in range(both.shape[0] // SIDE):
         moved = jnp.dot(swap, both[q * SIDE : (q + 1) * SIDE], preferred_element_type=jnp.float32)
         moved = moved.astype(jnp.bfloat16)
-        at = pl.ds(pl.multiple_of(first + q * ROWS, ROWS), ROWS)
+        at = pl.ds(first + q * ROWS, ROWS)
         for s in range(ROWS):
             out_ref[at, s * WIDE : (s + 1) * WIDE] = moved[s * ROWS : (s + 1) * ROWS]
+
+
+def lam_kernel(where_ref, *refs):
+    part_refs, (out_ref, panel_ref) = refs[:STEPS], refs[STEPS:]
+    z4, y = where_ref[1], where_ref[2]
+    for n, part_ref in enumerate(part_refs):
+        for k in range(STEPS):
+            panel_ref[((z4 ^ n) * STEPS + (y ^ k))] = part_ref[k]
+    all_panels(panel_ref, out_ref)
+
+
+def all_panels(parts_ref, out_ref, before=lambda step: None):
+    swap = swap_matrix()
+    panels, _, panel_size = parts_ref.shape[:3]
+    chunk = STEPS * panel_size
+    for step in range(panels // STEPS):
+        before(step)
+        tiles = [parts_ref[STEPS * step : STEPS * (step + 1), tile].reshape(chunk * ROWS, LANES) for tile in range(TILES)]
+        to_matrix(swap, tiles, out_ref, step * chunk)
 
 
 def upper_blocks(pairs):
@@ -98,25 +131,14 @@
     return [(i, j) for i in range(n) for j in range(i, n)]
 
 
-def cross_kernel(where_ref, *refs):
-    lam_refs, (parts_ref, sym_ref, amp_ref, lam_ref, cross_ref) = refs[:STEPS], refs[STEPS:]
-    zb, z4, y = where_ref[0], where_ref[1], where_ref[2]
-    swap = swap_matrix()
-    panels, _, panel_size = parts_ref.shape[:3]
-    chunk = STEPS * panel_size
-
-    def relayout(step, carry):
-        tiles = [parts_ref[pl.ds(STEPS * step, STEPS), tile].reshape(chunk * ROWS, LANES) for tile in range(TILES)]
-        to_matrix(swap, tiles, amp_ref, step * chunk)
-        return carry
-
-    lax.fori_loop(0, panels // STEPS, relayout, 0)
-    for u, part_ref in enumerate(lam_refs):
-        tiles = [
-            jnp.concatenate([part_ref[y ^ k, tile].reshape(panel_size * ROWS, LANES) for k in range(STEPS)], axis=0)
-            for tile in range(TILES)
-        ]
-        to_matrix(swap, tiles, lam_ref, (z4 ^ u) * chunk)
+def cross_kernel(where_ref, lam_ref, parts_in, sym_ref, amp_ref, parts_ref, cross_ref, sems):
+    zb = where_ref[0]
+    copies = []
+    for step in range(parts_ref.shape[0] // STEPS):
+        some = pl.ds(step * STEPS, STEPS)
+        copies.append(pltpu.make_async_copy(parts_in.at[some], parts_ref.at[some], sems.at[step]))
+        copies[-1].start()
+    all_panels(parts_ref, amp_ref, lambda step: copies[step].wait())
     half = lam_ref.shape[0]
     cross = lax.dot_general(
         lam_ref[...], amp_ref[...], (((1,), (1,)), ((), ())), preferred_element_type=jnp.float32
@@ -159,7 +181,7 @@
             out_ref[rows, tile] = moved[:, tile * LANES : (tile + 1) * LANES].reshape(ROWS, ROWS, LANES)
         return carry
 
-    lax.fori_loop(0, half // ROWS, relayout, 0)
+    lax.fori_loop(0, half // ROWS, relayout, 0, unroll=True)
 
 
 def exchange(x, axis):
@@ -187,11 +209,18 @@
     listed = jnp.minimum(listed + listed.T, 1.0)
 
     part = (TILES, panel_size, ROWS, LANES)
-    amp_parts = call(pack_amp, jax.ShapeDtypeStruct((npanels,) + part, bf16), (t_amps,))
+    amp_parts = call(pack_amp, jax.ShapeDtypeStruct((npanels,) + part, bf16), (t_amps,), [dma(2 * npanels)], free_in=(0,), free_out=(0,))
+    four = [jax.ShapeDtypeStruct((STEPS,) + part, bf16)] * STEPS
+    lam_parts = call(pack_lam, four, (where, lambda_amps), scalars=1)
     amp_parts = exchange(amp_parts, PAIR)
-    four = [jax.ShapeDtypeStruct((STEPS,) + part, bf16)] * STEPS
-    lam_parts = shifts(call(pack_lam, four, (where, lambda_amps), scalars=1), "y")
-    lam_parts = shifts(call(regroup, four, (where, *lam_parts), scalars=1), "z4")
+    lam_parts = call(regroup, four, (where, *shifts(lam_parts, "y")), scalars=1)
+    lam = call(
+        lam_kernel,
+        jax.ShapeDtypeStruct((half, depth), bf16),
+        (where, *shifts(lam_parts, "z4")),
+        [pltpu.VMEM((npanels // 2,) + part, bf16)],
+        scalars=1,
+    )
     nblocks = len(upper_blocks(pairs))
     sym, amp = call(
         cross_kernel,
@@ -199,9 +228,10 @@
             jax.ShapeDtypeStruct((nblocks * BLOCK, BLOCK), f32),
             jax.ShapeDtypeStruct((pairs, depth), bf16),
         ],
-        (where, *lam_parts, amp_parts),
-        [pltpu.VMEM((half, depth), bf16), pltpu.VMEM((pairs, pairs), f32)],
+        (where, lam, amp_parts),
+        [pltpu.VMEM((npanels,) + part, bf16), pltpu.VMEM((pairs, pairs), f32), dma(npanels // STEPS)],
         scalars=1,
+        free_in=(2,),
     )
     plane, height = lax.axis_size(PLANE), lax.axis_size(LINE)
     own = nblocks * BLOCK // plane
@@ -217,7 +247,9 @@
         scalars=1,
     )
     result = exchange(result.reshape(npanels // 2, panel_size, TILES, ROWS, LANES), HALF)
-    return call(unpack, jax.ShapeDtypeStruct(lambda_amps.shape, bf16), (result,))
+    return call(
+        unpack, jax.ShapeDtypeStruct(lambda_amps.shape, bf16), (result,), [dma(npanels)], free_in=(0,), free_out=(0,)
+    )
 
 
 def solution(mesh):

time: 290 us -> 286 us (0.986)
  local copies, waits for them, and re-layouts: 8.91 us -> 5.3 us
    unnamed x16 -> x8, local copies, waits for them, and re-layouts: 6.66 us -> 3.05 us
    pallas_call x6 -> x7, Pallas kernels: 15.6 us -> 13.9 us  [call(): pl.pallas_call(body, out_shape=out_shape, in_specs=[smem] * scalars + [fr...]
where the time goes in v4:
time: 286 us; the launch traced here: 285 us
  waiting for transfers between devices  154 us (54%)
  blocking collectives  59.4 us (21%)
  starting transfers between devices  49.7 us (17%)
  Pallas kernels  13.9 us (5%)
  local copies, waits for them, and re-layouts  5.3 us (2%)
    ppermute x6, waiting for transfers between devices, shifts(): lax.ppermute(part, axis, [(k, k ^ s) for k in range(STEPS)])  133 us
    all_to_all x2, blocking collectives, exchange(): return lax.all_to_all(x, axis, split_axis=0, concat_axis=0, tiled=True)  59.4 us
    all_to_all x3, starting transfers between devices, exchange(): return lax.all_to_all(x, axis, split_axis=0, concat_axis=0, tiled=True)  30.3 us
    all_to_all x3, waiting for transfers between devices, exchange(): return lax.all_to_all(x, axis, split_axis=0, concat_axis=0, tiled=True)  20.7 us
    ppermute x6, starting transfers between devices, shifts(): lax.ppermute(part, axis, [(k, k ^ s) for k in range(STEPS)])  19.3 us
    pallas_call x7, Pallas kernels, call(): pl.pallas_call(body, out_shape=out_shape, in_specs=[smem] * scalars + [fr...  13.9 us
  transfers between devices with their start and end apart: 9, of which 8 were waited for; matrix products, arithmetic and copies ran while one was open for 1% of the time, Pallas kernels for 1%

profile of v4, /device:TPU:1, one launch (start us, length us, event | category | flops | bytes accessed | tf_op | source)
XLA Modules:
  0.0 285.0 jit_solution(11362452643329476487)
XLA Ops:
  0.0 0.0 copy-start.3
  0.0 1.4 copy-done.3
  1.4 2.2 shard_map.49
  3.7 0.0 copy-start.2
  3.7 16.4 %all-to-all-start = ((bf16[32,2,12,16,128]{4,3,2,1,0:T(8,128)(2,1)}), bf16[32,2,12,16,128]{4,3,2,1,0:T(8,128)(2,1)}, u32[]{:S(2)}, u32[]{:S(2)}) async-start(bf16[32,2,12,16,128]{4,3,2,1,0:T(8,128)(2,1)} %shard_map.49), calls=%async_computation | async-start | bytes 6291456 | tf_op jit(solution)/shard_map/all_to_all | solution.py:188
  20.0 0.1 pad_add_fusion.where_ref
  20.1 0.0 copy-done.2
  20.1 1.0 shard_map.46
  21.1 3.1 %collective-permute-start = (bf16[4,2,12,16,128]{4,3,2,1,0:T(8,128)(2,1)S(1)}, bf16[4,2,12,16,128]{4,3,2,1,0:T(8,128)(2,1)S(1)}, u32[]{:S(2)}, u32[]{:S(2)}) collective-permute-start(bf16[4,2,12,16,128]{4,3,2,1,0:T(8,128)(2,1)S(1)} %get-tuple-element.16), channel_id=1, source_target_pairs={{0,16},{16,0},{32,48},{48,32},{1,17},{17,1},{33,49},{49,33},{2,18}... | collective-permute-start | bytes 1179656 | tf_op jit(solution)/shard_map/ppermute | solution.py:193
  24.2 4.3 %collective-permute-start.1 = (bf16[4,2,12,16,128]{4,3,2,1,0:T(8,128)(2,1)S(1)}, bf16[4,2,12,16,128]{4,3,2,1,0:T(8,128)(2,1)S(1)}, u32[]{:S(2)}, u32[]{:S(2)}) collective-permute-start(bf16[4,2,12,16,128]{4,3,2,1,0:T(8,128)(2,1)S(1)} %get-tuple-element.17), channel_id=1, source_target_pairs={{0,32},{16,48},{32,0},{48,16},{1,33},{17,49},{33,1},{49,17},{2,34}... | collective-permute-start | bytes 1179656 | tf_op jit(solution)/shard_map/ppermute | solution.py:193
  28.5 2.2 collective-permute-start.2
  30.7 12.4 %collective-permute-done.refs_1_ = bf16[4,2,12,16,128]{4,3,2,1,0:T(8,128)(2,1)S(1)} collective-permute-done((bf16[4,2,12,16,128]{4,3,2,1,0:T(8,128)(2,1)S(1)}, bf16[4,2,12,16,128]{4,3,2,1,0:T(8,128)(2,1)S(1)}, u32[]{:S(2)}, u32[]{:S(2)}) %collective-permute-start) | collective-permute-done | bytes 393248 | tf_op jit(solution)/shard_map/ppermute | solution.py:193
  43.1 9.1 %collective-permute-done.1.refs_2_ = bf16[4,2,12,16,128]{4,3,2,1,0:T(8,128)(2,1)S(1)} collective-permute-done((bf16[4,2,12,16,128]{4,3,2,1,0:T(8,128)(2,1)S(1)}, bf16[4,2,12,16,128]{4,3,2,1,0:T(8,128)(2,1)S(1)}, u32[]{:S(2)}, u32[]{:S(2)}) %collective-permute-start.1) | collective-permute-done | bytes 393248 | tf_op jit(solution)/shard_map/ppermute | solution.py:193
  52.2 6.6 %collective-permute-done.2.refs_3_ = bf16[4,2,12,16,128]{4,3,2,1,0:T(8,128)(2,1)S(1)} collective-permute-done((bf16[4,2,12,16,128]{4,3,2,1,0:T(8,128)(2,1)S(1)}, bf16[4,2,12,16,128]{4,3,2,1,0:T(8,128)(2,1)S(1)}, u32[]{:S(2)}, u32[]{:S(2)}) %collective-permute-start.2) | collective-permute-done | bytes 393248 | tf_op jit(solution)/shard_map/ppermute | solution.py:193
  58.9 0.6 shard_map.47
  59.5 3.8 %collective-permute-start.3 = (bf16[4,2,12,16,128]{4,3,2,1,0:T(8,128)(2,1)S(1)}, bf16[4,2,12,16,128]{4,3,2,1,0:T(8,128)(2,1)S(1)}, u32[]{:S(2)}, u32[]{:S(2)}) collective-permute-start(bf16[4,2,12,16,128]{4,3,2,1,0:T(8,128)(2,1)S(1)} %get-tuple-element.20), channel_id=1, source_target_pairs={{0,64},{64,0},{128,192},{192,128},{1,65},{65,1},{129,193},{193,129... | collective-permute-start | bytes 1179656 | tf_op jit(solution)/shard_map/ppermute | solution.py:193
  63.4 1.9 collective-permute-start.4
  65.3 4.0 %collective-permute-start.5 = (bf16[4,2,12,16,128]{4,3,2,1,0:T(8,128)(2,1)S(1)}, bf16[4,2,12,16,128]{4,3,2,1,0:T(8,128)(2,1)S(1)}, u32[]{:S(2)}, u32[]{:S(2)}) collective-permute-start(bf16[4,2,12,16,128]{4,3,2,1,0:T(8,128)(2,1)S(1)} %get-tuple-element.22), channel_id=1, source_target_pairs={{0,192},{64,128},{128,64},{192,0},{1,193},{65,129},{129,65},{193,1... | collective-permute-start | bytes 1179656 | tf_op jit(solution)/shard_map/ppermute | solution.py:193
  69.3 17.4 %collective-permute-done.3.refs_1_ = bf16[4,2,12,16,128]{4,3,2,1,0:T(8,128)(2,1)S(1)} collective-permute-done((bf16[4,2,12,16,128]{4,3,2,1,0:T(8,128)(2,1)S(1)}, bf16[4,2,12,16,128]{4,3,2,1,0:T(8,128)(2,1)S(1)}, u32[]{:S(2)}, u32[]{:S(2)}) %collective-permute-start.3) | collective-permute-done | bytes 393248 | tf_op jit(solution)/shard_map/ppermute | solution.py:193
  86.7 8.5 %collective-permute-done.4.refs_2_ = bf16[4,2,12,16,128]{4,3,2,1,0:T(8,128)(2,1)S(1)} collective-permute-done((bf16[4,2,12,16,128]{4,3,2,1,0:T(8,128)(2,1)S(1)}, bf16[4,2,12,16,128]{4,3,2,1,0:T(8,128)(2,1)S(1)}, u32[]{:S(2)}, u32[]{:S(2)}) %collective-permute-start.4) | collective-permute-done | bytes 393248 | tf_op jit(solution)/shard_map/ppermute | solution.py:193
  95.2 79.4 %collective-permute-done.5.refs_3_ = bf16[4,2,12,16,128]{4,3,2,1,0:T(8,128)(2,1)S(1)} collective-permute-done((bf16[4,2,12,16,128]{4,3,2,1,0:T(8,128)(2,1)S(1)}, bf16[4,2,12,16,128]{4,3,2,1,0:T(8,128)(2,1)S(1)}, u32[]{:S(2)}, u32[]{:S(2)}) %collective-permute-start.5) | collective-permute-done | bytes 393248 | tf_op jit(solution)/shard_map/ppermute | solution.py:193
  174.6 1.2 shard_map.48.lam_ref
  175.8 0.0 all-to-all-done.parts_in
  175.8 5.1 %shard_map.50 = (f32[768,128]{1,0:T(8,128)S(1)}, bf16[384,4096]{1,0:T(8,128)(2,1)S(1)}) custom-call(s32[3]{0:T(128)S(1)} %pad_add_fusion.where_ref, bf16[192,4096]{1,0:T(8,128)(2,1)S(1)} %shard_map.48.lam_ref, bf16[32,2,12,16,128]{4,3,2,1,0:T(8,128)(2,1)} %all-to-all-done.parts_in), custom_call_target="tpu_custom_call" | custom-call | tf_op jit(solution)/shard_map/pallas_call | solution.py:33
  181.0 0.0 copy-start
  181.0 1.6 copy-done
  182.6 0.0 copy-start.1
  182.6 18.9 %all_to_all.25 = f32[32,24,128]{2,1,0:T(8,128)S(1)} all-to-all(f32[32,24,128]{2,1,0:T(8,128)S(1)} %bitcast.14), channel_id=1, replica_groups=mesh['zb'=2,'z4'=4,'y'=4,'zh'=2,'x'=4,'c'=2] {'y','x','c'}, dimensions={0} | all-to-all | bytes 786432 | tf_op jit(solution)/shard_map/all_to_all | solution.py:188
  201.5 0.7 broadcast_in_dim.4
  202.2 7.4 %all-to-all-start.2 = ((f32[16,24,128]{2,1,0:T(8,128)}), f32[16,24,128]{2,1,0:T(8,128)S(1)}, u32[]{:S(2)}, u32[]{:S(2)}) async-start(f32[16,24,128]{2,1,0:T(8,128)} %broadcast_in_dim.4), calls=%async_computation.2 | async-start | bytes 393216 | tf_op jit(solution)/shard_map/all_to_all | solution.py:188
  209.7 0.8 slice_reduce_fusion
  210.4 0.9 fusion
  211.3 0.9 fusion.1
  212.2 0.4 fusion.7
  212.6 0.1 copy.6
  212.7 12.4 %all-to-all-done.2 = f32[16,24,128]{2,1,0:T(8,128)S(1)} async-done(((f32[16,24,128]{2,1,0:T(8,128)}), f32[16,24,128]{2,1,0:T(8,128)S(1)}, u32[]{:S(2)}, u32[]{:S(2)}) %all-to-all-start.2) | async-done | bytes 196640 | tf_op jit(solution)/shard_map/all_to_all | solution.py:188
  225.1 0.7 broadcast_in_dim.5
  225.8 6.6 %all-to-all-start.3 = ((bf16[32,24,128]{2,1,0:T(8,128)(2,1)}), bf16[32,24,128]{2,1,0:T(8,128)(2,1)S(1)}, u32[]{:S(2)}, u32[]{:S(2)}) async-start(bf16[32,24,128]{2,1,0:T(8,128)(2,1)} %broadcast_in_dim.5), calls=%async_computation.3 | async-start | bytes 393216 | tf_op jit(solution)/shard_map/all_to_all | solution.py:188
  232.4 8.4 %all-to-all-done.3 = bf16[32,24,128]{2,1,0:T(8,128)(2,1)S(1)} async-done(((bf16[32,24,128]{2,1,0:T(8,128)(2,1)}), bf16[32,24,128]{2,1,0:T(8,128)(2,1)S(1)}, u32[]{:S(2)}, u32[]{:S(2)}) %all-to-all-start.3) | async-done | bytes 196640 | tf_op jit(solution)/shard_map/all_to_all | solution.py:188
  240.7 0.0 copy-done.1
  240.7 2.3 shard_map.51
  243.1 40.5 %all_to_all.26.parts_ref = bf16[16,12,2,16,128]{4,3,2,1,0:T(8,128)(2,1)S(1)} all-to-all(bf16[16,12,2,16,128]{4,3,2,1,0:T(8,128)(2,1)S(1)} %bitcast.12), channel_id=1, replica_groups=mesh['zb'=2,'z4'=4,'y'=4,'zh'=2,'x'=4,'c'=2] {'z4','y'}, dimensions={0} | all-to-all | bytes 3145728 | tf_op jit(solution)/shard_map/all_to_all | solution.py:188
  283.6 1.4 shard_map.52
  (3 shorter events, 0.1 us)
Async XLA Ops:
  0.0 1.4 copy-start.3
  3.7 16.5 %copy-start.2 = (bf16[12,64,1024]{2,1,0:T(8,128)(2,1)S(1)}, bf16[12,64,1024]{2,1,0:T(8,128)(2,1)}, u32[]{:S(2)}) copy-start(bf16[12,64,1024]{2,1,0:T(8,128)(2,1)} %lam_ref.1) | copy-start | bytes 4718596
  3.7 172.1 %all-to-all-start = ((bf16[32,2,12,16,128]{4,3,2,1,0:T(8,128)(2,1)}), bf16[32,2,12,16,128]{4,3,2,1,0:T(8,128)(2,1)}, u32[]{:S(2)}, u32[]{:S(2)}) async-start(bf16[32,2,12,16,128]{4,3,2,1,0:T(8,128)(2,1)} %shard_map.49), calls=%async_computation | async-start | bytes 6291456 | tf_op jit(solution)/shard_map/all_to_all | solution.py:188
  21.1 22.0 %collective-permute-start = (bf16[4,2,12,16,128]{4,3,2,1,0:T(8,128)(2,1)S(1)}, bf16[4,2,12,16,128]{4,3,2,1,0:T(8,128)(2,1)S(1)}, u32[]{:S(2)}, u32[]{:S(2)}) collective-permute-start(bf16[4,2,12,16,128]{4,3,2,1,0:T(8,128)(2,1)S(1)} %get-tuple-element.16), channel_id=1, source_target_pairs={{0,16},{16,0},{32,48},{48,32},{1,17},{17,1},{33,49},{49,33},{2,18}... | collective-permute-start | bytes 1179656 | tf_op jit(solution)/shard_map/ppermute | solution.py:193
  24.2 28.1 %collective-permute-start.1 = (bf16[4,2,12,16,128]{4,3,2,1,0:T(8,128)(2,1)S(1)}, bf16[4,2,12,16,128]{4,3,2,1,0:T(8,128)(2,1)S(1)}, u32[]{:S(2)}, u32[]{:S(2)}) collective-permute-start(bf16[4,2,12,16,128]{4,3,2,1,0:T(8,128)(2,1)S(1)} %get-tuple-element.17), channel_id=1, source_target_pairs={{0,32},{16,48},{32,0},{48,16},{1,33},{17,49},{33,1},{49,17},{2,34}... | collective-permute-start | bytes 1179656 | tf_op jit(solution)/shard_map/ppermute | solution.py:193
  28.5 30.4 %collective-permute-start.2 = (bf16[4,2,12,16,128]{4,3,2,1,0:T(8,128)(2,1)S(1)}, bf16[4,2,12,16,128]{4,3,2,1,0:T(8,128)(2,1)S(1)}, u32[]{:S(2)}, u32[]{:S(2)}) collective-permute-start(bf16[4,2,12,16,128]{4,3,2,1,0:T(8,128)(2,1)S(1)} %get-tuple-element.18), channel_id=1, source_target_pairs={{0,48},{16,32},{32,16},{48,0},{1,49},{17,33},{33,17},{49,1},{2,50}... | collective-permute-start | bytes 1179656 | tf_op jit(solution)/shard_map/ppermute | solution.py:193
  59.5 27.2 %collective-permute-start.3 = (bf16[4,2,12,16,128]{4,3,2,1,0:T(8,128)(2,1)S(1)}, bf16[4,2,12,16,128]{4,3,2,1,0:T(8,128)(2,1)S(1)}, u32[]{:S(2)}, u32[]{:S(2)}) collective-permute-start(bf16[4,2,12,16,128]{4,3,2,1,0:T(8,128)(2,1)S(1)} %get-tuple-element.20), channel_id=1, source_target_pairs={{0,64},{64,0},{128,192},{192,128},{1,65},{65,1},{129,193},{193,129... | collective-permute-start | bytes 1179656 | tf_op jit(solution)/shard_map/ppermute | solution.py:193
  63.4 31.8 %collective-permute-start.4 = (bf16[4,2,12,16,128]{4,3,2,1,0:T(8,128)(2,1)S(1)}, bf16[4,2,12,16,128]{4,3,2,1,0:T(8,128)(2,1)S(1)}, u32[]{:S(2)}, u32[]{:S(2)}) collective-permute-start(bf16[4,2,12,16,128]{4,3,2,1,0:T(8,128)(2,1)S(1)} %get-tuple-element.21), channel_id=1, source_target_pairs={{0,128},{64,192},{128,0},{192,64},{1,129},{65,193},{129,1},{193,65... | collective-permute-start | bytes 1179656 | tf_op jit(solution)/shard_map/ppermute | solution.py:193
  65.3 109.3 %collective-permute-start.5 = (bf16[4,2,12,16,128]{4,3,2,1,0:T(8,128)(2,1)S(1)}, bf16[4,2,12,16,128]{4,3,2,1,0:T(8,128)(2,1)S(1)}, u32[]{:S(2)}, u32[]{:S(2)}) collective-permute-start(bf16[4,2,12,16,128]{4,3,2,1,0:T(8,128)(2,1)S(1)} %get-tuple-element.22), channel_id=1, source_target_pairs={{0,192},{64,128},{128,64},{192,0},{1,193},{65,129},{129,65},{193,1... | collective-permute-start | bytes 1179656 | tf_op jit(solution)/shard_map/ppermute | solution.py:193
  181.0 1.6 copy-start
  182.6 58.1 %copy-start.1 = (bf16[384,4096]{1,0:T(8,128)(2,1)S(1)}, bf16[384,4096]{1,0:T(8,128)(2,1)}, u32[]{:S(2)}) copy-start(bf16[384,4096]{1,0:T(8,128)(2,1)} %copy-done) | copy-start | bytes 9437188
  202.2 22.8 %all-to-all-start.2 = ((f32[16,24,128]{2,1,0:T(8,128)}), f32[16,24,128]{2,1,0:T(8,128)S(1)}, u32[]{:S(2)}, u32[]{:S(2)}) async-start(f32[16,24,128]{2,1,0:T(8,128)} %broadcast_in_dim.4), calls=%async_computation.2 | async-start | bytes 393216 | tf_op jit(solution)/shard_map/all_to_all | solution.py:188
  225.8 15.0 %all-to-all-start.3 = ((bf16[32,24,128]{2,1,0:T(8,128)(2,1)}), bf16[32,24,128]{2,1,0:T(8,128)(2,1)S(1)}, u32[]{:S(2)}, u32[]{:S(2)}) async-start(bf16[32,24,128]{2,1,0:T(8,128)(2,1)} %broadcast_in_dim.5), calls=%async_computation.3 | async-start | bytes 393216 | tf_op jit(solution)/shard_map/all_to_all | solution.py:188

commit v5 on v4

--- a/solution.py
+++ b/solution.py
@@ -17,7 +17,7 @@
 WIDE = TILES * LANES
 SIDE = ROWS * ROWS
 STEPS = 4
-BLOCK = 128
+SQUARE = 256
 VMEM_LIMIT = 48 * 1024 * 1024
 
 
@@ -126,9 +126,17 @@
         to_matrix(swap, tiles, out_ref, step * chunk)
 
 
-def upper_blocks(pairs):
-    n = pairs // BLOCK
-    return [(i, j) for i in range(n) for j in range(i, n)]
+def left_half(shape):
+    return lax.broadcasted_iota(jnp.int32, shape, 1) < LANES // 2
+
+
+def fold(x):
+    n = x.shape[0] // 2
+    return jnp.where(left_half((n, LANES)), x[:n], pltpu.roll(x[n:], LANES // 2, 1))
+
+
+def unfold(x):
+    return jnp.concatenate([x, pltpu.roll(x, LANES // 2, 1)], axis=0)
 
 
 def cross_kernel(where_ref, lam_ref, parts_in, sym_ref, amp_ref, parts_ref, cross_ref, sems):
@@ -140,33 +148,65 @@
         copies[-1].start()
     all_panels(parts_ref, amp_ref, lambda step: copies[step].wait())
     half = lam_ref.shape[0]
-    cross = lax.dot_general(
-        lam_ref[...], amp_ref[...], (((1,), (1,)), ((), ())), preferred_element_type=jnp.float32
-    )
-    cross_ref[pl.ds(pl.multiple_of(zb * half, half), half)] = cross
-    cross_ref[pl.ds(pl.multiple_of((1 - zb) * half, half), half)] = jnp.zeros_like(cross)
-    sym = 0.5 * (cross_ref[...] + cross_ref[...].T)
-    for n, (i, j) in enumerate(upper_blocks(2 * half)):
-        sym_ref[n * BLOCK : (n + 1) * BLOCK] = sym[i * BLOCK : (i + 1) * BLOCK, j * BLOCK : (j + 1) * BLOCK]
-
-
-def density_kernel(where_ref, upper_ref, listed_ref, amp_ref, out_ref, inter_ref, flat_ref):
+    cross_ref[...] = jnp.zeros_like(cross_ref)
+    for n, which in enumerate((zb, 1 - zb)):
+        amp = amp_ref[pl.ds(pl.multiple_of(which * half, half), half)]
+        cross_ref[n, :half, :half] = lax.dot_general(
+            lam_ref[...], amp, (((1,), (1,)), ((), ())), preferred_element_type=jnp.float32
+        )
+    within, between = cross_ref[0], cross_ref[1]
+    within = 0.5 * (within + within.T)
+    between = 0.5 * jnp.where(zb == 0, between, between.T)
+    at = 0
+    for rows in (
+        between[:half, :LANES],
+        fold(between[:half, LANES:]),
+        within[:LANES, :LANES],
+        fold(within[:LANES, LANES:]),
+        fold(within[LANES:half, LANES:]),
+    ):
+        sym_ref[at : at + rows.shape[0]] = rows
+        at += rows.shape[0]
+
+
+def density_kernel(where_ref, sym_ref, listed_ref, amp_ref, out_ref, square_ref, inter_ref, flat_ref):
     pairs, depth = amp_ref.shape
     half = flat_ref.shape[0]
     panels = listed_ref.shape[0]
     panel_size = pairs // panels
-    row = lax.broadcasted_iota(jnp.int32, (pairs, panels), 0)
-    first = lax.broadcasted_iota(jnp.int32, (pairs, panels), 1) * panel_size
-    spread = ((row >= first) & (row < first + panel_size)).astype(jnp.float32)
-    mask = jnp.dot(spread, listed_ref[...], preferred_element_type=jnp.float32)
-    mask = lax.dot_general(mask, spread, (((1,), (1,)), ((), ())), preferred_element_type=jnp.float32)
-    for n, (i, j) in enumerate(upper_blocks(pairs)):
-        block = upper_ref[n * BLOCK : (n + 1) * BLOCK].astype(jnp.float32)
-        rows, cols = slice(i * BLOCK, (i + 1) * BLOCK), slice(j * BLOCK, (j + 1) * BLOCK)
-        inter_ref[rows, cols] = (block * mask[rows, cols]).astype(jnp.bfloat16)
-        if i != j:
-            inter_ref[cols, rows] = (block.T * mask[cols, rows]).astype(jnp.bfloat16)
-    own = inter_ref[pl.ds(pl.multiple_of(where_ref[0] * half, half), half)]
+    zb = where_ref[0]
+
+    def spread(first_row, rows):
+        row = first_row + lax.broadcasted_iota(jnp.int32, (rows, panels), 0)
+        first = lax.broadcasted_iota(jnp.int32, (rows, panels), 1) * panel_size
+        return ((row >= first) & (row < first + panel_size)).astype(jnp.float32)
+
+    mask = jnp.dot(spread(zb * half, half), listed_ref[...], preferred_element_type=jnp.float32)
+    mask = lax.dot_general(mask, spread(0, pairs), (((1,), (1,)), ((), ())), preferred_element_type=jnp.float32)
+
+    sizes = [half, half // 2, LANES, LANES // 2, (half - LANES) // 2]
+    ends = [sum(sizes[: n + 1]) for n in range(len(sizes))]
+    x, x_right, w, w_right, w_last = (sym_ref[e - n : e].astype(jnp.float32) for e, n in zip(ends, sizes))
+    square_ref[...] = jnp.zeros_like(square_ref)
+    square_ref[:half, :LANES] = x
+    square_ref[:half, LANES:] = unfold(x_right)
+    between = jnp.where(zb == 0, square_ref[...], square_ref[...].T)[:half]
+    w_right = unfold(w_right)
+    square_ref[:LANES, :LANES] = w
+    square_ref[:LANES, LANES:] = w_right
+    square_ref[LANES:half, :LANES] = w_right.T[: half - LANES]
+    square_ref[LANES:half, LANES:] = unfold(w_last)
+    within = square_ref[:half]
+    left = jnp.where(zb == 0, within, between)
+    right = jnp.where(zb == 0, between, within)
+    keep = left_half((half, LANES))
+    turned = [pltpu.roll(right[:, n * LANES : (n + 1) * LANES], LANES // 2, 1) for n in range(2)]
+    for n, block in enumerate(
+        (left[:, :LANES], jnp.where(keep, left[:, LANES:], turned[0]), jnp.where(keep, turned[0], turned[1]))
+    ):
+        cols = slice(n * LANES, (n + 1) * LANES)
+        inter_ref[:, cols] = (block * mask[:, cols]).astype(jnp.bfloat16)
+    own = inter_ref[...]
     for c in range(depth // WIDE):
         flat_ref[:, c * WIDE : (c + 1) * WIDE] = jnp.dot(
             own, amp_ref[:, c * WIDE : (c + 1) * WIDE], preferred_element_type=jnp.float32
@@ -199,6 +239,7 @@
     panel_size, rows, cols = lambda_amps.shape
     pairs, half = npanels * panel_size, npanels * panel_size // 2
     depth = ROWS * WIDE
+    folded = half + half // 2 + LANES + LANES // 2 + (half - LANES) // 2
     bf16, f32 = jnp.bfloat16, jnp.float32
     where = jnp.stack([lax.axis_index("zb"), lax.axis_index("z4"), lax.axis_index("y")]).astype(jnp.int32)
 
@@ -221,29 +262,31 @@
         [pltpu.VMEM((npanels // 2,) + part, bf16)],
         scalars=1,
     )
-    nblocks = len(upper_blocks(pairs))
     sym, amp = call(
         cross_kernel,
         [
-            jax.ShapeDtypeStruct((nblocks * BLOCK, BLOCK), f32),
+            jax.ShapeDtypeStruct((folded, LANES), f32),
             jax.ShapeDtypeStruct((pairs, depth), bf16),
         ],
         (where, lam, amp_parts),
-        [pltpu.VMEM((npanels,) + part, bf16), pltpu.VMEM((pairs, pairs), f32), dma(npanels // STEPS)],
+        [pltpu.VMEM((npanels,) + part, bf16), pltpu.VMEM((2, SQUARE, SQUARE), f32), dma(npanels // STEPS)],
         scalars=1,
         free_in=(2,),
     )
     plane, height = lax.axis_size(PLANE), lax.axis_size(LINE)
-    own = nblocks * BLOCK // plane
-    terms = exchange(sym.reshape(plane, own, BLOCK), PLANE)
-    terms = jnp.broadcast_to(jnp.sum(terms, axis=0), (height, own, BLOCK))
-    total = jnp.sum(exchange(terms, LINE), axis=0).astype(bf16)
-    upper = exchange(jnp.broadcast_to(total, (plane, own, BLOCK)), PLANE)
+    own = folded // plane
+    terms = exchange(sym.reshape(plane, own, LANES), PLANE)
+    terms = exchange(jnp.broadcast_to(jnp.sum(terms, axis=0), (height, own, LANES)), LINE)
+    halves = terms.reshape(2, height // 2, own, LANES).sum(axis=1)
+    mine = jnp.where(where[0] == 0, halves[0], halves[1])
+    both = lax.axis_index(PLANE) * own < half * half // LANES
+    total = jnp.where(both, halves[0] + halves[1], mine).astype(bf16)
+    upper = exchange(jnp.broadcast_to(total, (plane, own, LANES)), PLANE)
     result = call(
         density_kernel,
         jax.ShapeDtypeStruct((half, TILES, ROWS, LANES), bf16),
-        (where, upper.reshape(nblocks * BLOCK, BLOCK), listed, amp),
-        [pltpu.VMEM((pairs, pairs), bf16), pltpu.VMEM((half, depth), bf16)],
+        (where, upper.reshape(folded, LANES), listed, amp),
+        [pltpu.VMEM((SQUARE, SQUARE), f32), pltpu.VMEM((half, pairs), bf16), pltpu.VMEM((half, depth), bf16)],
         scalars=1,
     )
     result = exchange(result.reshape(npanels // 2, panel_size, TILES, ROWS, LANES), HALF)

time: 286 us -> 284 us (level)
  blocking collectives: 59.4 us -> 39.7 us
  waiting for transfers between devices: 154 us -> 163 us
  starting transfers between devices: 49.7 us -> 58.1 us
    all_to_all x2 -> x1, blocking collectives: 59.4 us -> 39.7 us  [exchange(): return lax.all_to_all(x, axis, split_axis=0, concat_axis=0, tiled=True)]
    all_to_all x3 -> x4, starting transfers between devices: 30.3 us -> 38.7 us  [exchange(): return lax.all_to_all(x, axis, split_axis=0, concat_axis=0, tiled=True)]
    all_to_all x3 -> x4, waiting for transfers between devices: 20.7 us -> 29.1 us  [exchange(): return lax.all_to_all(x, axis, split_axis=0, concat_axis=0, tiled=True)]
  transfers between devices with their start and end apart: 9 -> 10, of which waited for: 8 -> 9; matrix products, arithmetic and copies ran while one was open for 1% -> 0% of each run, Pallas kernels for 1% -> 1%
where the time goes in v5:
time: 284 us; the launch traced here: 283 us
  waiting for transfers between devices  163 us (57%)
  starting transfers between devices  58.1 us (20%)
  blocking collectives  39.7 us (14%)
  Pallas kernels  14.6 us (5%)
  local copies, waits for them, and re-layouts  6.36 us (2%)
    ppermute x6, waiting for transfers between devices, shifts(): lax.ppermute(part, axis, [(k, k ^ s) for k in range(STEPS)])  133 us
    all_to_all x1, blocking collectives, exchange(): return lax.all_to_all(x, axis, split_axis=0, concat_axis=0, tiled=True)  39.7 us
    all_to_all x4, starting transfers between devices, exchange(): return lax.all_to_all(x, axis, split_axis=0, concat_axis=0, tiled=True)  38.7 us
    all_to_all x4, waiting for transfers between devices, exchange(): return lax.all_to_all(x, axis, split_axis=0, concat_axis=0, tiled=True)  29.1 us
    ppermute x6, starting transfers between devices, shifts(): lax.ppermute(part, axis, [(k, k ^ s) for k in range(STEPS)])  19.3 us
    pallas_call x7, Pallas kernels, call(): pl.pallas_call(body, out_shape=out_shape, in_specs=[smem] * scalars + [fr...  14.6 us
  transfers between devices with their start and end apart: 10, of which 9 were waited for; matrix products, arithmetic and copies ran while one was open for 0% of the time, Pallas kernels for 1%

profile of v5, /device:TPU:1, one launch (start us, length us, event | category | flops | bytes accessed | tf_op | source)
XLA Modules:
  0.0 282.5 jit_solution(8663883348622157281)
XLA Ops:
  0.0 0.0 copy-start.3
  0.0 1.4 copy-done.3
  1.4 2.3 shard_map.49
  3.7 0.0 copy-start.2
  3.7 16.4 %all-to-all-start = ((bf16[32,2,12,16,128]{4,3,2,1,0:T(8,128)(2,1)}), bf16[32,2,12,16,128]{4,3,2,1,0:T(8,128)(2,1)}, u32[]{:S(2)}, u32[]{:S(2)}) async-start(bf16[32,2,12,16,128]{4,3,2,1,0:T(8,128)(2,1)} %shard_map.49), calls=%async_computation | async-start | bytes 6291456 | tf_op jit(solution)/shard_map/all_to_all | solution.py:228
  20.1 0.1 pad_add_fusion.where_ref
  20.1 0.0 copy-done.2
  20.1 1.0 shard_map.46
  21.1 3.1 %collective-permute-start = (bf16[4,2,12,16,128]{4,3,2,1,0:T(8,128)(2,1)S(1)}, bf16[4,2,12,16,128]{4,3,2,1,0:T(8,128)(2,1)S(1)}, u32[]{:S(2)}, u32[]{:S(2)}) collective-permute-start(bf16[4,2,12,16,128]{4,3,2,1,0:T(8,128)(2,1)S(1)} %get-tuple-element.16), channel_id=1, source_target_pairs={{0,16},{16,0},{32,48},{48,32},{1,17},{17,1},{33,49},{49,33},{2,18}... | collective-permute-start | bytes 1179656 | tf_op jit(solution)/shard_map/ppermute | solution.py:233
  24.2 4.3 %collective-permute-start.1 = (bf16[4,2,12,16,128]{4,3,2,1,0:T(8,128)(2,1)S(1)}, bf16[4,2,12,16,128]{4,3,2,1,0:T(8,128)(2,1)S(1)}, u32[]{:S(2)}, u32[]{:S(2)}) collective-permute-start(bf16[4,2,12,16,128]{4,3,2,1,0:T(8,128)(2,1)S(1)} %get-tuple-element.17), channel_id=1, source_target_pairs={{0,32},{16,48},{32,0},{48,16},{1,33},{17,49},{33,1},{49,17},{2,34}... | collective-permute-start | bytes 1179656 | tf_op jit(solution)/shard_map/ppermute | solution.py:233
  28.5 2.2 collective-permute-start.2
  30.7 12.4 %collective-permute-done.refs_1_ = bf16[4,2,12,16,128]{4,3,2,1,0:T(8,128)(2,1)S(1)} collective-permute-done((bf16[4,2,12,16,128]{4,3,2,1,0:T(8,128)(2,1)S(1)}, bf16[4,2,12,16,128]{4,3,2,1,0:T(8,128)(2,1)S(1)}, u32[]{:S(2)}, u32[]{:S(2)}) %collective-permute-start) | collective-permute-done | bytes 393248 | tf_op jit(solution)/shard_map/ppermute | solution.py:233
  43.1 9.1 %collective-permute-done.1.refs_2_ = bf16[4,2,12,16,128]{4,3,2,1,0:T(8,128)(2,1)S(1)} collective-permute-done((bf16[4,2,12,16,128]{4,3,2,1,0:T(8,128)(2,1)S(1)}, bf16[4,2,12,16,128]{4,3,2,1,0:T(8,128)(2,1)S(1)}, u32[]{:S(2)}, u32[]{:S(2)}) %collective-permute-start.1) | collective-permute-done | bytes 393248 | tf_op jit(solution)/shard_map/ppermute | solution.py:233
  52.3 6.6 %collective-permute-done.2.refs_3_ = bf16[4,2,12,16,128]{4,3,2,1,0:T(8,128)(2,1)S(1)} collective-permute-done((bf16[4,2,12,16,128]{4,3,2,1,0:T(8,128)(2,1)S(1)}, bf16[4,2,12,16,128]{4,3,2,1,0:T(8,128)(2,1)S(1)}, u32[]{:S(2)}, u32[]{:S(2)}) %collective-permute-start.2) | collective-permute-done | bytes 393248 | tf_op jit(solution)/shard_map/ppermute | solution.py:233
  58.9 0.6 shard_map.47
  59.6 3.8 %collective-permute-start.3 = (bf16[4,2,12,16,128]{4,3,2,1,0:T(8,128)(2,1)S(1)}, bf16[4,2,12,16,128]{4,3,2,1,0:T(8,128)(2,1)S(1)}, u32[]{:S(2)}, u32[]{:S(2)}) collective-permute-start(bf16[4,2,12,16,128]{4,3,2,1,0:T(8,128)(2,1)S(1)} %get-tuple-element.20), channel_id=1, source_target_pairs={{0,64},{64,0},{128,192},{192,128},{1,65},{65,1},{129,193},{193,129... | collective-permute-start | bytes 1179656 | tf_op jit(solution)/shard_map/ppermute | solution.py:233
  63.4 1.9 collective-permute-start.4
  65.3 4.0 %collective-permute-start.5 = (bf16[4,2,12,16,128]{4,3,2,1,0:T(8,128)(2,1)S(1)}, bf16[4,2,12,16,128]{4,3,2,1,0:T(8,128)(2,1)S(1)}, u32[]{:S(2)}, u32[]{:S(2)}) collective-permute-start(bf16[4,2,12,16,128]{4,3,2,1,0:T(8,128)(2,1)S(1)} %get-tuple-element.22), channel_id=1, source_target_pairs={{0,192},{64,128},{128,64},{192,0},{1,193},{65,129},{129,65},{193,1... | collective-permute-start | bytes 1179656 | tf_op jit(solution)/shard_map/ppermute | solution.py:233
  69.3 17.4 %collective-permute-done.3.refs_1_ = bf16[4,2,12,16,128]{4,3,2,1,0:T(8,128)(2,1)S(1)} collective-permute-done((bf16[4,2,12,16,128]{4,3,2,1,0:T(8,128)(2,1)S(1)}, bf16[4,2,12,16,128]{4,3,2,1,0:T(8,128)(2,1)S(1)}, u32[]{:S(2)}, u32[]{:S(2)}) %collective-permute-start.3) | collective-permute-done | bytes 393248 | tf_op jit(solution)/shard_map/ppermute | solution.py:233
  86.7 8.5 %collective-permute-done.4.refs_2_ = bf16[4,2,12,16,128]{4,3,2,1,0:T(8,128)(2,1)S(1)} collective-permute-done((bf16[4,2,12,16,128]{4,3,2,1,0:T(8,128)(2,1)S(1)}, bf16[4,2,12,16,128]{4,3,2,1,0:T(8,128)(2,1)S(1)}, u32[]{:S(2)}, u32[]{:S(2)}) %collective-permute-start.4) | collective-permute-done | bytes 393248 | tf_op jit(solution)/shard_map/ppermute | solution.py:233
  95.2 79.4 %collective-permute-done.5.refs_3_ = bf16[4,2,12,16,128]{4,3,2,1,0:T(8,128)(2,1)S(1)} collective-permute-done((bf16[4,2,12,16,128]{4,3,2,1,0:T(8,128)(2,1)S(1)}, bf16[4,2,12,16,128]{4,3,2,1,0:T(8,128)(2,1)S(1)}, u32[]{:S(2)}, u32[]{:S(2)}) %collective-permute-start.5) | collective-permute-done | bytes 393248 | tf_op jit(solution)/shard_map/ppermute | solution.py:233
  174.6 1.2 shard_map.48.lam_ref
  175.8 0.0 copy-start.4
  175.8 0.0 copy-start.5
  175.9 0.0 all-to-all-done.parts_in
  175.9 5.9 %shard_map.50 = (f32[512,128]{1,0:T(8,128)}, bf16[384,4096]{1,0:T(8,128)(2,1)S(1)}) custom-call(s32[3]{0:T(128)S(1)} %pad_add_fusion.where_ref, bf16[192,4096]{1,0:T(8,128)(2,1)S(1)} %shard_map.48.lam_ref, bf16[32,2,12,16,128]{4,3,2,1,0:T(8,128)(2,1)} %all-to-all-done.parts_in), custom_call_target="tpu_custom_call" | custom-call | tf_op jit(solution)/shard_map/pallas_call | solution.py:33
  181.7 0.0 copy-start
  181.8 1.6 copy-done
  183.4 8.7 %all-to-all-start.1 = ((f32[32,16,128]{2,1,0:T(8,128)}), f32[32,16,128]{2,1,0:T(8,128)S(1)}, u32[]{:S(2)}, u32[]{:S(2)}) async-start(f32[32,16,128]{2,1,0:T(8,128)} %bitcast.3), calls=%async_computation.1 | async-start | bytes 524288 | tf_op jit(solution)/shard_map/all_to_all | solution.py:228
  192.1 0.0 copy-done.4
  192.1 8.9 %all-to-all-done.1 = f32[32,16,128]{2,1,0:T(8,128)S(1)} async-done(((f32[32,16,128]{2,1,0:T(8,128)}), f32[32,16,128]{2,1,0:T(8,128)S(1)}, u32[]{:S(2)}, u32[]{:S(2)}) %all-to-all-start.1) | async-done | bytes 262176 | tf_op jit(solution)/shard_map/all_to_all | solution.py:228
  201.0 0.7 broadcast_in_dim.4
  201.7 7.4 %all-to-all-start.2 = ((f32[16,16,128]{2,1,0:T(8,128)}), f32[16,16,128]{2,1,0:T(8,128)S(1)}, u32[]{:S(2)}, u32[]{:S(2)}) async-start(f32[16,16,128]{2,1,0:T(8,128)} %broadcast_in_dim.4), calls=%async_computation.2 | async-start | bytes 262144 | tf_op jit(solution)/shard_map/all_to_all | solution.py:228
  209.1 0.0 copy-done.5
  209.1 0.2 fusion
  209.3 0.2 fusion.1
  209.6 0.4 fusion.8
  210.0 0.1 copy.6
  210.1 12.5 %all-to-all-done.2 = f32[16,16,128]{2,1,0:T(8,128)S(1)} async-done(((f32[16,16,128]{2,1,0:T(8,128)}), f32[16,16,128]{2,1,0:T(8,128)S(1)}, u32[]{:S(2)}, u32[]{:S(2)}) %all-to-all-start.2) | async-done | bytes 131104 | tf_op jit(solution)/shard_map/all_to_all | solution.py:228
  222.5 0.7 broadcast_in_dim.5
  223.2 6.3 %all-to-all-start.3 = ((bf16[32,16,128]{2,1,0:T(8,128)(2,1)}), bf16[32,16,128]{2,1,0:T(8,128)(2,1)S(1)}, u32[]{:S(2)}, u32[]{:S(2)}) async-start(bf16[32,16,128]{2,1,0:T(8,128)(2,1)} %broadcast_in_dim.5), calls=%async_computation.3 | async-start | bytes 262144 | tf_op jit(solution)/shard_map/all_to_all | solution.py:228
  229.5 7.7 %all-to-all-done.3 = bf16[32,16,128]{2,1,0:T(8,128)(2,1)S(1)} async-done(((bf16[32,16,128]{2,1,0:T(8,128)(2,1)}), bf16[32,16,128]{2,1,0:T(8,128)(2,1)S(1)}, u32[]{:S(2)}, u32[]{:S(2)}) %all-to-all-start.3) | async-done | bytes 131104 | tf_op jit(solution)/shard_map/all_to_all | solution.py:228
  237.3 0.0 copy-start.1
  237.3 1.9 copy-done.1
  239.2 2.3 shard_map.51
  241.5 39.7 %all_to_all.25.parts_ref = bf16[16,12,2,16,128]{4,3,2,1,0:T(8,128)(2,1)S(1)} all-to-all(bf16[16,12,2,16,128]{4,3,2,1,0:T(8,128)(2,1)S(1)} %bitcast.16), channel_id=1, replica_groups=mesh['zb'=2,'z4'=4,'y'=4,'zh'=2,'x'=4,'c'=2] {'z4','y'}, dimensions={0} | all-to-all | bytes 3145728 | tf_op jit(solution)/shard_map/all_to_all | solution.py:228
  281.1 1.4 shard_map.52
  (5 shorter events, 0.1 us)
Async XLA Ops:
  0.0 1.4 copy-start.3
  3.7 16.5 %copy-start.2 = (bf16[12,64,1024]{2,1,0:T(8,128)(2,1)S(1)}, bf16[12,64,1024]{2,1,0:T(8,128)(2,1)}, u32[]{:S(2)}) copy-start(bf16[12,64,1024]{2,1,0:T(8,128)(2,1)} %lam_ref.1) | copy-start | bytes 4718596
  3.7 172.2 %all-to-all-start = ((bf16[32,2,12,16,128]{4,3,2,1,0:T(8,128)(2,1)}), bf16[32,2,12,16,128]{4,3,2,1,0:T(8,128)(2,1)}, u32[]{:S(2)}, u32[]{:S(2)}) async-start(bf16[32,2,12,16,128]{4,3,2,1,0:T(8,128)(2,1)} %shard_map.49), calls=%async_computation | async-start | bytes 6291456 | tf_op jit(solution)/shard_map/all_to_all | solution.py:228
  21.1 22.0 %collective-permute-start = (bf16[4,2,12,16,128]{4,3,2,1,0:T(8,128)(2,1)S(1)}, bf16[4,2,12,16,128]{4,3,2,1,0:T(8,128)(2,1)S(1)}, u32[]{:S(2)}, u32[]{:S(2)}) collective-permute-start(bf16[4,2,12,16,128]{4,3,2,1,0:T(8,128)(2,1)S(1)} %get-tuple-element.16), channel_id=1, source_target_pairs={{0,16},{16,0},{32,48},{48,32},{1,17},{17,1},{33,49},{49,33},{2,18}... | collective-permute-start | bytes 1179656 | tf_op jit(solution)/shard_map/ppermute | solution.py:233
  24.2 28.1 %collective-permute-start.1 = (bf16[4,2,12,16,128]{4,3,2,1,0:T(8,128)(2,1)S(1)}, bf16[4,2,12,16,128]{4,3,2,1,0:T(8,128)(2,1)S(1)}, u32[]{:S(2)}, u32[]{:S(2)}) collective-permute-start(bf16[4,2,12,16,128]{4,3,2,1,0:T(8,128)(2,1)S(1)} %get-tuple-element.17), channel_id=1, source_target_pairs={{0,32},{16,48},{32,0},{48,16},{1,33},{17,49},{33,1},{49,17},{2,34}... | collective-permute-start | bytes 1179656 | tf_op jit(solution)/shard_map/ppermute | solution.py:233
  28.5 30.4 %collective-permute-start.2 = (bf16[4,2,12,16,128]{4,3,2,1,0:T(8,128)(2,1)S(1)}, bf16[4,2,12,16,128]{4,3,2,1,0:T(8,128)(2,1)S(1)}, u32[]{:S(2)}, u32[]{:S(2)}) collective-permute-start(bf16[4,2,12,16,128]{4,3,2,1,0:T(8,128)(2,1)S(1)} %get-tuple-element.18), channel_id=1, source_target_pairs={{0,48},{16,32},{32,16},{48,0},{1,49},{17,33},{33,17},{49,1},{2,50}... | collective-permute-start | bytes 1179656 | tf_op jit(solution)/shard_map/ppermute | solution.py:233
  59.6 27.2 %collective-permute-start.3 = (bf16[4,2,12,16,128]{4,3,2,1,0:T(8,128)(2,1)S(1)}, bf16[4,2,12,16,128]{4,3,2,1,0:T(8,128)(2,1)S(1)}, u32[]{:S(2)}, u32[]{:S(2)}) collective-permute-start(bf16[4,2,12,16,128]{4,3,2,1,0:T(8,128)(2,1)S(1)} %get-tuple-element.20), channel_id=1, source_target_pairs={{0,64},{64,0},{128,192},{192,128},{1,65},{65,1},{129,193},{193,129... | collective-permute-start | bytes 1179656 | tf_op jit(solution)/shard_map/ppermute | solution.py:233
  63.4 31.8 %collective-permute-start.4 = (bf16[4,2,12,16,128]{4,3,2,1,0:T(8,128)(2,1)S(1)}, bf16[4,2,12,16,128]{4,3,2,1,0:T(8,128)(2,1)S(1)}, u32[]{:S(2)}, u32[]{:S(2)}) collective-permute-start(bf16[4,2,12,16,128]{4,3,2,1,0:T(8,128)(2,1)S(1)} %get-tuple-element.21), channel_id=1, source_target_pairs={{0,128},{64,192},{128,0},{192,64},{1,129},{65,193},{129,1},{193,65... | collective-permute-start | bytes 1179656 | tf_op jit(solution)/shard_map/ppermute | solution.py:233
  65.3 109.3 %collective-permute-start.5 = (bf16[4,2,12,16,128]{4,3,2,1,0:T(8,128)(2,1)S(1)}, bf16[4,2,12,16,128]{4,3,2,1,0:T(8,128)(2,1)S(1)}, u32[]{:S(2)}, u32[]{:S(2)}) collective-permute-start(bf16[4,2,12,16,128]{4,3,2,1,0:T(8,128)(2,1)S(1)} %get-tuple-element.22), channel_id=1, source_target_pairs={{0,192},{64,128},{128,64},{192,0},{1,193},{65,129},{129,65},{193,1... | collective-permute-start | bytes 1179656 | tf_op jit(solution)/shard_map/ppermute | solution.py:233
  175.8 16.2 %copy-start.4 = (s32[264,2]{0,1:T(2,128)S(1)}, s32[264,2]{0,1:T(2,128)}, u32[]{:S(2)}) copy-start(s32[264,2]{0,1:T(2,128)} %param.7) | copy-start | bytes 6340
  175.8 33.3 %copy-start.5 = (s32[32]{0:T(128)S(1)}, s32[32]{0:T(128)}, u32[]{:S(2)}) copy-start(s32[32]{0:T(128)} %param.6) | copy-start | bytes 388
  181.7 1.6 copy-start
  183.4 17.6 %all-to-all-start.1 = ((f32[32,16,128]{2,1,0:T(8,128)}), f32[32,16,128]{2,1,0:T(8,128)S(1)}, u32[]{:S(2)}, u32[]{:S(2)}) async-start(f32[32,16,128]{2,1,0:T(8,128)} %bitcast.3), calls=%async_computation.1 | async-start | bytes 524288 | tf_op jit(solution)/shard_map/all_to_all | solution.py:228
  201.7 20.8 %all-to-all-start.2 = ((f32[16,16,128]{2,1,0:T(8,128)}), f32[16,16,128]{2,1,0:T(8,128)S(1)}, u32[]{:S(2)}, u32[]{:S(2)}) async-start(f32[16,16,128]{2,1,0:T(8,128)} %broadcast_in_dim.4), calls=%async_computation.2 | async-start | bytes 262144 | tf_op jit(solution)/shard_map/all_to_all | solution.py:228
  223.2 14.0 %all-to-all-start.3 = ((bf16[32,16,128]{2,1,0:T(8,128)(2,1)}), bf16[32,16,128]{2,1,0:T(8,128)(2,1)S(1)}, u32[]{:S(2)}, u32[]{:S(2)}) async-start(bf16[32,16,128]{2,1,0:T(8,128)(2,1)} %broadcast_in_dim.5), calls=%async_computation.3 | async-start | bytes 262144 | tf_op jit(solution)/shard_map/all_to_all | solution.py:228
  237.3 1.9 copy-start.1

commit v6 on v5

--- a/solution.py
+++ b/solution.py
@@ -19,13 +19,14 @@
 STEPS = 4
 SQUARE = 256
 VMEM_LIMIT = 48 * 1024 * 1024
+VMEM_MOST = 62 * 1024 * 1024
 
 
 def onehot(index, count):
     return (index[:, None] == jnp.arange(count)[None, :]).astype(jnp.float32)
 
 
-def call(body, out_shape, args, scratch=(), scalars=0, free_in=(), free_out=()):
+def call(body, out_shape, args, scratch=(), scalars=0, free_in=(), free_out=(), limit=VMEM_LIMIT):
     many = isinstance(out_shape, (list, tuple))
     outs = out_shape if many else [out_shape]
     smem, vmem, free = (pl.BlockSpec(memory_space=m) for m in (pltpu.SMEM, pltpu.VMEM, pl.ANY))
@@ -36,7 +37,7 @@
         in_specs=[smem] * scalars + [free if n in free_in else vmem for n in range(scalars, len(args))],
         out_specs=out_specs if many else out_specs[0],
         scratch_shapes=list(scratch),
-        compiler_params=pltpu.CompilerParams(vmem_limit_bytes=VMEM_LIMIT),
+        compiler_params=pltpu.CompilerParams(vmem_limit_bytes=limit),
     )(*args)
 
 
@@ -139,14 +140,21 @@
     return jnp.concatenate([x, pltpu.roll(x, LANES // 2, 1)], axis=0)
 
 
-def cross_kernel(where_ref, lam_ref, parts_in, sym_ref, amp_ref, parts_ref, cross_ref, sems):
-    zb = where_ref[0]
+def amp_kernel(parts_in, amp_ref, parts_ref, sems):
     copies = []
     for step in range(parts_ref.shape[0] // STEPS):
         some = pl.ds(step * STEPS, STEPS)
         copies.append(pltpu.make_async_copy(parts_in.at[some], parts_ref.at[some], sems.at[step]))
         copies[-1].start()
     all_panels(parts_ref, amp_ref, lambda step: copies[step].wait())
+
+
+def cross_kernel(where_ref, lam_in, parts_ref, sym_ref, lam_ref, amp_ref, cross_ref, sem):
+    zb = where_ref[0]
+    come = pltpu.make_async_copy(lam_in, lam_ref, sem.at[0])
+    come.start()
+    all_panels(parts_ref, amp_ref)
+    come.wait()
     half = lam_ref.shape[0]
     cross_ref[...] = jnp.zeros_like(cross_ref)
     for n, which in enumerate((zb, 1 - zb)):
@@ -167,6 +175,18 @@
     ):
         sym_ref[at : at + rows.shape[0]] = rows
         at += rows.shape[0]
+
+
+def first_sum(terms_ref, out_ref):
+    out_ref[...] = jnp.broadcast_to(jnp.sum(terms_ref[...], axis=0), out_ref.shape)
+
+
+def second_sum(where_ref, terms_ref, out_ref):
+    height = terms_ref.shape[0]
+    halves = [jnp.sum(terms_ref[n * height // 2 : (n + 1) * height // 2], axis=0) for n in range(2)]
+    mine = jnp.where(where_ref[0] == 0, halves[0], halves[1])
+    total = jnp.where(where_ref[3] == 1, halves[0] + halves[1], mine).astype(jnp.bfloat16)
+    out_ref[...] = jnp.broadcast_to(total, out_ref.shape)
 
 
 def density_kernel(where_ref, sym_ref, listed_ref, amp_ref, out_ref, square_ref, inter_ref, flat_ref):
@@ -239,9 +259,13 @@
     panel_size, rows, cols = lambda_amps.shape
     pairs, half = npanels * panel_size, npanels * panel_size // 2
     depth = ROWS * WIDE
+    bf16, f32 = jnp.bfloat16, jnp.float32
     folded = half + half // 2 + LANES + LANES // 2 + (half - LANES) // 2
-    bf16, f32 = jnp.bfloat16, jnp.float32
-    where = jnp.stack([lax.axis_index("zb"), lax.axis_index("z4"), lax.axis_index("y")]).astype(jnp.int32)
+    plane, height = lax.axis_size(PLANE), lax.axis_size(LINE)
+    own = folded // plane
+    between = lax.axis_index(PLANE) * own < half * half // LANES
+    where = [lax.axis_index("zb"), lax.axis_index("z4"), lax.axis_index("y"), between]
+    where = jnp.stack([w.astype(jnp.int32) for w in where])
 
     home = onehot(panel_home, npanels)
     first = jnp.dot(onehot(pair_list[:, 0], npanels), home, precision=lax.Precision.HIGHEST)
@@ -250,7 +274,7 @@
     listed = jnp.minimum(listed + listed.T, 1.0)
 
     part = (TILES, panel_size, ROWS, LANES)
-    amp_parts = call(pack_amp, jax.ShapeDtypeStruct((npanels,) + part, bf16), (t_amps,), [dma(2 * npanels)], free_in=(0,), free_out=(0,))
+    amp_parts = call(pack_amp, jax.ShapeDtypeStruct((npanels,) + part, bf16), (t_amps,), [dma(2 * npanels)], free_out=(0,), limit=VMEM_MOST)
     four = [jax.ShapeDtypeStruct((STEPS,) + part, bf16)] * STEPS
     lam_parts = call(pack_lam, four, (where, lambda_amps), scalars=1)
     amp_parts = exchange(amp_parts, PAIR)
@@ -262,26 +286,28 @@
         [pltpu.VMEM((npanels // 2,) + part, bf16)],
         scalars=1,
     )
-    sym, amp = call(
+    brought = [pltpu.VMEM((npanels,) + part, bf16), dma(npanels // STEPS)]
+    sym = call(
         cross_kernel,
+        jax.ShapeDtypeStruct((folded, LANES), f32),
+        (where, lam, amp_parts),
         [
-            jax.ShapeDtypeStruct((folded, LANES), f32),
-            jax.ShapeDtypeStruct((pairs, depth), bf16),
+            pltpu.VMEM((half, depth), bf16),
+            pltpu.VMEM((pairs, depth), bf16),
+            pltpu.VMEM((2, SQUARE, SQUARE), f32),
+            dma(1),
         ],
-        (where, lam, amp_parts),
-        [pltpu.VMEM((npanels,) + part, bf16), pltpu.VMEM((2, SQUARE, SQUARE), f32), dma(npanels // STEPS)],
         scalars=1,
-        free_in=(2,),
-    )
-    plane, height = lax.axis_size(PLANE), lax.axis_size(LINE)
-    own = folded // plane
+        free_in=(1,),
+        limit=VMEM_LIMIT,
+    )
     terms = exchange(sym.reshape(plane, own, LANES), PLANE)
-    terms = exchange(jnp.broadcast_to(jnp.sum(terms, axis=0), (height, own, LANES)), LINE)
-    halves = terms.reshape(2, height // 2, own, LANES).sum(axis=1)
-    mine = jnp.where(where[0] == 0, halves[0], halves[1])
-    both = lax.axis_index(PLANE) * own < half * half // LANES
-    total = jnp.where(both, halves[0] + halves[1], mine).astype(bf16)
-    upper = exchange(jnp.broadcast_to(total, (plane, own, LANES)), PLANE)
+    terms = call(first_sum, jax.ShapeDtypeStruct((height, own, LANES), f32), (terms,))
+    terms = exchange(terms, LINE)
+    terms = call(second_sum, jax.ShapeDtypeStruct((plane, own, LANES), bf16), (where, terms), scalars=1)
+    later, _ = lax.optimization_barrier((amp_parts, terms))
+    upper = exchange(terms, PLANE)
+    amp = call(amp_kernel, jax.ShapeDtypeStruct((pairs, depth), bf16), (later,), brought, free_in=(0,))
     result = call(
         density_kernel,
         jax.ShapeDtypeStruct((half, TILES, ROWS, LANES), bf16),

time: 284 us -> 281 us (0.989)
  waiting for transfers between devices: 163 us -> 158 us
  Pallas kernels: 14.6 us -> 19 us
    pallas_call x7 -> x10, Pallas kernels: 14.6 us -> 19 us  [call(): pl.pallas_call(body, out_shape=out_shape, in_specs=[smem] * scalars + [fr...]
    all_to_all x4, waiting for transfers between devices: 29.1 us -> 25.7 us  [exchange(): return lax.all_to_all(x, axis, split_axis=0, concat_axis=0, tiled=True)]
  transfers between devices with their start and end apart: 10 -> 10, of which waited for: 9 -> 9; matrix products, arithmetic and copies ran while one was open for 0% -> 0% of each run, Pallas kernels for 1% -> 2%
where the time goes in v6:
time: 281 us; the launch traced here: 280 us
  waiting for transfers between devices  158 us (56%)
  starting transfers between devices  57.4 us (20%)
  blocking collectives  39.7 us (14%)
  Pallas kernels  19 us (7%)
  local copies, waits for them, and re-layouts  4.06 us (1%)
    ppermute x6, waiting for transfers between devices, shifts(): lax.ppermute(part, axis, [(k, k ^ s) for k in range(STEPS)])  133 us
    all_to_all x1, blocking collectives, exchange(): return lax.all_to_all(x, axis, split_axis=0, concat_axis=0, tiled=True)  39.7 us
    all_to_all x4, starting transfers between devices, exchange(): return lax.all_to_all(x, axis, split_axis=0, concat_axis=0, tiled=True)  38.5 us
    all_to_all x4, waiting for transfers between devices, exchange(): return lax.all_to_all(x, axis, split_axis=0, concat_axis=0, tiled=True)  25.7 us
    pallas_call x10, Pallas kernels, call(): pl.pallas_call(body, out_shape=out_shape, in_specs=[smem] * scalars + [fr...  19 us
    ppermute x6, starting transfers between devices, shifts(): lax.ppermute(part, axis, [(k, k ^ s) for k in range(STEPS)])  18.9 us
  transfers between devices with their start and end apart: 10, of which 9 were waited for; matrix products, arithmetic and copies ran while one was open for 0% of the time, Pallas kernels for 2%

profile of v6, /device:TPU:1, one launch (start us, length us, event | category | flops | bytes accessed | tf_op | source)
XLA Modules:
  0.0 279.6 jit_solution(10630815949778593912)
XLA Ops:
  0.0 3.6 %shard_map.49 = bf16[32,2,12,16,128]{4,3,2,1,0:T(8,128)(2,1)} custom-call(bf16[12,64,1024]{2,1,0:T(8,128)(2,1)} %amp_ref.1), custom_call_target="tpu_custom_call" | custom-call | tf_op jit(solution)/shard_map/pallas_call | solution.py:34
  3.6 16.1 %all-to-all-start = ((bf16[32,2,12,16,128]{4,3,2,1,0:T(8,128)(2,1)}), bf16[32,2,12,16,128]{4,3,2,1,0:T(8,128)(2,1)S(1)}, u32[]{:S(2)}, u32[]{:S(2)}) async-start(bf16[32,2,12,16,128]{4,3,2,1,0:T(8,128)(2,1)} %shard_map.49), calls=%async_computation | async-start | bytes 6291456 | tf_op jit(solution)/shard_map/all_to_all | solution.py:248
  19.8 0.1 pad_add_fusion.where_ref
  19.9 0.0 copy-start.3
  19.9 1.4 copy-done.3
  21.3 0.9 shard_map.46
  22.2 3.1 %collective-permute-start = (bf16[4,2,12,16,128]{4,3,2,1,0:T(8,128)(2,1)S(1)}, bf16[4,2,12,16,128]{4,3,2,1,0:T(8,128)(2,1)S(1)}, u32[]{:S(2)}, u32[]{:S(2)}) collective-permute-start(bf16[4,2,12,16,128]{4,3,2,1,0:T(8,128)(2,1)S(1)} %get-tuple-element.15), channel_id=1, source_target_pairs={{0,16},{16,0},{32,48},{48,32},{1,17},{17,1},{33,49},{49,33},{2,18}... | collective-permute-start | bytes 1179656 | tf_op jit(solution)/shard_map/ppermute | solution.py:253
  25.4 4.3 %collective-permute-start.1 = (bf16[4,2,12,16,128]{4,3,2,1,0:T(8,128)(2,1)S(1)}, bf16[4,2,12,16,128]{4,3,2,1,0:T(8,128)(2,1)S(1)}, u32[]{:S(2)}, u32[]{:S(2)}) collective-permute-start(bf16[4,2,12,16,128]{4,3,2,1,0:T(8,128)(2,1)S(1)} %get-tuple-element.16), channel_id=1, source_target_pairs={{0,32},{16,48},{32,0},{48,16},{1,33},{17,49},{33,1},{49,17},{2,34}... | collective-permute-start | bytes 1179656 | tf_op jit(solution)/shard_map/ppermute | solution.py:253
  29.7 2.1 collective-permute-start.2
  31.8 11.8 %collective-permute-done.refs_1_ = bf16[4,2,12,16,128]{4,3,2,1,0:T(8,128)(2,1)S(1)} collective-permute-done((bf16[4,2,12,16,128]{4,3,2,1,0:T(8,128)(2,1)S(1)}, bf16[4,2,12,16,128]{4,3,2,1,0:T(8,128)(2,1)S(1)}, u32[]{:S(2)}, u32[]{:S(2)}) %collective-permute-start) | collective-permute-done | bytes 393248 | tf_op jit(solution)/shard_map/ppermute | solution.py:253
  43.6 8.4 %collective-permute-done.1.refs_2_ = bf16[4,2,12,16,128]{4,3,2,1,0:T(8,128)(2,1)S(1)} collective-permute-done((bf16[4,2,12,16,128]{4,3,2,1,0:T(8,128)(2,1)S(1)}, bf16[4,2,12,16,128]{4,3,2,1,0:T(8,128)(2,1)S(1)}, u32[]{:S(2)}, u32[]{:S(2)}) %collective-permute-start.1) | collective-permute-done | bytes 393248 | tf_op jit(solution)/shard_map/ppermute | solution.py:253
  52.0 9.2 %collective-permute-done.2.refs_3_ = bf16[4,2,12,16,128]{4,3,2,1,0:T(8,128)(2,1)S(1)} collective-permute-done((bf16[4,2,12,16,128]{4,3,2,1,0:T(8,128)(2,1)S(1)}, bf16[4,2,12,16,128]{4,3,2,1,0:T(8,128)(2,1)S(1)}, u32[]{:S(2)}, u32[]{:S(2)}) %collective-permute-start.2) | collective-permute-done | bytes 393248 | tf_op jit(solution)/shard_map/ppermute | solution.py:253
  61.2 0.6 shard_map.47
  61.8 1.9 collective-permute-start.3
  63.8 1.9 collective-permute-start.4
  65.7 5.4 %collective-permute-start.5 = (bf16[4,2,12,16,128]{4,3,2,1,0:T(8,128)(2,1)S(1)}, bf16[4,2,12,16,128]{4,3,2,1,0:T(8,128)(2,1)S(1)}, u32[]{:S(2)}, u32[]{:S(2)}) collective-permute-start(bf16[4,2,12,16,128]{4,3,2,1,0:T(8,128)(2,1)S(1)} %get-tuple-element.21), channel_id=1, source_target_pairs={{0,192},{64,128},{128,64},{192,0},{1,193},{65,129},{129,65},{193,1... | collective-permute-start | bytes 1179656 | tf_op jit(solution)/shard_map/ppermute | solution.py:253
  71.1 15.4 %collective-permute-done.3.refs_1_ = bf16[4,2,12,16,128]{4,3,2,1,0:T(8,128)(2,1)S(1)} collective-permute-done((bf16[4,2,12,16,128]{4,3,2,1,0:T(8,128)(2,1)S(1)}, bf16[4,2,12,16,128]{4,3,2,1,0:T(8,128)(2,1)S(1)}, u32[]{:S(2)}, u32[]{:S(2)}) %collective-permute-start.3) | collective-permute-done | bytes 393248 | tf_op jit(solution)/shard_map/ppermute | solution.py:253
  86.5 8.5 %collective-permute-done.4.refs_2_ = bf16[4,2,12,16,128]{4,3,2,1,0:T(8,128)(2,1)S(1)} collective-permute-done((bf16[4,2,12,16,128]{4,3,2,1,0:T(8,128)(2,1)S(1)}, bf16[4,2,12,16,128]{4,3,2,1,0:T(8,128)(2,1)S(1)}, u32[]{:S(2)}, u32[]{:S(2)}) %collective-permute-start.4) | collective-permute-done | bytes 393248 | tf_op jit(solution)/shard_map/ppermute | solution.py:253
  95.0 79.4 %collective-permute-done.5.refs_3_ = bf16[4,2,12,16,128]{4,3,2,1,0:T(8,128)(2,1)S(1)} collective-permute-done((bf16[4,2,12,16,128]{4,3,2,1,0:T(8,128)(2,1)S(1)}, bf16[4,2,12,16,128]{4,3,2,1,0:T(8,128)(2,1)S(1)}, u32[]{:S(2)}, u32[]{:S(2)}) %collective-permute-start.5) | collective-permute-done | bytes 393248 | tf_op jit(solution)/shard_map/ppermute | solution.py:253
  174.4 1.2 shard_map.48.lam_in
  175.7 0.0 copy-start.1
  175.7 1.1 copy-done.1
  176.8 0.0 all-to-all-done.parts_ref.parts_in
  176.8 0.0 copy-start.2
  176.8 1.4 copy-done.2
  178.2 0.0 copy-start
  178.2 0.0 copy-start.4
  178.2 0.0 copy-start.5
  178.2 3.6 %shard_map.50 = f32[512,128]{1,0:T(8,128)} custom-call(s32[4]{0:T(128)S(1)} %pad_add_fusion.where_ref, bf16[192,4096]{1,0:T(8,128)(2,1)S(1)} %copy-done.2, bf16[32,2,12,16,128]{4,3,2,1,0:T(8,128)(2,1)S(1)} %all-to-all-done.parts_ref.parts_in), custom_call_target="tpu_custom_call" | custom-call | tf_op jit(solution)/shard_map/pallas_call | solution.py:34
  181.8 0.0 copy-done
  181.8 8.7 %all-to-all-start.1 = ((f32[32,16,128]{2,1,0:T(8,128)}), f32[32,16,128]{2,1,0:T(8,128)S(1)}, u32[]{:S(2)}, u32[]{:S(2)}) async-start(f32[32,16,128]{2,1,0:T(8,128)} %bitcast.4), calls=%async_computation.1 | async-start | bytes 524288 | tf_op jit(solution)/shard_map/all_to_all | solution.py:248
  190.5 0.0 copy-done.4
  190.6 8.9 %all-to-all-done.1.terms_ref = f32[32,16,128]{2,1,0:T(8,128)S(1)} async-done(((f32[32,16,128]{2,1,0:T(8,128)}), f32[32,16,128]{2,1,0:T(8,128)S(1)}, u32[]{:S(2)}, u32[]{:S(2)}) %all-to-all-start.1) | async-done | bytes 262176 | tf_op jit(solution)/shard_map/all_to_all | solution.py:248
  199.4 0.7 shard_map.51
  200.1 7.4 %all-to-all-start.2 = ((f32[16,16,128]{2,1,0:T(8,128)}), f32[16,16,128]{2,1,0:T(8,128)S(1)}, u32[]{:S(2)}, u32[]{:S(2)}) async-start(f32[16,16,128]{2,1,0:T(8,128)} %shard_map.51), calls=%async_computation.2 | async-start | bytes 262144 | tf_op jit(solution)/shard_map/all_to_all | solution.py:248
  207.5 0.0 copy-done.5
  207.5 0.2 fusion
  207.8 0.2 fusion.1
  208.0 0.4 fusion.7
  208.4 0.1 copy.5
  208.5 12.5 %all-to-all-done.2.terms_ref = f32[16,16,128]{2,1,0:T(8,128)S(1)} async-done(((f32[16,16,128]{2,1,0:T(8,128)}), f32[16,16,128]{2,1,0:T(8,128)S(1)}, u32[]{:S(2)}, u32[]{:S(2)}) %all-to-all-start.2) | async-done | bytes 131104 | tf_op jit(solution)/shard_map/all_to_all | solution.py:248
  221.0 1.2 shard_map.52
  222.2 6.3 %all-to-all-start.3 = ((bf16[32,16,128]{2,1,0:T(8,128)(2,1)}), bf16[32,16,128]{2,1,0:T(8,128)(2,1)S(1)}, u32[]{:S(2)}, u32[]{:S(2)}) async-start(bf16[32,16,128]{2,1,0:T(8,128)(2,1)} %shard_map.52), calls=%async_computation.3 | async-start | bytes 262144 | tf_op jit(solution)/shard_map/all_to_all | solution.py:248
  228.5 3.4 %shard_map.53.amp_ref = bf16[384,4096]{1,0:T(8,128)(2,1)S(1)} custom-call(bf16[32,2,12,16,128]{4,3,2,1,0:T(8,128)(2,1)} %copy-done), custom_call_target="tpu_custom_call" | custom-call | tf_op jit(solution)/shard_map/pallas_call | solution.py:34
  231.9 4.3 %all-to-all-done.3 = bf16[32,16,128]{2,1,0:T(8,128)(2,1)S(1)} async-done(((bf16[32,16,128]{2,1,0:T(8,128)(2,1)}), bf16[32,16,128]{2,1,0:T(8,128)(2,1)S(1)}, u32[]{:S(2)}, u32[]{:S(2)}) %all-to-all-start.3) | async-done | bytes 131104 | tf_op jit(solution)/shard_map/all_to_all | solution.py:248
  236.2 2.3 shard_map.54
  238.5 39.7 %all_to_all.25.parts_ref = bf16[16,12,2,16,128]{4,3,2,1,0:T(8,128)(2,1)S(1)} all-to-all(bf16[16,12,2,16,128]{4,3,2,1,0:T(8,128)(2,1)S(1)} %bitcast.13), channel_id=1, replica_groups=mesh['zb'=2,'z4'=4,'y'=4,'zh'=2,'x'=4,'c'=2] {'z4','y'}, dimensions={0} | all-to-all | bytes 3145728 | tf_op jit(solution)/shard_map/all_to_all | solution.py:248
  278.2 1.4 shard_map.55
  (2 shorter events, 0.0 us)
Async XLA Ops:
  3.6 173.2 %all-to-all-start = ((bf16[32,2,12,16,128]{4,3,2,1,0:T(8,128)(2,1)}), bf16[32,2,12,16,128]{4,3,2,1,0:T(8,128)(2,1)S(1)}, u32[]{:S(2)}, u32[]{:S(2)}) async-start(bf16[32,2,12,16,128]{4,3,2,1,0:T(8,128)(2,1)} %shard_map.49), calls=%async_computation | async-start | bytes 6291456 | tf_op jit(solution)/shard_map/all_to_all | solution.py:248
  19.9 1.4 copy-start.3
  22.2 21.4 %collective-permute-start = (bf16[4,2,12,16,128]{4,3,2,1,0:T(8,128)(2,1)S(1)}, bf16[4,2,12,16,128]{4,3,2,1,0:T(8,128)(2,1)S(1)}, u32[]{:S(2)}, u32[]{:S(2)}) collective-permute-start(bf16[4,2,12,16,128]{4,3,2,1,0:T(8,128)(2,1)S(1)} %get-tuple-element.15), channel_id=1, source_target_pairs={{0,16},{16,0},{32,48},{48,32},{1,17},{17,1},{33,49},{49,33},{2,18}... | collective-permute-start | bytes 1179656 | tf_op jit(solution)/shard_map/ppermute | solution.py:253
  25.4 26.6 %collective-permute-start.1 = (bf16[4,2,12,16,128]{4,3,2,1,0:T(8,128)(2,1)S(1)}, bf16[4,2,12,16,128]{4,3,2,1,0:T(8,128)(2,1)S(1)}, u32[]{:S(2)}, u32[]{:S(2)}) collective-permute-start(bf16[4,2,12,16,128]{4,3,2,1,0:T(8,128)(2,1)S(1)} %get-tuple-element.16), channel_id=1, source_target_pairs={{0,32},{16,48},{32,0},{48,16},{1,33},{17,49},{33,1},{49,17},{2,34}... | collective-permute-start | bytes 1179656 | tf_op jit(solution)/shard_map/ppermute | solution.py:253
  29.7 31.5 %collective-permute-start.2 = (bf16[4,2,12,16,128]{4,3,2,1,0:T(8,128)(2,1)S(1)}, bf16[4,2,12,16,128]{4,3,2,1,0:T(8,128)(2,1)S(1)}, u32[]{:S(2)}, u32[]{:S(2)}) collective-permute-start(bf16[4,2,12,16,128]{4,3,2,1,0:T(8,128)(2,1)S(1)} %get-tuple-element.17), channel_id=1, source_target_pairs={{0,48},{16,32},{32,16},{48,0},{1,49},{17,33},{33,17},{49,1},{2,50}... | collective-permute-start | bytes 1179656 | tf_op jit(solution)/shard_map/ppermute | solution.py:253
  61.8 24.7 %collective-permute-start.3 = (bf16[4,2,12,16,128]{4,3,2,1,0:T(8,128)(2,1)S(1)}, bf16[4,2,12,16,128]{4,3,2,1,0:T(8,128)(2,1)S(1)}, u32[]{:S(2)}, u32[]{:S(2)}) collective-permute-start(bf16[4,2,12,16,128]{4,3,2,1,0:T(8,128)(2,1)S(1)} %get-tuple-element.19), channel_id=1, source_target_pairs={{0,64},{64,0},{128,192},{192,128},{1,65},{65,1},{129,193},{193,129... | collective-permute-start | bytes 1179656 | tf_op jit(solution)/shard_map/ppermute | solution.py:253
  63.8 31.3 %collective-permute-start.4 = (bf16[4,2,12,16,128]{4,3,2,1,0:T(8,128)(2,1)S(1)}, bf16[4,2,12,16,128]{4,3,2,1,0:T(8,128)(2,1)S(1)}, u32[]{:S(2)}, u32[]{:S(2)}) collective-permute-start(bf16[4,2,12,16,128]{4,3,2,1,0:T(8,128)(2,1)S(1)} %get-tuple-element.20), channel_id=1, source_target_pairs={{0,128},{64,192},{128,0},{192,64},{1,129},{65,193},{129,1},{193,65... | collective-permute-start | bytes 1179656 | tf_op jit(solution)/shard_map/ppermute | solution.py:253
  65.7 108.7 %collective-permute-start.5 = (bf16[4,2,12,16,128]{4,3,2,1,0:T(8,128)(2,1)S(1)}, bf16[4,2,12,16,128]{4,3,2,1,0:T(8,128)(2,1)S(1)}, u32[]{:S(2)}, u32[]{:S(2)}) collective-permute-start(bf16[4,2,12,16,128]{4,3,2,1,0:T(8,128)(2,1)S(1)} %get-tuple-element.21), channel_id=1, source_target_pairs={{0,192},{64,128},{128,64},{192,0},{1,193},{65,129},{129,65},{193,1... | collective-permute-start | bytes 1179656 | tf_op jit(solution)/shard_map/ppermute | solution.py:253
  175.7 1.1 copy-start.1
  176.8 1.4 copy-start.2
  178.2 3.6 %copy-start = (bf16[32,2,12,16,128]{4,3,2,1,0:T(8,128)(2,1)}, bf16[32,2,12,16,128]{4,3,2,1,0:T(8,128)(2,1)S(1)}, u32[]{:S(2)}) copy-start(bf16[32,2,12,16,128]{4,3,2,1,0:T(8,128)(2,1)S(1)} %all-to-all-done.parts_ref.parts_in) | copy-start | bytes 9437188
  178.2 12.3 %copy-start.4 = (s32[264,2]{0,1:T(2,128)S(1)}, s32[264,2]{0,1:T(2,128)}, u32[]{:S(2)}) copy-start(s32[264,2]{0,1:T(2,128)} %param.7) | copy-start | bytes 6340
  178.2 29.3 %copy-start.5 = (s32[32]{0:T(128)S(1)}, s32[32]{0:T(128)}, u32[]{:S(2)}) copy-start(s32[32]{0:T(128)} %param.6) | copy-start | bytes 388
  181.8 17.6 %all-to-all-start.1 = ((f32[32,16,128]{2,1,0:T(8,128)}), f32[32,16,128]{2,1,0:T(8,128)S(1)}, u32[]{:S(2)}, u32[]{:S(2)}) async-start(f32[32,16,128]{2,1,0:T(8,128)} %bitcast.4), calls=%async_computation.1 | async-start | bytes 524288 | tf_op jit(solution)/shard_map/all_to_all | solution.py:248
  200.1 20.8 %all-to-all-start.2 = ((f32[16,16,128]{2,1,0:T(8,128)}), f32[16,16,128]{2,1,0:T(8,128)S(1)}, u32[]{:S(2)}, u32[]{:S(2)}) async-start(f32[16,16,128]{2,1,0:T(8,128)} %shard_map.51), calls=%async_computation.2 | async-start | bytes 262144 | tf_op jit(solution)/shard_map/all_to_all | solution.py:248
  222.2 14.0 %all-to-all-start.3 = ((bf16[32,16,128]{2,1,0:T(8,128)(2,1)}), bf16[32,16,128]{2,1,0:T(8,128)(2,1)S(1)}, u32[]{:S(2)}, u32[]{:S(2)}) async-start(bf16[32,16,128]{2,1,0:T(8,128)(2,1)} %shard_map.52), calls=%async_computation.3 | async-start | bytes 262144 | tf_op jit(solution)/shard_map/all_to_all | solution.py:248

commit v7 on v6

--- a/solution.py
+++ b/solution.py
@@ -45,19 +45,24 @@
     return pltpu.SemaphoreType.DMA((count,))
 
 
-def pack_amp(amp_ref, out_ref, sems):
+def pack_amp(amp_in, out_ref, amp_ref, sems):
     across = amp_ref.shape[2] // WIDE
-    parts = amp_ref.shape[1] // ROWS * across
-    copies = []
-    for d in range(parts):
-        i, c = divmod(d, across)
-        for tile in range(TILES):
-            at = c * WIDE + tile * LANES
-            part = amp_ref.at[:, pl.ds(i * ROWS, ROWS), pl.ds(at, LANES)]
-            for twin in (d, parts + d):
-                copies.append(pltpu.make_async_copy(part, out_ref.at[twin, tile], sems.at[len(copies)]))
-                copies[-1].start()
-    for copy in copies:
+    down = amp_ref.shape[1] // ROWS
+    come, go = [], []
+    for i in range(down):
+        rows = (slice(None), pl.ds(i * ROWS, ROWS))
+        come.append(pltpu.make_async_copy(amp_in.at[rows], amp_ref.at[rows], sems.at[i]))
+        come[-1].start()
+    for i in range(down):
+        come[i].wait()
+        for c in range(across):
+            for tile in range(TILES):
+                part = amp_ref.at[:, pl.ds(i * ROWS, ROWS), pl.ds(c * WIDE + tile * LANES, LANES)]
+                for twin in range(2):
+                    place = out_ref.at[(twin * down + i) * across + c, tile]
+                    go.append(pltpu.make_async_copy(part, place, sems.at[down + len(go)]))
+                    go[-1].start()
+    for copy in go:
         copy.wait()
 
 
@@ -149,12 +154,8 @@
     all_panels(parts_ref, amp_ref, lambda step: copies[step].wait())
 
 
-def cross_kernel(where_ref, lam_in, parts_ref, sym_ref, lam_ref, amp_ref, cross_ref, sem):
+def cross_kernel(where_ref, lam_ref, amp_ref, sym_ref, cross_ref):
     zb = where_ref[0]
-    come = pltpu.make_async_copy(lam_in, lam_ref, sem.at[0])
-    come.start()
-    all_panels(parts_ref, amp_ref)
-    come.wait()
     half = lam_ref.shape[0]
     cross_ref[...] = jnp.zeros_like(cross_ref)
     for n, which in enumerate((zb, 1 - zb)):
@@ -175,18 +176,6 @@
     ):
         sym_ref[at : at + rows.shape[0]] = rows
         at += rows.shape[0]
-
-
-def first_sum(terms_ref, out_ref):
-    out_ref[...] = jnp.broadcast_to(jnp.sum(terms_ref[...], axis=0), out_ref.shape)
-
-
-def second_sum(where_ref, terms_ref, out_ref):
-    height = terms_ref.shape[0]
-    halves = [jnp.sum(terms_ref[n * height // 2 : (n + 1) * height // 2], axis=0) for n in range(2)]
-    mine = jnp.where(where_ref[0] == 0, halves[0], halves[1])
-    total = jnp.where(where_ref[3] == 1, halves[0] + halves[1], mine).astype(jnp.bfloat16)
-    out_ref[...] = jnp.broadcast_to(total, out_ref.shape)
 
 
 def density_kernel(where_ref, sym_ref, listed_ref, amp_ref, out_ref, square_ref, inter_ref, flat_ref):
@@ -274,7 +263,7 @@
     listed = jnp.minimum(listed + listed.T, 1.0)
 
     part = (TILES, panel_size, ROWS, LANES)
-    amp_parts = call(pack_amp, jax.ShapeDtypeStruct((npanels,) + part, bf16), (t_amps,), [dma(2 * npanels)], free_out=(0,), limit=VMEM_MOST)
+    amp_parts = call(pack_amp, jax.ShapeDtypeStruct((npanels,) + part, bf16), (t_amps,), [pltpu.VMEM(t_amps.shape, bf16), dma(2 * npanels + rows // ROWS)], free_in=(0,), free_out=(0,), limit=VMEM_MOST)
     four = [jax.ShapeDtypeStruct((STEPS,) + part, bf16)] * STEPS
     lam_parts = call(pack_lam, four, (where, lambda_amps), scalars=1)
     amp_parts = exchange(amp_parts, PAIR)
@@ -286,28 +275,24 @@
         [pltpu.VMEM((npanels // 2,) + part, bf16)],
         scalars=1,
     )
-    brought = [pltpu.VMEM((npanels,) + part, bf16), dma(npanels // STEPS)]
+    matrix = jax.ShapeDtypeStruct((pairs, depth), bf16)
     sym = call(
         cross_kernel,
         jax.ShapeDtypeStruct((folded, LANES), f32),
-        (where, lam, amp_parts),
-        [
-            pltpu.VMEM((half, depth), bf16),
-            pltpu.VMEM((pairs, depth), bf16),
-            pltpu.VMEM((2, SQUARE, SQUARE), f32),
-            dma(1),
-        ],
+        (where, lam, call(all_panels, matrix, (amp_parts,))),
+        [pltpu.VMEM((2, SQUARE, SQUARE), f32)],
         scalars=1,
-        free_in=(1,),
-        limit=VMEM_LIMIT,
     )
     terms = exchange(sym.reshape(plane, own, LANES), PLANE)
-    terms = call(first_sum, jax.ShapeDtypeStruct((height, own, LANES), f32), (terms,))
-    terms = exchange(terms, LINE)
-    terms = call(second_sum, jax.ShapeDtypeStruct((plane, own, LANES), bf16), (where, terms), scalars=1)
-    later, _ = lax.optimization_barrier((amp_parts, terms))
+    terms = exchange(jnp.broadcast_to(jnp.sum(terms, axis=0), (height, own, LANES)), LINE)
+    halves = terms.reshape(2, height // 2, own, LANES).sum(axis=1)
+    mine = jnp.where(where[0] == 0, halves[0], halves[1])
+    total = jnp.where(where[3] == 1, halves[0] + halves[1], mine).astype(bf16)
+    terms = jnp.broadcast_to(total, (plane, own, LANES))
+    later, _ = lax.optimization_barrier((amp_parts, total))
     upper = exchange(terms, PLANE)
-    amp = call(amp_kernel, jax.ShapeDtypeStruct((pairs, depth), bf16), (later,), brought, free_in=(0,))
+    brought = [pltpu.VMEM((npanels,) + part, bf16), dma(npanels // STEPS)]
+    amp = call(amp_kernel, matrix, (later,), brought, free_in=(0,))
     result = call(
         density_kernel,
         jax.ShapeDtypeStruct((half, TILES, ROWS, LANES), bf16),

time: 281 us -> 279 us (level)
    unnamed x12 -> x6, local copies, waits for them, and re-layouts: 3.97 us -> 0.02 us
    pallas_call x10 -> x9, Pallas kernels: 19 us -> 18.5 us  [call(): pl.pallas_call(body, out_shape=out_shape, in_specs=[smem] * scalars + [fr...]
where the time goes in v7:
time: 279 us; the launch traced here: 278 us
  waiting for transfers between devices  159 us (57%)
  starting transfers between devices  58.1 us (21%)
  blocking collectives  39.7 us (14%)
  Pallas kernels  18.5 us (7%)
    ppermute x6, waiting for transfers between devices, shifts(): lax.ppermute(part, axis, [(k, k ^ s) for k in range(STEPS)])  133 us
    all_to_all x1, blocking collectives, exchange(): return lax.all_to_all(x, axis, split_axis=0, concat_axis=0, tiled=True)  39.7 us
    all_to_all x4, starting transfers between devices, exchange(): return lax.all_to_all(x, axis, split_axis=0, concat_axis=0, tiled=True)  38.7 us
    all_to_all x4, waiting for transfers between devices, exchange(): return lax.all_to_all(x, axis, split_axis=0, concat_axis=0, tiled=True)  25.6 us
    ppermute x6, starting transfers between devices, shifts(): lax.ppermute(part, axis, [(k, k ^ s) for k in range(STEPS)])  19.3 us
    pallas_call x9, Pallas kernels, call(): pl.pallas_call(body, out_shape=out_shape, in_specs=[smem] * scalars + [fr...  18.5 us
  transfers between devices with their start and end apart: 10, of which 9 were waited for; matrix products, arithmetic and copies ran while one was open for 0% of the time, Pallas kernels for 2%

profile of v7, /device:TPU:1, one launch (start us, length us, event | category | flops | bytes accessed | tf_op | source)
XLA Modules:
  0.0 278.1 jit_solution(17305761431347145403)
XLA Ops:
  0.0 3.3 %shard_map.49 = bf16[32,2,12,16,128]{4,3,2,1,0:T(8,128)(2,1)} custom-call(bf16[12,64,1024]{2,1,0:T(8,128)(2,1)} %amp_in.1), custom_call_target="tpu_custom_call" | custom-call | tf_op jit(solution)/shard_map/pallas_call | solution.py:34
  3.3 0.0 copy-start
  3.3 16.4 %all-to-all-start = ((bf16[32,2,12,16,128]{4,3,2,1,0:T(8,128)(2,1)}), bf16[32,2,12,16,128]{4,3,2,1,0:T(8,128)(2,1)}, u32[]{:S(2)}, u32[]{:S(2)}) async-start(bf16[32,2,12,16,128]{4,3,2,1,0:T(8,128)(2,1)} %shard_map.49), calls=%async_computation | async-start | bytes 6291456 | tf_op jit(solution)/shard_map/all_to_all | solution.py:237
  19.7 0.1 pad_add_fusion.where_ref
  19.8 0.0 copy-done
  19.8 1.0 shard_map.46
  20.7 3.1 %collective-permute-start = (bf16[4,2,12,16,128]{4,3,2,1,0:T(8,128)(2,1)S(1)}, bf16[4,2,12,16,128]{4,3,2,1,0:T(8,128)(2,1)S(1)}, u32[]{:S(2)}, u32[]{:S(2)}) collective-permute-start(bf16[4,2,12,16,128]{4,3,2,1,0:T(8,128)(2,1)S(1)} %get-tuple-element.15), channel_id=1, source_target_pairs={{0,16},{16,0},{32,48},{48,32},{1,17},{17,1},{33,49},{49,33},{2,18}... | collective-permute-start | bytes 1179656 | tf_op jit(solution)/shard_map/ppermute | solution.py:242
  23.8 4.3 %collective-permute-start.1 = (bf16[4,2,12,16,128]{4,3,2,1,0:T(8,128)(2,1)S(1)}, bf16[4,2,12,16,128]{4,3,2,1,0:T(8,128)(2,1)S(1)}, u32[]{:S(2)}, u32[]{:S(2)}) collective-permute-start(bf16[4,2,12,16,128]{4,3,2,1,0:T(8,128)(2,1)S(1)} %get-tuple-element.16), channel_id=1, source_target_pairs={{0,32},{16,48},{32,0},{48,16},{1,33},{17,49},{33,1},{49,17},{2,34}... | collective-permute-start | bytes 1179656 | tf_op jit(solution)/shard_map/ppermute | solution.py:242
  28.1 2.2 collective-permute-start.2
  30.3 12.4 %collective-permute-done.refs_1_ = bf16[4,2,12,16,128]{4,3,2,1,0:T(8,128)(2,1)S(1)} collective-permute-done((bf16[4,2,12,16,128]{4,3,2,1,0:T(8,128)(2,1)S(1)}, bf16[4,2,12,16,128]{4,3,2,1,0:T(8,128)(2,1)S(1)}, u32[]{:S(2)}, u32[]{:S(2)}) %collective-permute-start) | collective-permute-done | bytes 393248 | tf_op jit(solution)/shard_map/ppermute | solution.py:242
  42.7 9.1 %collective-permute-done.1.refs_2_ = bf16[4,2,12,16,128]{4,3,2,1,0:T(8,128)(2,1)S(1)} collective-permute-done((bf16[4,2,12,16,128]{4,3,2,1,0:T(8,128)(2,1)S(1)}, bf16[4,2,12,16,128]{4,3,2,1,0:T(8,128)(2,1)S(1)}, u32[]{:S(2)}, u32[]{:S(2)}) %collective-permute-start.1) | collective-permute-done | bytes 393248 | tf_op jit(solution)/shard_map/ppermute | solution.py:242
  51.9 6.6 %collective-permute-done.2.refs_3_ = bf16[4,2,12,16,128]{4,3,2,1,0:T(8,128)(2,1)S(1)} collective-permute-done((bf16[4,2,12,16,128]{4,3,2,1,0:T(8,128)(2,1)S(1)}, bf16[4,2,12,16,128]{4,3,2,1,0:T(8,128)(2,1)S(1)}, u32[]{:S(2)}, u32[]{:S(2)}) %collective-permute-start.2) | collective-permute-done | bytes 393248 | tf_op jit(solution)/shard_map/ppermute | solution.py:242
  58.5 0.6 shard_map.47
  59.2 3.8 %collective-permute-start.3 = (bf16[4,2,12,16,128]{4,3,2,1,0:T(8,128)(2,1)S(1)}, bf16[4,2,12,16,128]{4,3,2,1,0:T(8,128)(2,1)S(1)}, u32[]{:S(2)}, u32[]{:S(2)}) collective-permute-start(bf16[4,2,12,16,128]{4,3,2,1,0:T(8,128)(2,1)S(1)} %get-tuple-element.19), channel_id=1, source_target_pairs={{0,64},{64,0},{128,192},{192,128},{1,65},{65,1},{129,193},{193,129... | collective-permute-start | bytes 1179656 | tf_op jit(solution)/shard_map/ppermute | solution.py:242
  63.0 1.9 collective-permute-start.4
  64.9 4.0 %collective-permute-start.5 = (bf16[4,2,12,16,128]{4,3,2,1,0:T(8,128)(2,1)S(1)}, bf16[4,2,12,16,128]{4,3,2,1,0:T(8,128)(2,1)S(1)}, u32[]{:S(2)}, u32[]{:S(2)}) collective-permute-start(bf16[4,2,12,16,128]{4,3,2,1,0:T(8,128)(2,1)S(1)} %get-tuple-element.21), channel_id=1, source_target_pairs={{0,192},{64,128},{128,64},{192,0},{1,193},{65,129},{129,65},{193,1... | collective-permute-start | bytes 1179656 | tf_op jit(solution)/shard_map/ppermute | solution.py:242
  68.9 17.4 %collective-permute-done.3.refs_1_ = bf16[4,2,12,16,128]{4,3,2,1,0:T(8,128)(2,1)S(1)} collective-permute-done((bf16[4,2,12,16,128]{4,3,2,1,0:T(8,128)(2,1)S(1)}, bf16[4,2,12,16,128]{4,3,2,1,0:T(8,128)(2,1)S(1)}, u32[]{:S(2)}, u32[]{:S(2)}) %collective-permute-start.3) | collective-permute-done | bytes 393248 | tf_op jit(solution)/shard_map/ppermute | solution.py:242
  86.3 8.5 %collective-permute-done.4.refs_2_ = bf16[4,2,12,16,128]{4,3,2,1,0:T(8,128)(2,1)S(1)} collective-permute-done((bf16[4,2,12,16,128]{4,3,2,1,0:T(8,128)(2,1)S(1)}, bf16[4,2,12,16,128]{4,3,2,1,0:T(8,128)(2,1)S(1)}, u32[]{:S(2)}, u32[]{:S(2)}) %collective-permute-start.4) | collective-permute-done | bytes 393248 | tf_op jit(solution)/shard_map/ppermute | solution.py:242
  94.8 79.4 %collective-permute-done.5.refs_3_ = bf16[4,2,12,16,128]{4,3,2,1,0:T(8,128)(2,1)S(1)} collective-permute-done((bf16[4,2,12,16,128]{4,3,2,1,0:T(8,128)(2,1)S(1)}, bf16[4,2,12,16,128]{4,3,2,1,0:T(8,128)(2,1)S(1)}, u32[]{:S(2)}, u32[]{:S(2)}) %collective-permute-start.5) | collective-permute-done | bytes 393248 | tf_op jit(solution)/shard_map/ppermute | solution.py:242
  174.2 1.2 shard_map.48.lam_ref
  175.4 0.0 all-to-all-done.parts_ref.parts_in
  175.5 2.9 %shard_map.50.amp_ref = bf16[384,4096]{1,0:T(8,128)(2,1)S(1)} custom-call(bf16[32,2,12,16,128]{4,3,2,1,0:T(8,128)(2,1)} %all-to-all-done.parts_ref.parts_in), custom_call_target="tpu_custom_call" | custom-call | tf_op jit(solution)/shard_map/pallas_call | solution.py:34
  178.3 0.0 copy-start.1
  178.3 0.0 copy-start.2
  178.4 2.5 shard_map.51
  180.8 8.7 %all-to-all-start.1 = ((f32[32,16,128]{2,1,0:T(8,128)}), f32[32,16,128]{2,1,0:T(8,128)S(1)}, u32[]{:S(2)}, u32[]{:S(2)}) async-start(f32[32,16,128]{2,1,0:T(8,128)} %bitcast.4), calls=%async_computation.1 | async-start | bytes 524288 | tf_op jit(solution)/shard_map/all_to_all | solution.py:237
  189.5 0.0 copy-done.1
  189.6 8.9 %all-to-all-done.1 = f32[32,16,128]{2,1,0:T(8,128)S(1)} async-done(((f32[32,16,128]{2,1,0:T(8,128)}), f32[32,16,128]{2,1,0:T(8,128)S(1)}, u32[]{:S(2)}, u32[]{:S(2)}) %all-to-all-start.1) | async-done | bytes 262176 | tf_op jit(solution)/shard_map/all_to_all | solution.py:237
  198.5 0.7 broadcast_in_dim.4
  199.1 7.4 %all-to-all-start.2 = ((f32[16,16,128]{2,1,0:T(8,128)}), f32[16,16,128]{2,1,0:T(8,128)S(1)}, u32[]{:S(2)}, u32[]{:S(2)}) async-start(f32[16,16,128]{2,1,0:T(8,128)} %broadcast_in_dim.4), calls=%async_computation.2 | async-start | bytes 262144 | tf_op jit(solution)/shard_map/all_to_all | solution.py:237
  206.6 0.0 copy-done.2
  206.6 0.2 fusion
  206.8 0.2 fusion.1
  207.0 0.4 fusion.8
  207.4 0.1 copy.6
  207.5 12.5 %all-to-all-done.2 = f32[16,16,128]{2,1,0:T(8,128)S(1)} async-done(((f32[16,16,128]{2,1,0:T(8,128)}), f32[16,16,128]{2,1,0:T(8,128)S(1)}, u32[]{:S(2)}, u32[]{:S(2)}) %all-to-all-start.2) | async-done | bytes 131104 | tf_op jit(solution)/shard_map/all_to_all | solution.py:237
  220.0 0.7 broadcast_in_dim.5
  220.7 6.3 %all-to-all-start.3 = ((bf16[32,16,128]{2,1,0:T(8,128)(2,1)}), bf16[32,16,128]{2,1,0:T(8,128)(2,1)S(1)}, u32[]{:S(2)}, u32[]{:S(2)}) async-start(bf16[32,16,128]{2,1,0:T(8,128)(2,1)} %broadcast_in_dim.5), calls=%async_computation.3 | async-start | bytes 262144 | tf_op jit(solution)/shard_map/all_to_all | solution.py:237
  227.0 3.4 %shard_map.52.amp_ref = bf16[384,4096]{1,0:T(8,128)(2,1)S(1)} custom-call(bf16[32,2,12,16,128]{4,3,2,1,0:T(8,128)(2,1)} %all-to-all-done.parts_ref.parts_in), custom_call_target="tpu_custom_call" | custom-call | tf_op jit(solution)/shard_map/pallas_call | solution.py:34
  230.4 4.3 %all-to-all-done.3 = bf16[32,16,128]{2,1,0:T(8,128)(2,1)S(1)} async-done(((bf16[32,16,128]{2,1,0:T(8,128)(2,1)}), bf16[32,16,128]{2,1,0:T(8,128)(2,1)S(1)}, u32[]{:S(2)}, u32[]{:S(2)}) %all-to-all-start.3) | async-done | bytes 131104 | tf_op jit(solution)/shard_map/all_to_all | solution.py:237
  234.7 2.3 shard_map.53
  237.0 39.7 %all_to_all.25.parts_ref = bf16[16,12,2,16,128]{4,3,2,1,0:T(8,128)(2,1)S(1)} all-to-all(bf16[16,12,2,16,128]{4,3,2,1,0:T(8,128)(2,1)S(1)} %bitcast.17), channel_id=1, replica_groups=mesh['zb'=2,'z4'=4,'y'=4,'zh'=2,'x'=4,'c'=2] {'z4','y'}, dimensions={0} | all-to-all | bytes 3145728 | tf_op jit(solution)/shard_map/all_to_all | solution.py:237
  276.7 1.4 shard_map.54
  (5 shorter events, 0.1 us)
Async XLA Ops:
  3.3 16.5 %copy-start = (bf16[12,64,1024]{2,1,0:T(8,128)(2,1)S(1)}, bf16[12,64,1024]{2,1,0:T(8,128)(2,1)}, u32[]{:S(2)}) copy-start(bf16[12,64,1024]{2,1,0:T(8,128)(2,1)} %lam_ref.1) | copy-start | bytes 4718596
  3.3 172.1 %all-to-all-start = ((bf16[32,2,12,16,128]{4,3,2,1,0:T(8,128)(2,1)}), bf16[32,2,12,16,128]{4,3,2,1,0:T(8,128)(2,1)}, u32[]{:S(2)}, u32[]{:S(2)}) async-start(bf16[32,2,12,16,128]{4,3,2,1,0:T(8,128)(2,1)} %shard_map.49), calls=%async_computation | async-start | bytes 6291456 | tf_op jit(solution)/shard_map/all_to_all | solution.py:237
  20.7 22.0 %collective-permute-start = (bf16[4,2,12,16,128]{4,3,2,1,0:T(8,128)(2,1)S(1)}, bf16[4,2,12,16,128]{4,3,2,1,0:T(8,128)(2,1)S(1)}, u32[]{:S(2)}, u32[]{:S(2)}) collective-permute-start(bf16[4,2,12,16,128]{4,3,2,1,0:T(8,128)(2,1)S(1)} %get-tuple-element.15), channel_id=1, source_target_pairs={{0,16},{16,0},{32,48},{48,32},{1,17},{17,1},{33,49},{49,33},{2,18}... | collective-permute-start | bytes 1179656 | tf_op jit(solution)/shard_map/ppermute | solution.py:242
  23.8 28.1 %collective-permute-start.1 = (bf16[4,2,12,16,128]{4,3,2,1,0:T(8,128)(2,1)S(1)}, bf16[4,2,12,16,128]{4,3,2,1,0:T(8,128)(2,1)S(1)}, u32[]{:S(2)}, u32[]{:S(2)}) collective-permute-start(bf16[4,2,12,16,128]{4,3,2,1,0:T(8,128)(2,1)S(1)} %get-tuple-element.16), channel_id=1, source_target_pairs={{0,32},{16,48},{32,0},{48,16},{1,33},{17,49},{33,1},{49,17},{2,34}... | collective-permute-start | bytes 1179656 | tf_op jit(solution)/shard_map/ppermute | solution.py:242
  28.1 30.4 %collective-permute-start.2 = (bf16[4,2,12,16,128]{4,3,2,1,0:T(8,128)(2,1)S(1)}, bf16[4,2,12,16,128]{4,3,2,1,0:T(8,128)(2,1)S(1)}, u32[]{:S(2)}, u32[]{:S(2)}) collective-permute-start(bf16[4,2,12,16,128]{4,3,2,1,0:T(8,128)(2,1)S(1)} %get-tuple-element.17), channel_id=1, source_target_pairs={{0,48},{16,32},{32,16},{48,0},{1,49},{17,33},{33,17},{49,1},{2,50}... | collective-permute-start | bytes 1179656 | tf_op jit(solution)/shard_map/ppermute | solution.py:242
  59.2 27.2 %collective-permute-start.3 = (bf16[4,2,12,16,128]{4,3,2,1,0:T(8,128)(2,1)S(1)}, bf16[4,2,12,16,128]{4,3,2,1,0:T(8,128)(2,1)S(1)}, u32[]{:S(2)}, u32[]{:S(2)}) collective-permute-start(bf16[4,2,12,16,128]{4,3,2,1,0:T(8,128)(2,1)S(1)} %get-tuple-element.19), channel_id=1, source_target_pairs={{0,64},{64,0},{128,192},{192,128},{1,65},{65,1},{129,193},{193,129... | collective-permute-start | bytes 1179656 | tf_op jit(solution)/shard_map/ppermute | solution.py:242
  63.0 31.8 %collective-permute-start.4 = (bf16[4,2,12,16,128]{4,3,2,1,0:T(8,128)(2,1)S(1)}, bf16[4,2,12,16,128]{4,3,2,1,0:T(8,128)(2,1)S(1)}, u32[]{:S(2)}, u32[]{:S(2)}) collective-permute-start(bf16[4,2,12,16,128]{4,3,2,1,0:T(8,128)(2,1)S(1)} %get-tuple-element.20), channel_id=1, source_target_pairs={{0,128},{64,192},{128,0},{192,64},{1,129},{65,193},{129,1},{193,65... | collective-permute-start | bytes 1179656 | tf_op jit(solution)/shard_map/ppermute | solution.py:242
  64.9 109.3 %collective-permute-start.5 = (bf16[4,2,12,16,128]{4,3,2,1,0:T(8,128)(2,1)S(1)}, bf16[4,2,12,16,128]{4,3,2,1,0:T(8,128)(2,1)S(1)}, u32[]{:S(2)}, u32[]{:S(2)}) collective-permute-start(bf16[4,2,12,16,128]{4,3,2,1,0:T(8,128)(2,1)S(1)} %get-tuple-element.21), channel_id=1, source_target_pairs={{0,192},{64,128},{128,64},{192,0},{1,193},{65,129},{129,65},{193,1... | collective-permute-start | bytes 1179656 | tf_op jit(solution)/shard_map/ppermute | solution.py:242
  178.3 11.2 %copy-start.1 = (s32[264,2]{0,1:T(2,128)S(1)}, s32[264,2]{0,1:T(2,128)}, u32[]{:S(2)}) copy-start(s32[264,2]{0,1:T(2,128)} %param.7) | copy-start | bytes 6340
  178.3 28.2 %copy-start.2 = (s32[32]{0:T(128)S(1)}, s32[32]{0:T(128)}, u32[]{:S(2)}) copy-start(s32[32]{0:T(128)} %param.6) | copy-start | bytes 388
  180.8 17.6 %all-to-all-start.1 = ((f32[32,16,128]{2,1,0:T(8,128)}), f32[32,16,128]{2,1,0:T(8,128)S(1)}, u32[]{:S(2)}, u32[]{:S(2)}) async-start(f32[32,16,128]{2,1,0:T(8,128)} %bitcast.4), calls=%async_computation.1 | async-start | bytes 524288 | tf_op jit(solution)/shard_map/all_to_all | solution.py:237
  199.1 20.8 %all-to-all-start.2 = ((f32[16,16,128]{2,1,0:T(8,128)}), f32[16,16,128]{2,1,0:T(8,128)S(1)}, u32[]{:S(2)}, u32[]{:S(2)}) async-start(f32[16,16,128]{2,1,0:T(8,128)} %broadcast_in_dim.4), calls=%async_computation.2 | async-start | bytes 262144 | tf_op jit(solution)/shard_map/all_to_all | solution.py:237
  220.7 14.0 %all-to-all-start.3 = ((bf16[32,16,128]{2,1,0:T(8,128)(2,1)}), bf16[32,16,128]{2,1,0:T(8,128)(2,1)S(1)}, u32[]{:S(2)}, u32[]{:S(2)}) async-start(bf16[32,16,128]{2,1,0:T(8,128)(2,1)} %broadcast_in_dim.5), calls=%async_computation.3 | async-start | bytes 262144 | tf_op jit(solution)/shard_map/all_to_all | solution.py:237

commit v8 on v7

--- a/solution.py
+++ b/solution.py
@@ -145,12 +145,24 @@
     return jnp.concatenate([x, pltpu.roll(x, LANES // 2, 1)], axis=0)
 
 
-def amp_kernel(parts_in, amp_ref, parts_ref, sems):
+def amp_kernel(where_ref, parts_in, listed_ref, amp_ref, mask_ref, parts_ref, sems):
     copies = []
     for step in range(parts_ref.shape[0] // STEPS):
         some = pl.ds(step * STEPS, STEPS)
         copies.append(pltpu.make_async_copy(parts_in.at[some], parts_ref.at[some], sems.at[step]))
         copies[-1].start()
+    half, pairs = mask_ref.shape
+    panels = listed_ref.shape[0]
+    panel_size = pairs // panels
+    zb = where_ref[0]
+
+    def spread(first_row, rows):
+        row = first_row + lax.broadcasted_iota(jnp.int32, (rows, panels), 0)
+        first = lax.broadcasted_iota(jnp.int32, (rows, panels), 1) * panel_size
+        return ((row >= first) & (row < first + panel_size)).astype(jnp.float32)
+
+    mask = jnp.dot(spread(zb * half, half), listed_ref[...], preferred_element_type=jnp.float32)
+    mask_ref[...] = lax.dot_general(mask, spread(0, pairs), (((1,), (1,)), ((), ())), preferred_element_type=jnp.float32)
     all_panels(parts_ref, amp_ref, lambda step: copies[step].wait())
 
 
@@ -178,21 +190,10 @@
         at += rows.shape[0]
 
 
-def density_kernel(where_ref, sym_ref, listed_ref, amp_ref, out_ref, square_ref, inter_ref, flat_ref):
+def density_kernel(where_ref, sym_ref, mask_ref, amp_ref, out_ref, square_ref, inter_ref, flat_ref):
     pairs, depth = amp_ref.shape
     half = flat_ref.shape[0]
-    panels = listed_ref.shape[0]
-    panel_size = pairs // panels
     zb = where_ref[0]
-
-    def spread(first_row, rows):
-        row = first_row + lax.broadcasted_iota(jnp.int32, (rows, panels), 0)
-        first = lax.broadcasted_iota(jnp.int32, (rows, panels), 1) * panel_size
-        return ((row >= first) & (row < first + panel_size)).astype(jnp.float32)
-
-    mask = jnp.dot(spread(zb * half, half), listed_ref[...], preferred_element_type=jnp.float32)
-    mask = lax.dot_general(mask, spread(0, pairs), (((1,), (1,)), ((), ())), preferred_element_type=jnp.float32)
-
     sizes = [half, half // 2, LANES, LANES // 2, (half - LANES) // 2]
     ends = [sum(sizes[: n + 1]) for n in range(len(sizes))]
     x, x_right, w, w_right, w_last = (sym_ref[e - n : e].astype(jnp.float32) for e, n in zip(ends, sizes))
@@ -214,7 +215,7 @@
         (left[:, :LANES], jnp.where(keep, left[:, LANES:], turned[0]), jnp.where(keep, turned[0], turned[1]))
     ):
         cols = slice(n * LANES, (n + 1) * LANES)
-        inter_ref[:, cols] = (block * mask[:, cols]).astype(jnp.bfloat16)
+        inter_ref[:, cols] = (block * mask_ref[:, cols]).astype(jnp.bfloat16)
     own = inter_ref[...]
     for c in range(depth // WIDE):
         flat_ref[:, c * WIDE : (c + 1) * WIDE] = jnp.dot(
@@ -292,11 +293,12 @@
     later, _ = lax.optimization_barrier((amp_parts, total))
     upper = exchange(terms, PLANE)
     brought = [pltpu.VMEM((npanels,) + part, bf16), dma(npanels // STEPS)]
-    amp = call(amp_kernel, matrix, (later,), brought, free_in=(0,))
+    mask = jax.ShapeDtypeStruct((half, pairs), f32)
+    amp, mask = call(amp_kernel, [matrix, mask], (where, later, listed), brought, scalars=1, free_in=(1,))
     result = call(
         density_kernel,
         jax.ShapeDtypeStruct((half, TILES, ROWS, LANES), bf16),
-        (where, upper.reshape(folded, LANES), listed, amp),
+        (where, upper.reshape(folded, LANES), mask, amp),
         [pltpu.VMEM((SQUARE, SQUARE), f32), pltpu.VMEM((half, pairs), bf16), pltpu.VMEM((half, depth), bf16)],
         scalars=1,
     )

time: 279 us -> 280 us (level)
  no operation moved by 1% of the time
where the time goes in v8:
time: 280 us; the launch traced here: 279 us
  waiting for transfers between devices  158 us (56%)
  starting transfers between devices  58 us (21%)
  blocking collectives  39.7 us (14%)
  Pallas kernels  19.1 us (7%)
  local copies, waits for them, and re-layouts  3.1 us (1%)
    ppermute x6, waiting for transfers between devices, shifts(): lax.ppermute(part, axis, [(k, k ^ s) for k in range(STEPS)])  133 us
    all_to_all x1, blocking collectives, exchange(): return lax.all_to_all(x, axis, split_axis=0, concat_axis=0, tiled=True)  39.7 us
    all_to_all x4, starting transfers between devices, exchange(): return lax.all_to_all(x, axis, split_axis=0, concat_axis=0, tiled=True)  38.7 us
    all_to_all x4, waiting for transfers between devices, exchange(): return lax.all_to_all(x, axis, split_axis=0, concat_axis=0, tiled=True)  24.4 us
    ppermute x6, starting transfers between devices, shifts(): lax.ppermute(part, axis, [(k, k ^ s) for k in range(STEPS)])  19.3 us
    pallas_call x9, Pallas kernels, call(): pl.pallas_call(body, out_shape=out_shape, in_specs=[smem] * scalars + [fr...  19.1 us
  transfers between devices with their start and end apart: 10, of which 9 were waited for; matrix products, arithmetic and copies ran while one was open for 0% of the time, Pallas kernels for 2%

profile of v8, /device:TPU:1, one launch (start us, length us, event | category | flops | bytes accessed | tf_op | source)
XLA Modules:
  0.0 279.0 jit_solution(1347908246593074348)
XLA Ops:
  0.0 3.3 %shard_map.49 = bf16[32,2,12,16,128]{4,3,2,1,0:T(8,128)(2,1)} custom-call(bf16[12,64,1024]{2,1,0:T(8,128)(2,1)} %amp_in.1), custom_call_target="tpu_custom_call" | custom-call | tf_op jit(solution)/shard_map/pallas_call | solution.py:34
  3.3 0.0 copy-start
  3.3 16.4 %all-to-all-start = ((bf16[32,2,12,16,128]{4,3,2,1,0:T(8,128)(2,1)}), bf16[32,2,12,16,128]{4,3,2,1,0:T(8,128)(2,1)}, u32[]{:S(2)}, u32[]{:S(2)}) async-start(bf16[32,2,12,16,128]{4,3,2,1,0:T(8,128)(2,1)} %shard_map.49), calls=%async_computation | async-start | bytes 6291456 | tf_op jit(solution)/shard_map/all_to_all | solution.py:238
  19.7 0.1 pad_add_fusion.where_ref
  19.7 0.0 copy-done
  19.7 1.0 shard_map.46
  20.7 3.1 %collective-permute-start = (bf16[4,2,12,16,128]{4,3,2,1,0:T(8,128)(2,1)S(1)}, bf16[4,2,12,16,128]{4,3,2,1,0:T(8,128)(2,1)S(1)}, u32[]{:S(2)}, u32[]{:S(2)}) collective-permute-start(bf16[4,2,12,16,128]{4,3,2,1,0:T(8,128)(2,1)S(1)} %get-tuple-element.17), channel_id=1, source_target_pairs={{0,16},{16,0},{32,48},{48,32},{1,17},{17,1},{33,49},{49,33},{2,18}... | collective-permute-start | bytes 1179656 | tf_op jit(solution)/shard_map/ppermute | solution.py:243
  23.8 4.3 %collective-permute-start.1 = (bf16[4,2,12,16,128]{4,3,2,1,0:T(8,128)(2,1)S(1)}, bf16[4,2,12,16,128]{4,3,2,1,0:T(8,128)(2,1)S(1)}, u32[]{:S(2)}, u32[]{:S(2)}) collective-permute-start(bf16[4,2,12,16,128]{4,3,2,1,0:T(8,128)(2,1)S(1)} %get-tuple-element.18), channel_id=1, source_target_pairs={{0,32},{16,48},{32,0},{48,16},{1,33},{17,49},{33,1},{49,17},{2,34}... | collective-permute-start | bytes 1179656 | tf_op jit(solution)/shard_map/ppermute | solution.py:243
  28.1 2.2 collective-permute-start.2
  30.3 12.4 %collective-permute-done.refs_1_ = bf16[4,2,12,16,128]{4,3,2,1,0:T(8,128)(2,1)S(1)} collective-permute-done((bf16[4,2,12,16,128]{4,3,2,1,0:T(8,128)(2,1)S(1)}, bf16[4,2,12,16,128]{4,3,2,1,0:T(8,128)(2,1)S(1)}, u32[]{:S(2)}, u32[]{:S(2)}) %collective-permute-start) | collective-permute-done | bytes 393248 | tf_op jit(solution)/shard_map/ppermute | solution.py:243
  42.7 9.1 %collective-permute-done.1.refs_2_ = bf16[4,2,12,16,128]{4,3,2,1,0:T(8,128)(2,1)S(1)} collective-permute-done((bf16[4,2,12,16,128]{4,3,2,1,0:T(8,128)(2,1)S(1)}, bf16[4,2,12,16,128]{4,3,2,1,0:T(8,128)(2,1)S(1)}, u32[]{:S(2)}, u32[]{:S(2)}) %collective-permute-start.1) | collective-permute-done | bytes 393248 | tf_op jit(solution)/shard_map/ppermute | solution.py:243
  51.9 6.6 %collective-permute-done.2.refs_3_ = bf16[4,2,12,16,128]{4,3,2,1,0:T(8,128)(2,1)S(1)} collective-permute-done((bf16[4,2,12,16,128]{4,3,2,1,0:T(8,128)(2,1)S(1)}, bf16[4,2,12,16,128]{4,3,2,1,0:T(8,128)(2,1)S(1)}, u32[]{:S(2)}, u32[]{:S(2)}) %collective-permute-start.2) | collective-permute-done | bytes 393248 | tf_op jit(solution)/shard_map/ppermute | solution.py:243
  58.5 0.6 shard_map.47
  59.2 3.8 %collective-permute-start.3 = (bf16[4,2,12,16,128]{4,3,2,1,0:T(8,128)(2,1)S(1)}, bf16[4,2,12,16,128]{4,3,2,1,0:T(8,128)(2,1)S(1)}, u32[]{:S(2)}, u32[]{:S(2)}) collective-permute-start(bf16[4,2,12,16,128]{4,3,2,1,0:T(8,128)(2,1)S(1)} %get-tuple-element.21), channel_id=1, source_target_pairs={{0,64},{64,0},{128,192},{192,128},{1,65},{65,1},{129,193},{193,129... | collective-permute-start | bytes 1179656 | tf_op jit(solution)/shard_map/ppermute | solution.py:243
  63.0 1.9 collective-permute-start.4
  64.9 4.0 %collective-permute-start.5 = (bf16[4,2,12,16,128]{4,3,2,1,0:T(8,128)(2,1)S(1)}, bf16[4,2,12,16,128]{4,3,2,1,0:T(8,128)(2,1)S(1)}, u32[]{:S(2)}, u32[]{:S(2)}) collective-permute-start(bf16[4,2,12,16,128]{4,3,2,1,0:T(8,128)(2,1)S(1)} %get-tuple-element.23), channel_id=1, source_target_pairs={{0,192},{64,128},{128,64},{192,0},{1,193},{65,129},{129,65},{193,1... | collective-permute-start | bytes 1179656 | tf_op jit(solution)/shard_map/ppermute | solution.py:243
  68.9 17.4 %collective-permute-done.3.refs_1_ = bf16[4,2,12,16,128]{4,3,2,1,0:T(8,128)(2,1)S(1)} collective-permute-done((bf16[4,2,12,16,128]{4,3,2,1,0:T(8,128)(2,1)S(1)}, bf16[4,2,12,16,128]{4,3,2,1,0:T(8,128)(2,1)S(1)}, u32[]{:S(2)}, u32[]{:S(2)}) %collective-permute-start.3) | collective-permute-done | bytes 393248 | tf_op jit(solution)/shard_map/ppermute | solution.py:243
  86.3 8.5 %collective-permute-done.4.refs_2_ = bf16[4,2,12,16,128]{4,3,2,1,0:T(8,128)(2,1)S(1)} collective-permute-done((bf16[4,2,12,16,128]{4,3,2,1,0:T(8,128)(2,1)S(1)}, bf16[4,2,12,16,128]{4,3,2,1,0:T(8,128)(2,1)S(1)}, u32[]{:S(2)}, u32[]{:S(2)}) %collective-permute-start.4) | collective-permute-done | bytes 393248 | tf_op jit(solution)/shard_map/ppermute | solution.py:243
  94.8 79.4 %collective-permute-done.5.refs_3_ = bf16[4,2,12,16,128]{4,3,2,1,0:T(8,128)(2,1)S(1)} collective-permute-done((bf16[4,2,12,16,128]{4,3,2,1,0:T(8,128)(2,1)S(1)}, bf16[4,2,12,16,128]{4,3,2,1,0:T(8,128)(2,1)S(1)}, u32[]{:S(2)}, u32[]{:S(2)}) %collective-permute-start.5) | collective-permute-done | bytes 393248 | tf_op jit(solution)/shard_map/ppermute | solution.py:243
  174.2 1.2 shard_map.48.lam_ref
  175.4 0.0 all-to-all-done.parts_ref.parts_in
  175.4 2.9 %shard_map.50.amp_ref = bf16[384,4096]{1,0:T(8,128)(2,1)S(1)} custom-call(bf16[32,2,12,16,128]{4,3,2,1,0:T(8,128)(2,1)} %all-to-all-done.parts_ref.parts_in), custom_call_target="tpu_custom_call" | custom-call | tf_op jit(solution)/shard_map/pallas_call | solution.py:34
  178.3 0.0 copy-start.3
  178.3 0.0 copy-start.4
  178.3 2.5 shard_map.51
  180.8 8.7 %all-to-all-start.1 = ((f32[32,16,128]{2,1,0:T(8,128)}), f32[32,16,128]{2,1,0:T(8,128)S(1)}, u32[]{:S(2)}, u32[]{:S(2)}) async-start(f32[32,16,128]{2,1,0:T(8,128)} %bitcast.4), calls=%async_computation.1 | async-start | bytes 524288 | tf_op jit(solution)/shard_map/all_to_all | solution.py:238
  189.5 0.0 copy-done.3
  189.5 8.9 %all-to-all-done.1 = f32[32,16,128]{2,1,0:T(8,128)S(1)} async-done(((f32[32,16,128]{2,1,0:T(8,128)}), f32[32,16,128]{2,1,0:T(8,128)S(1)}, u32[]{:S(2)}, u32[]{:S(2)}) %all-to-all-start.1) | async-done | bytes 262176 | tf_op jit(solution)/shard_map/all_to_all | solution.py:238
  198.5 0.7 broadcast_in_dim.4
  199.1 7.4 %all-to-all-start.2 = ((f32[16,16,128]{2,1,0:T(8,128)}), f32[16,16,128]{2,1,0:T(8,128)S(1)}, u32[]{:S(2)}, u32[]{:S(2)}) async-start(f32[16,16,128]{2,1,0:T(8,128)} %broadcast_in_dim.4), calls=%async_computation.2 | async-start | bytes 262144 | tf_op jit(solution)/shard_map/all_to_all | solution.py:238
  206.5 0.0 copy-done.4
  206.5 0.2 fusion
  206.8 0.2 fusion.1
  207.0 0.4 fusion.8
  207.4 0.1 copy.6
  207.5 12.5 %all-to-all-done.2 = f32[16,16,128]{2,1,0:T(8,128)S(1)} async-done(((f32[16,16,128]{2,1,0:T(8,128)}), f32[16,16,128]{2,1,0:T(8,128)S(1)}, u32[]{:S(2)}, u32[]{:S(2)}) %all-to-all-start.2) | async-done | bytes 131104 | tf_op jit(solution)/shard_map/all_to_all | solution.py:238
  220.0 0.7 broadcast_in_dim.5
  220.7 6.3 %all-to-all-start.3 = ((bf16[32,16,128]{2,1,0:T(8,128)(2,1)}), bf16[32,16,128]{2,1,0:T(8,128)(2,1)S(1)}, u32[]{:S(2)}, u32[]{:S(2)}) async-start(bf16[32,16,128]{2,1,0:T(8,128)(2,1)} %broadcast_in_dim.5), calls=%async_computation.3 | async-start | bytes 262144 | tf_op jit(solution)/shard_map/all_to_all | solution.py:238
  227.0 3.9 %shard_map.52 = (bf16[384,4096]{1,0:T(8,128)(2,1)S(1)}, f32[192,384]{1,0:T(8,128)S(1)}) custom-call(s32[4]{0:T(128)S(1)} %pad_add_fusion.where_ref, bf16[32,2,12,16,128]{4,3,2,1,0:T(8,128)(2,1)} %all-to-all-done.parts_ref.parts_in, f32[32,32]{1,0:T(8,128)S(1)} %fusion.4.listed_ref), custom_call_target="tpu_custom_call" | custom-call | tf_op jit(solution)/shard_map/pallas_call | solution.py:34
  230.9 0.0 copy-start.1
  230.9 0.7 copy-done.1
  231.6 3.1 %all-to-all-done.3 = bf16[32,16,128]{2,1,0:T(8,128)(2,1)S(1)} async-done(((bf16[32,16,128]{2,1,0:T(8,128)(2,1)}), bf16[32,16,128]{2,1,0:T(8,128)(2,1)S(1)}, u32[]{:S(2)}, u32[]{:S(2)}) %all-to-all-start.3) | async-done | bytes 131104 | tf_op jit(solution)/shard_map/all_to_all | solution.py:238
  234.7 0.0 copy-start.2
  234.7 1.0 copy-done.2
  235.6 2.3 shard_map.53
  237.9 39.7 %all_to_all.25.parts_ref = bf16[16,12,2,16,128]{4,3,2,1,0:T(8,128)(2,1)S(1)} all-to-all(bf16[16,12,2,16,128]{4,3,2,1,0:T(8,128)(2,1)S(1)} %bitcast.17), channel_id=1, replica_groups=mesh['zb'=2,'z4'=4,'y'=4,'zh'=2,'x'=4,'c'=2] {'z4','y'}, dimensions={0} | all-to-all | bytes 3145728 | tf_op jit(solution)/shard_map/all_to_all | solution.py:238
  277.6 1.4 shard_map.54
  (5 shorter events, 0.1 us)
Async XLA Ops:
  3.3 16.5 %copy-start = (bf16[12,64,1024]{2,1,0:T(8,128)(2,1)S(1)}, bf16[12,64,1024]{2,1,0:T(8,128)(2,1)}, u32[]{:S(2)}) copy-start(bf16[12,64,1024]{2,1,0:T(8,128)(2,1)} %lam_ref.1) | copy-start | bytes 4718596
  3.3 172.1 %all-to-all-start = ((bf16[32,2,12,16,128]{4,3,2,1,0:T(8,128)(2,1)}), bf16[32,2,12,16,128]{4,3,2,1,0:T(8,128)(2,1)}, u32[]{:S(2)}, u32[]{:S(2)}) async-start(bf16[32,2,12,16,128]{4,3,2,1,0:T(8,128)(2,1)} %shard_map.49), calls=%async_computation | async-start | bytes 6291456 | tf_op jit(solution)/shard_map/all_to_all | solution.py:238
  20.7 22.0 %collective-permute-start = (bf16[4,2,12,16,128]{4,3,2,1,0:T(8,128)(2,1)S(1)}, bf16[4,2,12,16,128]{4,3,2,1,0:T(8,128)(2,1)S(1)}, u32[]{:S(2)}, u32[]{:S(2)}) collective-permute-start(bf16[4,2,12,16,128]{4,3,2,1,0:T(8,128)(2,1)S(1)} %get-tuple-element.17), channel_id=1, source_target_pairs={{0,16},{16,0},{32,48},{48,32},{1,17},{17,1},{33,49},{49,33},{2,18}... | collective-permute-start | bytes 1179656 | tf_op jit(solution)/shard_map/ppermute | solution.py:243
  23.8 28.1 %collective-permute-start.1 = (bf16[4,2,12,16,128]{4,3,2,1,0:T(8,128)(2,1)S(1)}, bf16[4,2,12,16,128]{4,3,2,1,0:T(8,128)(2,1)S(1)}, u32[]{:S(2)}, u32[]{:S(2)}) collective-permute-start(bf16[4,2,12,16,128]{4,3,2,1,0:T(8,128)(2,1)S(1)} %get-tuple-element.18), channel_id=1, source_target_pairs={{0,32},{16,48},{32,0},{48,16},{1,33},{17,49},{33,1},{49,17},{2,34}... | collective-permute-start | bytes 1179656 | tf_op jit(solution)/shard_map/ppermute | solution.py:243
  28.1 30.4 %collective-permute-start.2 = (bf16[4,2,12,16,128]{4,3,2,1,0:T(8,128)(2,1)S(1)}, bf16[4,2,12,16,128]{4,3,2,1,0:T(8,128)(2,1)S(1)}, u32[]{:S(2)}, u32[]{:S(2)}) collective-permute-start(bf16[4,2,12,16,128]{4,3,2,1,0:T(8,128)(2,1)S(1)} %get-tuple-element.19), channel_id=1, source_target_pairs={{0,48},{16,32},{32,16},{48,0},{1,49},{17,33},{33,17},{49,1},{2,50}... | collective-permute-start | bytes 1179656 | tf_op jit(solution)/shard_map/ppermute | solution.py:243
  59.2 27.2 %collective-permute-start.3 = (bf16[4,2,12,16,128]{4,3,2,1,0:T(8,128)(2,1)S(1)}, bf16[4,2,12,16,128]{4,3,2,1,0:T(8,128)(2,1)S(1)}, u32[]{:S(2)}, u32[]{:S(2)}) collective-permute-start(bf16[4,2,12,16,128]{4,3,2,1,0:T(8,128)(2,1)S(1)} %get-tuple-element.21), channel_id=1, source_target_pairs={{0,64},{64,0},{128,192},{192,128},{1,65},{65,1},{129,193},{193,129... | collective-permute-start | bytes 1179656 | tf_op jit(solution)/shard_map/ppermute | solution.py:243
  63.0 31.8 %collective-permute-start.4 = (bf16[4,2,12,16,128]{4,3,2,1,0:T(8,128)(2,1)S(1)}, bf16[4,2,12,16,128]{4,3,2,1,0:T(8,128)(2,1)S(1)}, u32[]{:S(2)}, u32[]{:S(2)}) collective-permute-start(bf16[4,2,12,16,128]{4,3,2,1,0:T(8,128)(2,1)S(1)} %get-tuple-element.22), channel_id=1, source_target_pairs={{0,128},{64,192},{128,0},{192,64},{1,129},{65,193},{129,1},{193,65... | collective-permute-start | bytes 1179656 | tf_op jit(solution)/shard_map/ppermute | solution.py:243
  64.9 109.3 %collective-permute-start.5 = (bf16[4,2,12,16,128]{4,3,2,1,0:T(8,128)(2,1)S(1)}, bf16[4,2,12,16,128]{4,3,2,1,0:T(8,128)(2,1)S(1)}, u32[]{:S(2)}, u32[]{:S(2)}) collective-permute-start(bf16[4,2,12,16,128]{4,3,2,1,0:T(8,128)(2,1)S(1)} %get-tuple-element.23), channel_id=1, source_target_pairs={{0,192},{64,128},{128,64},{192,0},{1,193},{65,129},{129,65},{193,1... | collective-permute-start | bytes 1179656 | tf_op jit(solution)/shard_map/ppermute | solution.py:243
  178.3 11.2 %copy-start.3 = (s32[264,2]{0,1:T(2,128)S(1)}, s32[264,2]{0,1:T(2,128)}, u32[]{:S(2)}) copy-start(s32[264,2]{0,1:T(2,128)} %param.7) | copy-start | bytes 6340
  178.3 28.2 %copy-start.4 = (s32[32]{0:T(128)S(1)}, s32[32]{0:T(128)}, u32[]{:S(2)}) copy-start(s32[32]{0:T(128)} %param.6) | copy-start | bytes 388
  180.8 17.6 %all-to-all-start.1 = ((f32[32,16,128]{2,1,0:T(8,128)}), f32[32,16,128]{2,1,0:T(8,128)S(1)}, u32[]{:S(2)}, u32[]{:S(2)}) async-start(f32[32,16,128]{2,1,0:T(8,128)} %bitcast.4), calls=%async_computation.1 | async-start | bytes 524288 | tf_op jit(solution)/shard_map/all_to_all | solution.py:238
  199.1 20.8 %all-to-all-start.2 = ((f32[16,16,128]{2,1,0:T(8,128)}), f32[16,16,128]{2,1,0:T(8,128)S(1)}, u32[]{:S(2)}, u32[]{:S(2)}) async-start(f32[16,16,128]{2,1,0:T(8,128)} %broadcast_in_dim.4), calls=%async_computation.2 | async-start | bytes 262144 | tf_op jit(solution)/shard_map/all_to_all | solution.py:238
  220.7 14.0 %all-to-all-start.3 = ((bf16[32,16,128]{2,1,0:T(8,128)(2,1)}), bf16[32,16,128]{2,1,0:T(8,128)(2,1)S(1)}, u32[]{:S(2)}, u32[]{:S(2)}) async-start(bf16[32,16,128]{2,1,0:T(8,128)(2,1)} %broadcast_in_dim.5), calls=%async_computation.3 | async-start | bytes 262144 | tf_op jit(solution)/shard_map/all_to_all | solution.py:238
  230.9 0.7 copy-start.1
  234.7 1.0 copy-start.2

commit v9 on v7

--- a/solution.py
+++ b/solution.py
@@ -8,8 +8,8 @@
 HALF = ("z4", "y")
 PAIR = ("zb",) + HALF
 VIRT = ("zh", "x", "c")
-PLANE = ("y", "x", "c")
-LINE = ("zb", "z4", "zh")
+PLANE = ("c", "y", "x")
+LINE = ("zh", "zb", "z4")
 
 ROWS = 16
 LANES = 128
@@ -285,7 +285,7 @@
     )
     terms = exchange(sym.reshape(plane, own, LANES), PLANE)
     terms = exchange(jnp.broadcast_to(jnp.sum(terms, axis=0), (height, own, LANES)), LINE)
-    halves = terms.reshape(2, height // 2, own, LANES).sum(axis=1)
+    halves = terms.reshape(2, 2, height // 4, own, LANES).sum(axis=(0, 2))
     mine = jnp.where(where[0] == 0, halves[0], halves[1])
     total = jnp.where(where[3] == 1, halves[0] + halves[1], mine).astype(bf16)
     terms = jnp.broadcast_to(total, (plane, own, LANES))

time: 279 us -> 278 us (level)
  no operation moved by 1% of the time
where the time goes in v9:
time: 278 us; the launch traced here: 277 us
  waiting for transfers between devices  157 us (56%)
  starting transfers between devices  59.2 us (21%)
  blocking collectives  39.9 us (14%)
  Pallas kernels  18.5 us (7%)
    ppermute x6, waiting for transfers between devices, shifts(): lax.ppermute(part, axis, [(k, k ^ s) for k in range(STEPS)])  133 us
    all_to_all x1, blocking collectives, exchange(): return lax.all_to_all(x, axis, split_axis=0, concat_axis=0, tiled=True)  39.9 us
    all_to_all x4, starting transfers between devices, exchange(): return lax.all_to_all(x, axis, split_axis=0, concat_axis=0, tiled=True)  39.8 us
    all_to_all x4, waiting for transfers between devices, exchange(): return lax.all_to_all(x, axis, split_axis=0, concat_axis=0, tiled=True)  23.4 us
    ppermute x6, starting transfers between devices, shifts(): lax.ppermute(part, axis, [(k, k ^ s) for k in range(STEPS)])  19.3 us
    pallas_call x9, Pallas kernels, call(): pl.pallas_call(body, out_shape=out_shape, in_specs=[smem] * scalars + [fr...  18.5 us
  transfers between devices with their start and end apart: 10, of which 9 were waited for; matrix products, arithmetic and copies ran while one was open for 0% of the time, Pallas kernels for 2%

profile of v9, /device:TPU:1, one launch (start us, length us, event | category | flops | bytes accessed | tf_op | source)
XLA Modules:
  0.0 277.1 jit_solution(5433097455465892137)
XLA Ops:
  0.0 3.3 %shard_map.49 = bf16[32,2,12,16,128]{4,3,2,1,0:T(8,128)(2,1)} custom-call(bf16[12,64,1024]{2,1,0:T(8,128)(2,1)} %amp_in.1), custom_call_target="tpu_custom_call" | custom-call | tf_op jit(solution)/shard_map/pallas_call | solution.py:34
  3.3 0.0 copy-start
  3.3 16.4 %all-to-all-start = ((bf16[32,2,12,16,128]{4,3,2,1,0:T(8,128)(2,1)}), bf16[32,2,12,16,128]{4,3,2,1,0:T(8,128)(2,1)}, u32[]{:S(2)}, u32[]{:S(2)}) async-start(bf16[32,2,12,16,128]{4,3,2,1,0:T(8,128)(2,1)} %shard_map.49), calls=%async_computation | async-start | bytes 6291456 | tf_op jit(solution)/shard_map/all_to_all | solution.py:237
  19.7 0.1 pad_add_fusion.where_ref
  19.8 0.0 copy-done
  19.8 1.0 shard_map.46
  20.7 3.1 %collective-permute-start = (bf16[4,2,12,16,128]{4,3,2,1,0:T(8,128)(2,1)S(1)}, bf16[4,2,12,16,128]{4,3,2,1,0:T(8,128)(2,1)S(1)}, u32[]{:S(2)}, u32[]{:S(2)}) collective-permute-start(bf16[4,2,12,16,128]{4,3,2,1,0:T(8,128)(2,1)S(1)} %get-tuple-element.15), channel_id=1, source_target_pairs={{0,16},{16,0},{32,48},{48,32},{1,17},{17,1},{33,49},{49,33},{2,18}... | collective-permute-start | bytes 1179656 | tf_op jit(solution)/shard_map/ppermute | solution.py:242
  23.8 4.3 %collective-permute-start.1 = (bf16[4,2,12,16,128]{4,3,2,1,0:T(8,128)(2,1)S(1)}, bf16[4,2,12,16,128]{4,3,2,1,0:T(8,128)(2,1)S(1)}, u32[]{:S(2)}, u32[]{:S(2)}) collective-permute-start(bf16[4,2,12,16,128]{4,3,2,1,0:T(8,128)(2,1)S(1)} %get-tuple-element.16), channel_id=1, source_target_pairs={{0,32},{16,48},{32,0},{48,16},{1,33},{17,49},{33,1},{49,17},{2,34}... | collective-permute-start | bytes 1179656 | tf_op jit(solution)/shard_map/ppermute | solution.py:242
  28.1 2.2 collective-permute-start.2
  30.3 12.4 %collective-permute-done.refs_1_ = bf16[4,2,12,16,128]{4,3,2,1,0:T(8,128)(2,1)S(1)} collective-permute-done((bf16[4,2,12,16,128]{4,3,2,1,0:T(8,128)(2,1)S(1)}, bf16[4,2,12,16,128]{4,3,2,1,0:T(8,128)(2,1)S(1)}, u32[]{:S(2)}, u32[]{:S(2)}) %collective-permute-start) | collective-permute-done | bytes 393248 | tf_op jit(solution)/shard_map/ppermute | solution.py:242
  42.7 9.1 %collective-permute-done.1.refs_2_ = bf16[4,2,12,16,128]{4,3,2,1,0:T(8,128)(2,1)S(1)} collective-permute-done((bf16[4,2,12,16,128]{4,3,2,1,0:T(8,128)(2,1)S(1)}, bf16[4,2,12,16,128]{4,3,2,1,0:T(8,128)(2,1)S(1)}, u32[]{:S(2)}, u32[]{:S(2)}) %collective-permute-start.1) | collective-permute-done | bytes 393248 | tf_op jit(solution)/shard_map/ppermute | solution.py:242
  51.9 6.6 %collective-permute-done.2.refs_3_ = bf16[4,2,12,16,128]{4,3,2,1,0:T(8,128)(2,1)S(1)} collective-permute-done((bf16[4,2,12,16,128]{4,3,2,1,0:T(8,128)(2,1)S(1)}, bf16[4,2,12,16,128]{4,3,2,1,0:T(8,128)(2,1)S(1)}, u32[]{:S(2)}, u32[]{:S(2)}) %collective-permute-start.2) | collective-permute-done | bytes 393248 | tf_op jit(solution)/shard_map/ppermute | solution.py:242
  58.5 0.6 shard_map.47
  59.2 3.8 %collective-permute-start.3 = (bf16[4,2,12,16,128]{4,3,2,1,0:T(8,128)(2,1)S(1)}, bf16[4,2,12,16,128]{4,3,2,1,0:T(8,128)(2,1)S(1)}, u32[]{:S(2)}, u32[]{:S(2)}) collective-permute-start(bf16[4,2,12,16,128]{4,3,2,1,0:T(8,128)(2,1)S(1)} %get-tuple-element.19), channel_id=1, source_target_pairs={{0,64},{64,0},{128,192},{192,128},{1,65},{65,1},{129,193},{193,129... | collective-permute-start | bytes 1179656 | tf_op jit(solution)/shard_map/ppermute | solution.py:242
  63.0 1.9 collective-permute-start.4
  64.9 4.0 %collective-permute-start.5 = (bf16[4,2,12,16,128]{4,3,2,1,0:T(8,128)(2,1)S(1)}, bf16[4,2,12,16,128]{4,3,2,1,0:T(8,128)(2,1)S(1)}, u32[]{:S(2)}, u32[]{:S(2)}) collective-permute-start(bf16[4,2,12,16,128]{4,3,2,1,0:T(8,128)(2,1)S(1)} %get-tuple-element.21), channel_id=1, source_target_pairs={{0,192},{64,128},{128,64},{192,0},{1,193},{65,129},{129,65},{193,1... | collective-permute-start | bytes 1179656 | tf_op jit(solution)/shard_map/ppermute | solution.py:242
  68.9 17.4 %collective-permute-done.3.refs_1_ = bf16[4,2,12,16,128]{4,3,2,1,0:T(8,128)(2,1)S(1)} collective-permute-done((bf16[4,2,12,16,128]{4,3,2,1,0:T(8,128)(2,1)S(1)}, bf16[4,2,12,16,128]{4,3,2,1,0:T(8,128)(2,1)S(1)}, u32[]{:S(2)}, u32[]{:S(2)}) %collective-permute-start.3) | collective-permute-done | bytes 393248 | tf_op jit(solution)/shard_map/ppermute | solution.py:242
  86.3 8.5 %collective-permute-done.4.refs_2_ = bf16[4,2,12,16,128]{4,3,2,1,0:T(8,128)(2,1)S(1)} collective-permute-done((bf16[4,2,12,16,128]{4,3,2,1,0:T(8,128)(2,1)S(1)}, bf16[4,2,12,16,128]{4,3,2,1,0:T(8,128)(2,1)S(1)}, u32[]{:S(2)}, u32[]{:S(2)}) %collective-permute-start.4) | collective-permute-done | bytes 393248 | tf_op jit(solution)/shard_map/ppermute | solution.py:242
  94.8 79.4 %collective-permute-done.5.refs_3_ = bf16[4,2,12,16,128]{4,3,2,1,0:T(8,128)(2,1)S(1)} collective-permute-done((bf16[4,2,12,16,128]{4,3,2,1,0:T(8,128)(2,1)S(1)}, bf16[4,2,12,16,128]{4,3,2,1,0:T(8,128)(2,1)S(1)}, u32[]{:S(2)}, u32[]{:S(2)}) %collective-permute-start.5) | collective-permute-done | bytes 393248 | tf_op jit(solution)/shard_map/ppermute | solution.py:242
  174.2 1.2 shard_map.48.lam_ref
  175.4 0.0 all-to-all-done.parts_ref.parts_in
  175.5 2.9 %shard_map.50.amp_ref = bf16[384,4096]{1,0:T(8,128)(2,1)S(1)} custom-call(bf16[32,2,12,16,128]{4,3,2,1,0:T(8,128)(2,1)} %all-to-all-done.parts_ref.parts_in), custom_call_target="tpu_custom_call" | custom-call | tf_op jit(solution)/shard_map/pallas_call | solution.py:34
  178.3 0.0 copy-start.1
  178.3 0.0 copy-start.2
  178.4 2.5 shard_map.51
  180.8 8.7 %all-to-all-start.1 = ((f32[32,16,128]{2,1,0:T(8,128)}), f32[32,16,128]{2,1,0:T(8,128)S(1)}, u32[]{:S(2)}, u32[]{:S(2)}) async-start(f32[32,16,128]{2,1,0:T(8,128)} %bitcast.4), calls=%async_computation.1 | async-start | bytes 524288 | tf_op jit(solution)/shard_map/all_to_all | solution.py:237
  189.5 0.0 copy-done.1
  189.6 8.3 %all-to-all-done.1 = f32[32,16,128]{2,1,0:T(8,128)S(1)} async-done(((f32[32,16,128]{2,1,0:T(8,128)}), f32[32,16,128]{2,1,0:T(8,128)S(1)}, u32[]{:S(2)}, u32[]{:S(2)}) %all-to-all-start.1) | async-done | bytes 262176 | tf_op jit(solution)/shard_map/all_to_all | solution.py:237
  197.9 0.7 broadcast_in_dim.4
  198.5 7.4 %all-to-all-start.2 = ((f32[16,16,128]{2,1,0:T(8,128)}), f32[16,16,128]{2,1,0:T(8,128)S(1)}, u32[]{:S(2)}, u32[]{:S(2)}) async-start(f32[16,16,128]{2,1,0:T(8,128)} %broadcast_in_dim.4), calls=%async_computation.2 | async-start | bytes 262144 | tf_op jit(solution)/shard_map/all_to_all | solution.py:237
  206.0 0.0 copy-done.2
  206.0 0.2 fusion
  206.2 0.2 fusion.1
  206.4 0.4 fusion.8
  206.8 0.1 copy.6
  206.9 11.0 %all-to-all-done.2 = f32[16,16,128]{2,1,0:T(8,128)S(1)} async-done(((f32[16,16,128]{2,1,0:T(8,128)}), f32[16,16,128]{2,1,0:T(8,128)S(1)}, u32[]{:S(2)}, u32[]{:S(2)}) %all-to-all-start.2) | async-done | bytes 131104 | tf_op jit(solution)/shard_map/all_to_all | solution.py:237
  218.0 0.7 broadcast_in_dim.5
  218.6 7.4 %all-to-all-start.3 = ((bf16[32,16,128]{2,1,0:T(8,128)(2,1)}), bf16[32,16,128]{2,1,0:T(8,128)(2,1)S(1)}, u32[]{:S(2)}, u32[]{:S(2)}) async-start(bf16[32,16,128]{2,1,0:T(8,128)(2,1)} %broadcast_in_dim.5), calls=%async_computation.3 | async-start | bytes 262144 | tf_op jit(solution)/shard_map/all_to_all | solution.py:237
  226.1 3.4 %shard_map.52.amp_ref = bf16[384,4096]{1,0:T(8,128)(2,1)S(1)} custom-call(bf16[32,2,12,16,128]{4,3,2,1,0:T(8,128)(2,1)} %all-to-all-done.parts_ref.parts_in), custom_call_target="tpu_custom_call" | custom-call | tf_op jit(solution)/shard_map/pallas_call | solution.py:34
  229.5 4.1 %all-to-all-done.3 = bf16[32,16,128]{2,1,0:T(8,128)(2,1)S(1)} async-done(((bf16[32,16,128]{2,1,0:T(8,128)(2,1)}), bf16[32,16,128]{2,1,0:T(8,128)(2,1)S(1)}, u32[]{:S(2)}, u32[]{:S(2)}) %all-to-all-start.3) | async-done | bytes 131104 | tf_op jit(solution)/shard_map/all_to_all | solution.py:237
  233.6 2.3 shard_map.53
  235.9 39.9 %all_to_all.25.parts_ref = bf16[16,12,2,16,128]{4,3,2,1,0:T(8,128)(2,1)S(1)} all-to-all(bf16[16,12,2,16,128]{4,3,2,1,0:T(8,128)(2,1)S(1)} %bitcast.16), channel_id=1, replica_groups=mesh['zb'=2,'z4'=4,'y'=4,'zh'=2,'x'=4,'c'=2] {'z4','y'}, dimensions={0} | all-to-all | bytes 3145728 | tf_op jit(solution)/shard_map/all_to_all | solution.py:237
  275.7 1.4 shard_map.54
  (5 shorter events, 0.1 us)
Async XLA Ops:
  3.3 16.5 %copy-start = (bf16[12,64,1024]{2,1,0:T(8,128)(2,1)S(1)}, bf16[12,64,1024]{2,1,0:T(8,128)(2,1)}, u32[]{:S(2)}) copy-start(bf16[12,64,1024]{2,1,0:T(8,128)(2,1)} %lam_ref.1) | copy-start | bytes 4718596
  3.3 172.1 %all-to-all-start = ((bf16[32,2,12,16,128]{4,3,2,1,0:T(8,128)(2,1)}), bf16[32,2,12,16,128]{4,3,2,1,0:T(8,128)(2,1)}, u32[]{:S(2)}, u32[]{:S(2)}) async-start(bf16[32,2,12,16,128]{4,3,2,1,0:T(8,128)(2,1)} %shard_map.49), calls=%async_computation | async-start | bytes 6291456 | tf_op jit(solution)/shard_map/all_to_all | solution.py:237
  20.7 22.0 %collective-permute-start = (bf16[4,2,12,16,128]{4,3,2,1,0:T(8,128)(2,1)S(1)}, bf16[4,2,12,16,128]{4,3,2,1,0:T(8,128)(2,1)S(1)}, u32[]{:S(2)}, u32[]{:S(2)}) collective-permute-start(bf16[4,2,12,16,128]{4,3,2,1,0:T(8,128)(2,1)S(1)} %get-tuple-element.15), channel_id=1, source_target_pairs={{0,16},{16,0},{32,48},{48,32},{1,17},{17,1},{33,49},{49,33},{2,18}... | collective-permute-start | bytes 1179656 | tf_op jit(solution)/shard_map/ppermute | solution.py:242
  23.8 28.1 %collective-permute-start.1 = (bf16[4,2,12,16,128]{4,3,2,1,0:T(8,128)(2,1)S(1)}, bf16[4,2,12,16,128]{4,3,2,1,0:T(8,128)(2,1)S(1)}, u32[]{:S(2)}, u32[]{:S(2)}) collective-permute-start(bf16[4,2,12,16,128]{4,3,2,1,0:T(8,128)(2,1)S(1)} %get-tuple-element.16), channel_id=1, source_target_pairs={{0,32},{16,48},{32,0},{48,16},{1,33},{17,49},{33,1},{49,17},{2,34}... | collective-permute-start | bytes 1179656 | tf_op jit(solution)/shard_map/ppermute | solution.py:242
  28.1 30.4 %collective-permute-start.2 = (bf16[4,2,12,16,128]{4,3,2,1,0:T(8,128)(2,1)S(1)}, bf16[4,2,12,16,128]{4,3,2,1,0:T(8,128)(2,1)S(1)}, u32[]{:S(2)}, u32[]{:S(2)}) collective-permute-start(bf16[4,2,12,16,128]{4,3,2,1,0:T(8,128)(2,1)S(1)} %get-tuple-element.17), channel_id=1, source_target_pairs={{0,48},{16,32},{32,16},{48,0},{1,49},{17,33},{33,17},{49,1},{2,50}... | collective-permute-start | bytes 1179656 | tf_op jit(solution)/shard_map/ppermute | solution.py:242
  59.2 27.2 %collective-permute-start.3 = (bf16[4,2,12,16,128]{4,3,2,1,0:T(8,128)(2,1)S(1)}, bf16[4,2,12,16,128]{4,3,2,1,0:T(8,128)(2,1)S(1)}, u32[]{:S(2)}, u32[]{:S(2)}) collective-permute-start(bf16[4,2,12,16,128]{4,3,2,1,0:T(8,128)(2,1)S(1)} %get-tuple-element.19), channel_id=1, source_target_pairs={{0,64},{64,0},{128,192},{192,128},{1,65},{65,1},{129,193},{193,129... | collective-permute-start | bytes 1179656 | tf_op jit(solution)/shard_map/ppermute | solution.py:242
  63.0 31.8 %collective-permute-start.4 = (bf16[4,2,12,16,128]{4,3,2,1,0:T(8,128)(2,1)S(1)}, bf16[4,2,12,16,128]{4,3,2,1,0:T(8,128)(2,1)S(1)}, u32[]{:S(2)}, u32[]{:S(2)}) collective-permute-start(bf16[4,2,12,16,128]{4,3,2,1,0:T(8,128)(2,1)S(1)} %get-tuple-element.20), channel_id=1, source_target_pairs={{0,128},{64,192},{128,0},{192,64},{1,129},{65,193},{129,1},{193,65... | collective-permute-start | bytes 1179656 | tf_op jit(solution)/shard_map/ppermute | solution.py:242
  64.9 109.3 %collective-permute-start.5 = (bf16[4,2,12,16,128]{4,3,2,1,0:T(8,128)(2,1)S(1)}, bf16[4,2,12,16,128]{4,3,2,1,0:T(8,128)(2,1)S(1)}, u32[]{:S(2)}, u32[]{:S(2)}) collective-permute-start(bf16[4,2,12,16,128]{4,3,2,1,0:T(8,128)(2,1)S(1)} %get-tuple-element.21), channel_id=1, source_target_pairs={{0,192},{64,128},{128,64},{192,0},{1,193},{65,129},{129,65},{193,1... | collective-permute-start | bytes 1179656 | tf_op jit(solution)/shard_map/ppermute | solution.py:242
  178.3 11.2 %copy-start.1 = (s32[264,2]{0,1:T(2,128)S(1)}, s32[264,2]{0,1:T(2,128)}, u32[]{:S(2)}) copy-start(s32[264,2]{0,1:T(2,128)} %param.7) | copy-start | bytes 6340
  178.3 27.6 %copy-start.2 = (s32[32]{0:T(128)S(1)}, s32[32]{0:T(128)}, u32[]{:S(2)}) copy-start(s32[32]{0:T(128)} %param.6) | copy-start | bytes 388
  180.8 17.0 %all-to-all-start.1 = ((f32[32,16,128]{2,1,0:T(8,128)}), f32[32,16,128]{2,1,0:T(8,128)S(1)}, u32[]{:S(2)}, u32[]{:S(2)}) async-start(f32[32,16,128]{2,1,0:T(8,128)} %bitcast.4), calls=%async_computation.1 | async-start | bytes 524288 | tf_op jit(solution)/shard_map/all_to_all | solution.py:237
  198.5 19.4 %all-to-all-start.2 = ((f32[16,16,128]{2,1,0:T(8,128)}), f32[16,16,128]{2,1,0:T(8,128)S(1)}, u32[]{:S(2)}, u32[]{:S(2)}) async-start(f32[16,16,128]{2,1,0:T(8,128)} %broadcast_in_dim.4), calls=%async_computation.2 | async-start | bytes 262144 | tf_op jit(solution)/shard_map/all_to_all | solution.py:237
  218.6 14.9 %all-to-all-start.3 = ((bf16[32,16,128]{2,1,0:T(8,128)(2,1)}), bf16[32,16,128]{2,1,0:T(8,128)(2,1)S(1)}, u32[]{:S(2)}, u32[]{:S(2)}) async-start(bf16[32,16,128]{2,1,0:T(8,128)(2,1)} %broadcast_in_dim.5), calls=%async_computation.3 | async-start | bytes 262144 | tf_op jit(solution)/shard_map/all_to_all | solution.py:237
